TPU v7x, 32 devices: a whole 2x2x4 slice. The times are simulated.
32 devices in a mesh: groups: 2 (over y), dp: 4 (over z), feat: 2 (over x), sub: 2 (over core).
Axes of the slice: x: 2, y: 2, z: 4, core: 2. Of those that a mesh axis runs over, the one named last changes fastest.
Arguments:
- layer_inputs: bfloat16 [14336, 4096], P(('groups', 'dp'), ('feat', 'sub')), parts along dimension 0, may hold values from -6 to 6
- output_grads: bfloat16 [14336, 4096], P(('groups', 'dp'), ('feat', 'sub')), parts along dimension 0, may hold values from -6 to 6
- proj_in: bfloat16 [4096, 64], P(('feat', 'sub')), may hold values from -0.09375 to 0.09375
- proj_out: bfloat16 [4096, 128], P(('feat', 'sub')), may hold values from -0.09375 to 0.09375
- lengths: int32 [8, 56], P(('groups', 'dp')), parts along dimension 0, may hold values from 1 to 128, 1792 in all within a row
- target_ids: int32 [512], P(('groups', 'dp')), parts along dimension 0, may hold values from 0 to 223
Outputs:
- covariance: float32 [16384, 8192], P(('groups', 'feat', 'sub'), 'dp'), parts along dimension 0
- scores: float32 [512, 224], P(('groups', 'dp'), ('feat', 'sub')), parts along dimension 0
There are 2 independent parts, one for each index of `groups`. A program takes and returns all parts, laid end to end along the dimension named above; an argument that names none is the same for every part. Nothing has to cross between parts.
Inputs may be any that keep to these rules, and one draw needn't show every extreme that they name: Each row of lengths sums to 1792, its largest entry is exactly 128. `target_ids`: global sequence numbers.
All inputs are finite; a program needn't handle non-finite values.
Results may differ from a plain program's by a relative error of at most 0.004.
Values may be sent and summed in bfloat16 or wider, within the bound.
No kernel may reach another device: no remote copies, remote signals or barrier semaphores. Data moves between devices by JAX's collectives and lax.ppermute only.
A program may use at most 128 MiB of HBM per device.

v0:
```python
import jax
import jax.numpy as jnp
from jax import lax
from jax.sharding import PartitionSpec as P


def shards(layer_inputs, output_grads, proj_in, proj_out, lengths, target_ids):
    group = lax.axis_size(("feat", "sub"))
    tok_rows = layer_inputs.shape[0]
    rank_in = proj_in.shape[1]
    part_u = jnp.dot(layer_inputs, proj_in, preferred_element_type=jnp.float32)
    part_v = jnp.dot(output_grads, proj_out, preferred_element_type=jnp.float32)
    share = proj_out.shape[1] // group
    u_full = lax.psum(part_u, ("feat", "sub"))
    v_mine = lax.psum_scatter(part_v, ("feat", "sub"), scatter_dimension=1, tiled=True)
    seq_len = lengths[0]
    seq_count = seq_len.shape[0]
    ends = jnp.cumsum(seq_len)
    starts = ends - seq_len
    position = jnp.arange(tok_rows, dtype=jnp.int32)
    member = ((position[None, :] >= starts[:, None]) & (position[None, :] < ends[:, None])).astype(
        jnp.float32
    )
    member = member / jnp.sqrt(seq_len.astype(jnp.float32))[:, None]
    masked_v = (member[:, None, :] * jnp.transpose(v_mine)[None, :, :]).reshape(
        seq_count * share, tok_rows
    )
    summed = jnp.dot(
        masked_v, u_full, precision=lax.Precision.HIGHEST, preferred_element_type=jnp.float32
    )
    local_feat = summed.reshape(seq_count, share * rank_in).astype(jnp.bfloat16)
    gathered = lax.all_gather(local_feat, "dp", axis=0, tiled=True)
    seq_total = gathered.shape[0]
    block_width = gathered.shape[1]
    col_width = block_width * group // lax.axis_size("dp")
    col_start = lax.axis_index("dp") * col_width
    owner = col_start // block_width
    offset = col_start % block_width
    own_slice = lax.dynamic_slice_in_dim(gathered, offset, col_width, 1)
    every_slice = lax.all_gather(own_slice, ("feat", "sub"), axis=1, tiled=True)
    other_cols = lax.dynamic_slice_in_dim(every_slice, owner * col_width, col_width, 1)
    cov_tile = (
        lax.dot_general(
            gathered, other_cols, (((0,), (0,)), ((), ())), preferred_element_type=jnp.float32
        )
        / seq_total
    )
    diag_part = (
        jnp.einsum("sk,sk->k", gathered, gathered, preferred_element_type=jnp.float32) / seq_total
    )
    weights = 1.0 / (diag_part + 1e-05)
    chosen = jnp.take(gathered, target_ids, axis=0)
    weighted = (chosen.astype(jnp.float32) * weights[None, :]).astype(jnp.bfloat16)
    partial_scores = lax.dot_general(
        weighted, gathered, (((1,), (1,)), ((), ())), preferred_element_type=jnp.float32
    )
    summed_scores = lax.psum_scatter(
        partial_scores, ("feat", "sub"), scatter_dimension=1, tiled=True
    )
    scores = summed_scores / jnp.sqrt(jnp.float32(block_width * group))
    return (cov_tile, scores)


def solution(mesh):
    placed = (
        P(("groups", "dp"), ("feat", "sub")),
        P(("groups", "dp"), ("feat", "sub")),
        P(("feat", "sub"), None),
        P(("feat", "sub"), None),
        P(("groups", "dp"), None),
        P(("groups", "dp")),
    )
    return jax.shard_map(
        shards,
        mesh=mesh,
        in_specs=placed,
        out_specs=(P(("groups", "feat", "sub"), "dp"), P(("groups", "dp"), ("feat", "sub"))),
        check_vma=False,
    )
```

profile of v0, /device:TPU:0, one launch (start us, length us, event | category | flops | bytes accessed | tf_op | source)
XLA Modules:
  0.0 180.8 jit_solution(16412726500588813380)
XLA Ops:
  7.2 0.0 copy-start
  7.2 0.0 copy-start.2
  7.2 0.0 reduce-scatter.5.cloned.1.call-start
  7.2 0.9 copy-done
  8.1 4.3 %fusion.11 = f32[1792,128]{0,1:T(8,128)} fusion(bf16[1792,1024]{1,0:T(8,128)(2,1)} %param.7, bf16[1024,128]{1,0:T(8,128)(2,1)S(1)} %copy-done), kind=kOutput, calls=%fused_computation.27 | convolution fusion | flops 469762048 | bytes 4849664 | tf_op jit(solution)/shard_map/dot_general | solution.py:12
  12.4 0.0 copy-start.4
  12.4 0.0 copy-start.3
  12.4 0.0 reduce-scatter.5.cloned.1.call-update
  12.5 0.0 all-reduce.3.cloned.1.call-start
  12.5 0.0 copy-done.2
  12.5 4.1 %fusion.12 = f32[1792,64]{0,1:T(8,128)} fusion(bf16[1792,1024]{1,0:T(8,128)(2,1)} %param.6, bf16[1024,64]{0,1:T(8,128)(2,1)S(1)} %copy-done.2), kind=kOutput, calls=%fused_computation.28 | convolution fusion | flops 234881024 | bytes 4259840 | tf_op jit(solution)/shard_map/dot_general | solution.py:11
  16.6 0.0 all-reduce.3.cloned.1.call-update
  16.6 0.0 reduce-scatter.7.cloned.1.call-start
  16.6 0.0 copy-done.4
  16.7 0.0 copy-done.3
  16.7 0.1 copy.11
  16.8 0.1 reduce-window.7
  16.9 0.1 reduce.1
  17.0 0.2 convert_divide_fusion
  17.2 22.2 %reduce-scatter.5.cloned.1.call-done = f32[1792,32]{0,1:T(8,128)} async-done(((f32[1792,128]{0,1:T(8,128)}), f32[1792,32]{0,1:T(8,128)}) %reduce-scatter.5.cloned.1.call-update) | async-done | bytes 229392 | tf_op jit(solution)/shard_map/reduce_scatter | solution.py:15
  39.4 7.4 %broadcast_multiply_fusion = f32[56,32,1792]{2,1,0:T(8,128)} fusion(f32[32,1792]{1,0:T(8,128)} %bitcast.21, f32[56,1792]{1,0:T(8,128)S(1)} %convert_divide_fusion), kind=kLoop, calls=%fused_computation.2 | loop fusion | flops 3211264 | bytes 13475840 | tf_op jit(solution)/shard_map/mul | solution.py:25
  46.7 28.2 %all-reduce.3.cloned.1.call-done = f32[1792,64]{0,1:T(8,128)} async-done(((f32[1792,64]{0,1:T(8,128)}), f32[1792,64]{0,1:T(8,128)}) %all-reduce.3.cloned.1.call-update) | async-done | bytes 458768 | tf_op jit(solution)/shard_map/psum | solution.py:14
  74.9 14.7 %convolution_convert_fusion = bf16[1792,64]{0,1:T(8,128)(2,1)S(1)} fusion(f32[1792,1792]{1,0:T(8,128)} %bitcast.20, f32[1792,64]{0,1:T(8,128)} %all-reduce.3.cloned.1.call-done), kind=kOutput, calls=%fused_computation.3 | convolution fusion | flops 2466365440 | bytes 13533184 | tf_op jit(solution)/shard_map/dot_general | solution.py:28
  89.6 0.3 copy.12
  89.9 0.4 convert_element_type.29
  90.3 21.1 %all_gather.6 = bf16[224,2048]{1,0:T(8,128)(2,1)S(1)} all-gather(bf16[56,2048]{1,0:T(8,128)(2,1)S(1)} %convert_element_type.29), channel_id=1, replica_groups=mesh['groups'=2,'dp'=4,'feat'=2,'sub'=2] {'dp'}, dimensions={0}, use_global_device_ids=true | all-gather | bytes 1146880 | tf_op jit(solution)/shard_map/all_gather | solution.py:32
  111.4 0.0 copy-start.1
  111.4 0.2 fusion
  111.6 0.7 gather_fusion
  112.4 1.1 fusion.3
  113.5 0.0 reduce-scatter.7.cloned.1.call-update
  113.5 0.0 all-gather.2.cloned.1.call-start
  113.6 0.0 copy-done.1
  113.6 0.5 all-gather.2.cloned.1.call-update
  114.1 17.1 %reduce-scatter.7.cloned.1.call-done = f32[64,56]{0,1:T(8,128)} async-done(((f32[64,224]{0,1:T(8,128)}), f32[64,56]{0,1:T(8,128)}) %reduce-scatter.7.cloned.1.call-update) | async-done | bytes 14352
  131.2 1.4 broadcast_multiply_fusion.1
  132.6 31.7 %all-gather.2.cloned.1.call-done = bf16[224,8192]{1,0:T(8,128)(2,1)} async-done(((bf16[224,2048]{1,0:T(8,128)(2,1)}), bf16[224,8192]{1,0:T(8,128)(2,1)}) %all-gather.2.cloned.1.call-update) | async-done | bytes 3670032 | tf_op jit(solution)/shard_map/all_gather | solution.py:40
  164.3 10.0 %convolution_multiply_fusion = f32[2048,2048]{1,0:T(8,128)} fusion(bf16[224,2048]{1,0:T(8,128)(2,1)} %copy-done.1, bf16[224,8192]{1,0:T(8,128)(2,1)} %all-gather.2.cloned.1.call-done, s32[]{:T(128)S(6)} %select_n.23), kind=kOutput, calls=%fused_computation.1 | convolution fusion | flops 1883242496 | bytes 18612228 | tf_op jit(solution)/shard_map/dot_general | solution.py:43
  (6 shorter events, 0.0 us)
Async XLA Ops:
  7.2 1.0 copy-start
  7.2 5.3 %copy-start.2 = (bf16[1024,64]{0,1:T(8,128)(2,1)S(1)}, bf16[1024,64]{0,1:T(8,128)(2,1)}, u32[]{:S(2)}) copy-start(bf16[1024,64]{0,1:T(8,128)(2,1)} %param.8) | copy-start | bytes 393220
  7.2 32.2 %reduce-scatter.5.cloned.1.call-start = ((), (), s32[]{:S(2)}) async-start(), calls=%async_computation.2 | async-start | bytes 1146880 | tf_op jit(solution)/shard_map/reduce_scatter | solution.py:15
  12.4 4.2 %copy-start.4 = (s32[64]{0:T(128)S(1)}, s32[64]{0:T(128)}, u32[]{:S(2)}) copy-start(s32[64]{0:T(128)} %param.11) | copy-start | bytes 772
  12.4 4.3 %copy-start.3 = (s32[1,56]{1,0:T(1,128)S(1)}, s32[1,56]{1,0:T(1,128)}, u32[]{:S(2)}) copy-start(s32[1,56]{1,0:T(1,128)} %param.10) | copy-start | bytes 676
  12.5 62.5 %all-reduce.3.cloned.1.call-start = ((), (), s32[]{:S(2)}) async-start(), calls=%async_computation.3 | async-start | bytes 917504 | tf_op jit(solution)/shard_map/psum | solution.py:14
  16.6 114.6 %reduce-scatter.7.cloned.1.call-start = ((), (), s32[]{:S(2)}) async-start(), calls=%async_computation.5 | async-start | bytes 143360
  111.4 2.1 %copy-start.1 = (bf16[224,2048]{1,0:T(8,128)(2,1)}, bf16[224,2048]{1,0:T(8,128)(2,1)S(1)}, u32[]{:S(2)}) copy-start(bf16[224,2048]{1,0:T(8,128)(2,1)S(1)} %all_gather.6) | copy-start | bytes 2752516
  113.5 50.8 %all-gather.2.cloned.1.call-start = ((), (), s32[]{:S(2)}) async-start(), calls=%async_computation.4 | async-start | bytes 4587520 | tf_op jit(solution)/shard_map/all_gather | solution.py:40
Sparse Core Ops, SparseCore 0:
  12.6 26.7 reduce-scatter.4
  41.8 33.0 all-reduce.2
  113.7 17.5 reduce-scatter.6
  132.7 31.5 all-gather.1
where the time goes:
time: 181 us
  waiting for transfers between devices  99.7 us (55%)
  matrix products  34.2 us (19%)
  blocking collectives  21.1 us (12%)
  between operations  13.9 us (8%)
  other arithmetic  9.34 us (5%)
  local copies, waits for them, and re-layouts  2.43 us (1%)
    all_gather x1, waiting for transfers between devices, shards(): every_slice = lax.all_gather(own_slice, ('feat', 'sub'), axis=1, tiled=True)  31.7 us
    psum x1, waiting for transfers between devices, shards(): u_full = lax.psum(part_u, ('feat', 'sub'))  28.2 us
    reduce_scatter x1, waiting for transfers between devices, shards(): lax.psum_scatter(part_v, ('feat', 'sub'), scatter_dimension=1, tiled=True)  22.2 us
    all_gather x1, blocking collectives, shards(): gathered = lax.all_gather(local_feat, 'dp', axis=0, tiled=True)  21.1 us
    unnamed x5, waiting for transfers between devices  17.7 us
    dot_general x1, matrix products, shards(): jnp.dot(masked_v, u_full, precision=lax.Precision.HIGHEST, preferred_elem...  14.7 us
    dot_general x1, matrix products, shards(): lax.dot_general(gathered, other_cols, (((0,), (0,)), ((), ())), preferred...  10 us
    mul x1, other arithmetic, shards(): member[:, None, :] * jnp.transpose(v_mine)[None, :, :]  7.37 us
  transfers between devices with their start and end apart: 4, of which 4 were waited for; matrix products, arithmetic and copies ran while one was open for 7% of the time, Pallas kernels for 0%

commit v1 on v0

v1 whole, which is shorter than its diff:
```python
import jax
import jax.numpy as jnp
from jax import lax
from jax.experimental import pallas as pl
from jax.experimental.pallas import tpu as pltpu
from jax.sharding import PartitionSpec as P

F32, BF16, I32 = jnp.float32, jnp.bfloat16, jnp.int32
WIDE = ("feat", "sub")
MIB = 1 << 20
VMEM = pl.BlockSpec(memory_space=pltpu.VMEM)
SMEM = pl.BlockSpec(memory_space=pltpu.SMEM)


def params(mib):
    return pltpu.CompilerParams(vmem_limit_bytes=mib * MIB)


def project_kernel(x_ref, g_ref, in_ref, out_ref, full_ref):
    rank_in = in_ref.shape[1]
    u = jnp.dot(x_ref[...], in_ref[...], preferred_element_type=F32)
    v = jnp.dot(g_ref[...], out_ref[...], preferred_element_type=F32)
    full_ref[0:rank_in, :] = jnp.transpose(u)
    full_ref[rank_in:, :] = jnp.transpose(v)


def project(layer_inputs, output_grads, proj_in, proj_out):
    rows, width = layer_inputs.shape
    tile = 256
    total = proj_in.shape[1] + proj_out.shape[1]
    return pl.pallas_call(
        project_kernel,
        grid=(rows // tile,),
        in_specs=[
            pl.BlockSpec((tile, width), lambda i: (i, 0)),
            pl.BlockSpec((tile, width), lambda i: (i, 0)),
            pl.BlockSpec(proj_in.shape, lambda i: (0, 0)),
            pl.BlockSpec(proj_out.shape, lambda i: (0, 0)),
        ],
        out_specs=pl.BlockSpec((total, tile), lambda i: (0, i)),
        out_shape=jax.ShapeDtypeStruct((total, rows), F32),
        compiler_params=params(16),
        name="project",
    )(layer_inputs, output_grads, proj_in, proj_out)


def split(x):
    high = x.astype(BF16)
    return high, (x - high.astype(F32)).astype(BF16)


def feature_kernel(start_ref, end_ref, u_ref, v_ref, scale_ref, feat_ref, uu, vh, vl, acc, wide):
    rank_in = u_ref.shape[0]
    share = v_ref.shape[0]
    tokens = u_ref.shape[1]
    seqs = scale_ref.shape[0]
    tile = 256
    high, low = split(u_ref[...])
    uu[0:rank_in, :] = high
    uu[rank_in:, :] = low
    high, low = split(v_ref[...])
    vh[...] = high
    vl[...] = low
    lane = lax.broadcasted_iota(I32, (8, tile), 1)
    left = lax.broadcasted_iota(I32, (8, 2 * rank_in), 1) < rank_in
    for group in range(seqs // 8):
        first = start_ref[8 * group]
        last = end_ref[8 * group + 7]
        acc[...] = jnp.zeros_like(acc)

        def step(k, carry):
            at = pl.multiple_of(k * tile, tile)
            tops, lows = [], []
            v_high = vh[:, pl.ds(at, tile)]
            v_low = vl[:, pl.ds(at, tile)]
            for s in range(8):
                begin = start_ref[8 * group + s] - at
                stop = end_ref[8 * group + s] - at
                inside = jnp.where((lane >= begin) & (lane < stop), 1.0, 0.0).astype(F32)
                inside = jnp.concatenate([inside] * (share // 8), axis=0).astype(BF16)
                tops.append(v_high * inside)
                lows.append(v_low * inside)
            right = uu[:, pl.ds(at, tile)]
            dims = (((1,), (1,)), ((), ()))
            total = lax.dot_general(jnp.concatenate(tops, 0), right, dims, preferred_element_type=F32)
            total += lax.dot_general(jnp.concatenate(lows, 0), right, dims, preferred_element_type=F32)
            acc[...] += total
            return carry

        lax.fori_loop(first // tile, (last + tile - 1) // tile, step, 0)
        factor = scale_ref[8 * group : 8 * group + 8, :]
        for pair in range(share // 2):
            even = acc[pl.ds(2 * pair, 8, stride=share), :]
            odd = acc[pl.ds(2 * pair + 1, 8, stride=share), :]
            even = even + pltpu.roll(even, rank_in, 1)
            odd = odd + pltpu.roll(odd, rank_in, 1)
            both = jnp.where(left, even, odd) * factor
            wide[8 * group : 8 * group + 8, 2 * rank_in * pair : 2 * rank_in * (pair + 1)] = both
    feat_ref[...] = wide[...].astype(BF16)


def features_of(starts, ends, u, v, scale):
    rank_in, tokens = u.shape
    share = v.shape[0]
    seqs = starts.shape[0]
    return pl.pallas_call(
        feature_kernel,
        in_specs=[SMEM, SMEM, VMEM, VMEM, VMEM],
        out_specs=VMEM,
        out_shape=jax.ShapeDtypeStruct((seqs, share * rank_in), BF16),
        scratch_shapes=[
            pltpu.VMEM((2 * rank_in, tokens), BF16),
            pltpu.VMEM((share, tokens), BF16),
            pltpu.VMEM((share, tokens), BF16),
            pltpu.VMEM((8 * share, 2 * rank_in), F32),
            pltpu.VMEM((seqs, share * rank_in), F32),
        ],
        compiler_params=params(16),
        name="features",
    )(starts, ends, u, v, scale)


def score_kernel(ids_ref, all_ref, part_ref):
    every = all_ref[...]
    seqs = every.shape[0]
    picks = ids_ref.shape[0]
    wide = every.astype(F32)
    diag = jnp.sum(wide * wide, axis=0, keepdims=True) / seqs
    weights = 1.0 / (diag + 1e-05)
    column = lax.broadcasted_iota(I32, (picks, seqs), 1)
    chosen_of = jnp.where(column == ids_ref[...], 1.0, 0.0).astype(BF16)
    chosen = jnp.dot(chosen_of, every, preferred_element_type=F32)
    weighted = (chosen * weights).astype(BF16)
    part_ref[...] = lax.dot_general(
        every, weighted, (((1,), (1,)), ((), ())), preferred_element_type=F32
    )


def partial_scores_of(ids, gathered):
    return pl.pallas_call(
        score_kernel,
        in_specs=[VMEM, VMEM],
        out_specs=VMEM,
        out_shape=jax.ShapeDtypeStruct((gathered.shape[0], ids.shape[0]), F32),
        compiler_params=params(24),
        name="partial_scores",
    )(ids[:, None], gathered)


def covariance_kernel(row_ref, col_ref, tile_ref):
    seqs = row_ref.shape[0]
    product = lax.dot_general(
        row_ref[...], col_ref[...], (((0,), (0,)), ((), ())), preferred_element_type=F32
    )
    tile_ref[...] = product * (1.0 / seqs)


def covariance_of(gathered, other_cols):
    seqs, rows = gathered.shape
    cols = other_cols.shape[1]
    tile = 256
    return pl.pallas_call(
        covariance_kernel,
        grid=(rows // tile,),
        in_specs=[
            pl.BlockSpec((seqs, tile), lambda i: (0, i)),
            pl.BlockSpec((seqs, cols), lambda i: (0, 0)),
        ],
        out_specs=pl.BlockSpec((tile, cols), lambda i: (i, 0)),
        out_shape=jax.ShapeDtypeStruct((rows, cols), F32),
        compiler_params=params(24),
        name="covariance",
    )(gathered, other_cols)


def both_ways(x, axis):
    return lax.ppermute(x, axis, [(0, 1), (1, 0)])


def reduced(partial, rank_in, share):
    feats, subs = lax.axis_size("feat"), lax.axis_size("sub")
    if feats != 2 or subs != 2:
        u = lax.psum(partial[:rank_in], WIDE)
        return u, lax.psum_scatter(partial[rank_in:], WIDE, scatter_dimension=0, tiled=True)
    feat, sub = lax.axis_index("feat"), lax.axis_index("sub")
    u = partial[:rank_in].reshape(2, rank_in // 2, -1)
    v = partial[rank_in:].reshape(2, 2, share, -1)
    keep = jnp.concatenate([jnp.where(sub == 0, u[0], u[1]), jnp.where(sub == 0, v[0, 0], v[0, 1]), jnp.where(sub == 0, v[1, 0], v[1, 1])])
    give = jnp.concatenate([jnp.where(sub == 0, u[1], u[0]), jnp.where(sub == 0, v[0, 1], v[0, 0]), jnp.where(sub == 0, v[1, 1], v[1, 0])])
    chip = keep + both_ways(give, "sub")
    half = rank_in // 2
    u_chip, v_low, v_high = chip[:half], chip[half : half + share], chip[half + share :]
    keep = jnp.concatenate([u_chip, jnp.where(feat == 0, v_low, v_high)])
    give = jnp.concatenate([u_chip, jnp.where(feat == 0, v_high, v_low)])
    whole = keep + both_ways(give, "feat")
    u_mine, v_mine = whole[:half], whole[half:]
    u_other = both_ways(u_mine, "sub")
    u = jnp.concatenate([jnp.where(sub == 0, u_mine, u_other), jnp.where(sub == 0, u_other, u_mine)])
    return u, v_mine


def column_block(gathered, col_width):
    group = lax.axis_size(WIDE)
    block_width = gathered.shape[1]
    dp = lax.axis_size("dp")
    at = lax.axis_index("dp")
    if lax.axis_size("feat") == 2 and lax.axis_size("sub") == 2 and dp == 4:
        axes = ("dp",) + WIDE
        me = lax.axis_index(WIDE)
        over = lax.ppermute(gathered, axes, [(4 * d + d, 4 * d + (d ^ 2)) for d in range(4)])
        held = jnp.where(me == at, gathered, over)
        across = [(4 * d + d, 4 * d + (d ^ 1)) for d in range(4)]
        across += [(4 * d + (d ^ 2), 4 * d + (d ^ 3)) for d in range(4)]
        beside = lax.ppermute(held, axes, across)
        return jnp.where((me == at) | (me == (at ^ 2)), held, beside)
    col_start = at * col_width
    owner = col_start // block_width
    own_slice = lax.dynamic_slice_in_dim(gathered, col_start % block_width, col_width, 1)
    every_slice = lax.all_gather(own_slice, WIDE, axis=1, tiled=True)
    return lax.dynamic_slice_in_dim(every_slice, owner * col_width, col_width, 1)


def shards(layer_inputs, output_grads, proj_in, proj_out, lengths, target_ids):
    group = lax.axis_size(WIDE)
    rank_in = proj_in.shape[1]
    share = proj_out.shape[1] // group
    partial = project(layer_inputs, output_grads, proj_in, proj_out)
    u, v_mine = reduced(partial, rank_in, share)
    seq_len = lengths[0]
    ends = jnp.cumsum(seq_len)
    starts = ends - seq_len
    scale = jnp.broadcast_to(1.0 / jnp.sqrt(seq_len.astype(F32))[:, None], (seq_len.shape[0], 2 * rank_in))
    local_feat = features_of(starts, ends, u, v_mine, scale)
    gathered = lax.all_gather(local_feat, "dp", axis=0, tiled=True)
    block_width = gathered.shape[1]
    col_width = block_width * group // lax.axis_size("dp")
    other_cols = column_block(gathered, col_width)
    part = partial_scores_of(target_ids, gathered)
    own = part.shape[0] // group
    me = lax.axis_index(WIDE)
    if lax.axis_size("feat") == 2 and lax.axis_size("sub") == 2:
        pieces = part.reshape(group, own, -1)
        total = lax.dynamic_index_in_dim(pieces, me, 0, keepdims=False)
        for k in range(1, group):
            given = lax.dynamic_index_in_dim(pieces, me ^ k, 0, keepdims=False)
            total = total + lax.ppermute(given, WIDE, [(i, i ^ k) for i in range(group)])
    else:
        total = lax.psum_scatter(part, WIDE, scatter_dimension=0, tiled=True)
    scores = jnp.transpose(total) / jnp.sqrt(jnp.float32(block_width * group))
    return (covariance_of(gathered, other_cols), scores)


def solution(mesh):
    placed = (
        P(("groups", "dp"), ("feat", "sub")),
        P(("groups", "dp"), ("feat", "sub")),
        P(("feat", "sub"), None),
        P(("feat", "sub"), None),
        P(("groups", "dp"), None),
        P(("groups", "dp")),
    )
    return jax.shard_map(
        shards,
        mesh=mesh,
        in_specs=placed,
        out_specs=(P(("groups", "feat", "sub"), "dp"), P(("groups", "dp"), ("feat", "sub"))),
        check_vma=False,
    )
```

time: 181 us -> 85.3 us (0.47)
  waiting for transfers between devices: 99.7 us -> 26.6 us
  matrix products: 34.2 us -> 0 us
  Pallas kernels: 0 us -> 16.9 us
  between operations: 13.9 us -> 0.87 us
  starting transfers between devices: 0.16 us -> 11 us
  other arithmetic: 9.34 us -> 1.44 us
  local copies, waits for them, and re-layouts: 2.43 us -> 6.47 us
    dot_general x5 -> x0, matrix products: 34.2 us -> none  [the longest x1 14.7 us: shards(): jnp.dot(masked_v, u_full, precision=lax.Precision.HIGHEST, preferred_elem...]
    all_gather x1 -> x0, waiting for transfers between devices: 31.7 us -> none  [shards(): every_slice = lax.all_gather(own_slice, ('feat', 'sub'), axis=1, tiled=True)]
    psum x1 -> x0, waiting for transfers between devices: 28.2 us -> none  [shards(): u_full = lax.psum(part_u, ('feat', 'sub'))]
    ppermute x0 -> x8, waiting for transfers between devices: none -> 26.6 us  [the longest x3 13.7 us: both_ways(): return lax.ppermute(x, axis, [(0, 1), (1, 0)])]
    reduce_scatter x1 -> x0, waiting for transfers between devices: 22.2 us -> none  [shards(): lax.psum_scatter(part_v, ('feat', 'sub'), scatter_dimension=1, tiled=True)]
    unnamed x5 -> x0, waiting for transfers between devices: 17.7 us -> none
    pallas_call x0 -> x4, Pallas kernels: none -> 16.9 us  [the longest x1 7.9 us: covariance_of(): pl.pallas_call(covariance_kernel, grid=(rows // tile,), in_specs=[pl.Bloc...]
    ppermute x0 -> x8, starting transfers between devices: none -> 11 us  [the longest x3 3.51 us: both_ways(): return lax.ppermute(x, axis, [(0, 1), (1, 0)])]
  transfers between devices with their start and end apart: 4 -> 8, of which waited for: 4 -> 6; matrix products, arithmetic and copies ran while one was open for 7% -> 1% of each run, Pallas kernels for 0% -> 1%
where the time goes in v1:
time: 85.3 us; the launch traced here: 84.8 us
  waiting for transfers between devices  26.6 us (31%)
  blocking collectives  21.5 us (25%)
  Pallas kernels  16.9 us (20%)
  starting transfers between devices  11 us (13%)
  local copies, waits for them, and re-layouts  6.47 us (8%)
  other arithmetic  1.44 us (2%)
  between operations  0.87 us (1%)
    all_gather x1, blocking collectives, shards(): gathered = lax.all_gather(local_feat, 'dp', axis=0, tiled=True)  21.5 us
    ppermute x3, waiting for transfers between devices, both_ways(): return lax.ppermute(x, axis, [(0, 1), (1, 0)])  13.7 us
    ppermute x1, waiting for transfers between devices, column_block(): lax.ppermute(gathered, axes, [(4 * d + d, 4 * d + (d ^ 2)) for d in range...  10.8 us
    pallas_call x1, Pallas kernels, covariance_of(): pl.pallas_call(covariance_kernel, grid=(rows // tile,), in_specs=[pl.Bloc...  7.9 us
    unnamed x11, local copies, waits for them, and re-layouts  6.11 us
    pallas_call x1, Pallas kernels, features_of(): pl.pallas_call(feature_kernel, in_specs=[SMEM, SMEM, VMEM, VMEM, VMEM], o...  4.7 us
    pallas_call x1, Pallas kernels, project(): pl.pallas_call(project_kernel, grid=(rows // tile,), in_specs=[pl.BlockSp...  3.65 us
    ppermute x3, starting transfers between devices, both_ways(): return lax.ppermute(x, axis, [(0, 1), (1, 0)])  3.51 us
  transfers between devices with their start and end apart: 8, of which 6 were waited for; matrix products, arithmetic and copies ran while one was open for 1% of the time, Pallas kernels for 1%

profile of v1, /device:TPU:0, one launch (start us, length us, event | category | flops | bytes accessed | tf_op | source)
XLA Modules:
  0.0 84.8 jit_solution(17508034790197004254)
XLA Ops:
  0.6 1.1 %copy.12.in_ref = bf16[1024,64]{1,0:T(8,128)(2,1)S(1)} copy(bf16[1024,64]{0,1:T(8,128)(2,1)} %param.8) | data formatting | bytes 262144 | tf_op args[2]
  1.7 0.0 copy-start
  1.7 2.0 %copy-done = bf16[1792,1024]{1,0:T(8,128)(2,1)S(1)} copy-done((bf16[1792,1024]{1,0:T(8,128)(2,1)S(1)}, bf16[1792,1024]{1,0:T(8,128)(2,1)}, u32[]{:S(2)}) %copy-start) | copy-done | bytes 3670040
  3.8 0.0 copy-start.1
  3.8 2.0 %copy-done.1 = bf16[1792,1024]{1,0:T(8,128)(2,1)S(1)} copy-done((bf16[1792,1024]{1,0:T(8,128)(2,1)S(1)}, bf16[1792,1024]{1,0:T(8,128)(2,1)}, u32[]{:S(2)}) %copy-start.1) | copy-done | bytes 3670040
  5.8 0.0 copy-start.2
  5.8 0.9 %copy-done.2 = bf16[1024,128]{1,0:T(8,128)(2,1)S(1)} copy-done((bf16[1024,128]{1,0:T(8,128)(2,1)S(1)}, bf16[1024,128]{1,0:T(8,128)(2,1)}, u32[]{:S(2)}) %copy-start.2) | copy-done | bytes 262168
  6.7 3.7 %project.1 = f32[192,1792]{1,0:T(8,128)S(1)} custom-call(bf16[1792,1024]{1,0:T(8,128)(2,1)S(1)} %copy-done, bf16[1792,1024]{1,0:T(8,128)(2,1)S(1)} %copy-done.1, bf16[1024,64]{1,0:T(8,128)(2,1)S(1)} %copy.12.in_ref, bf16[1024,128]{1,0:T(8,128)(2,1)S(1)} %copy-done.2), custom_call_target="tpu_custom_call" | custom-call | tf_op jit(solution)/shard_map/project/pallas_call | solution.py:31
  10.4 0.1 slice.61
  10.5 0.1 select_bitcast_fusion.3
  10.6 0.0 copy-start.3
  10.7 0.5 collective-permute-start
  11.2 1.8 %collective-permute-done = f32[96,1792]{1,0:T(8,128)S(1)} collective-permute-done((f32[96,1792]{1,0:T(8,128)S(1)}, f32[96,1792]{1,0:T(8,128)S(1)}, u32[]{:S(2)}, u32[]{:S(2)}) %collective-permute-start) | collective-permute-done | bytes 688160 | tf_op jit(solution)/shard_map/ppermute | solution.py:177
  13.0 0.1 maximum_add_fusion
  13.1 2.9 %collective-permute-start.1 = (f32[64,1792]{1,0:T(8,128)S(1)}, f32[64,1792]{1,0:T(8,128)S(1)}, u32[]{:S(2)}, u32[]{:S(2)}) collective-permute-start(f32[64,1792]{1,0:T(8,128)S(1)} %pad_maximum_fusion.1), channel_id=1, source_target_pairs={{0,2},{2,0},{1,3},{3,1},{4,6},{6,4},{5,7},{7,5},{8,10},{10,8},{9,1... | collective-permute-start | bytes 1376264 | tf_op jit(solution)/shard_map/ppermute | solution.py:177
  16.0 10.8 %collective-permute-done.1 = f32[64,1792]{1,0:T(8,128)S(1)} collective-permute-done((f32[64,1792]{1,0:T(8,128)S(1)}, f32[64,1792]{1,0:T(8,128)S(1)}, u32[]{:S(2)}, u32[]{:S(2)}) %collective-permute-start.1) | collective-permute-done | bytes 458784 | tf_op jit(solution)/shard_map/ppermute | solution.py:177
  26.9 0.0 copy-start.4
  27.0 0.1 collective-permute-start.2
  27.0 0.0 copy-done.3
  27.1 0.1 copy.11
  27.2 0.1 reduce-window.9
  27.2 0.1 reduce.end_ref
  27.4 1.1 %collective-permute-done.2 = f32[32,1792]{1,0:T(8,128)S(1)} collective-permute-done((f32[32,1792]{1,0:T(8,128)S(1)}, f32[32,1792]{1,0:T(8,128)S(1)}, u32[]{:S(2)}, u32[]{:S(2)}) %collective-permute-start.2) | collective-permute-done | bytes 229408 | tf_op jit(solution)/shard_map/ppermute | solution.py:177
  28.6 0.1 broadcast_in_dim.4.scale_ref
  28.7 4.7 %features.1 = bf16[56,2048]{1,0:T(8,128)(2,1)S(1)} custom-call(s32[56]{0:T(128)S(1)} %bitcast_subtract_fusion.start_ref, s32[56]{0:T(128)S(1)} %reduce.end_ref, f32[64,1792]{1,0:T(8,128)S(1)} %pad_maximum_fusion.3.u_ref, f32[32,1792]{1,0:T(8,128)S(1)} %get-tuple-element.13.v_ref, f32[56,128]{1,0:T(8,128)S(1)} %broadcast_in_dim.4.scale_ref), custom_call_target="tpu_custom_call" | custom-call | tf_op jit(solution)/shard_map/features/pallas_call | solution.py:106
  33.4 21.5 %all_gather.3.row_ref.all_ref = bf16[224,2048]{1,0:T(8,128)(2,1)S(1)} all-gather(bf16[56,2048]{1,0:T(8,128)(2,1)S(1)} %features.1), channel_id=1, replica_groups=mesh['groups'=2,'dp'=4,'feat'=2,'sub'=2] {'dp'}, dimensions={0}, use_global_device_ids=true | all-gather | bytes 1146880 | tf_op jit(solution)/shard_map/all_gather | solution.py:234
  54.9 3.4 %collective-permute-start.3 = (bf16[224,2048]{1,0:T(8,128)(2,1)S(1)}, bf16[224,2048]{1,0:T(8,128)(2,1)S(1)}, u32[]{:S(2)}, u32[]{:S(2)}) collective-permute-start(bf16[224,2048]{1,0:T(8,128)(2,1)S(1)} %all_gather.3.row_ref.all_ref), channel_id=1, source_target_pairs={{0,2},{5,7},{10,8},{15,13},{16,18},{21,23},{26,24},{31,29}} | collective-permute-start | bytes 2752520 | tf_op jit(solution)/shard_map/ppermute | solution.py:210
  58.4 10.8 %collective-permute-done.3 = bf16[224,2048]{1,0:T(8,128)(2,1)S(1)} collective-permute-done((bf16[224,2048]{1,0:T(8,128)(2,1)S(1)}, bf16[224,2048]{1,0:T(8,128)(2,1)S(1)}, u32[]{:S(2)}, u32[]{:S(2)}) %collective-permute-start.3) | collective-permute-done | bytes 917536 | tf_op jit(solution)/shard_map/ppermute | solution.py:210
  69.2 0.1 broadcast_select_fusion
  69.3 1.3 %collective-permute-start.4 = (bf16[224,2048]{1,0:T(8,128)(2,1)S(1)}, bf16[224,2048]{1,0:T(8,128)(2,1)S(1)}, u32[]{:S(2)}, u32[]{:S(2)}) collective-permute-start(bf16[224,2048]{1,0:T(8,128)(2,1)S(1)} %broadcast_select_fusion), channel_id=1, source_target_pairs={{0,1},{5,4},{10,11},{15,14},{2,3},{7,6},{8,9},{13,12},{16,17},{21,... | collective-permute-start | bytes 2752520 | tf_op jit(solution)/shard_map/ppermute | solution.py:214
  70.6 0.0 copy-done.4
  70.7 0.1 copy.13.ids_ref
  70.8 0.7 partial_scores.1
  71.4 0.1 collective-permute-start.7
  71.5 2.5 %collective-permute-start.6 = (f32[56,64]{1,0:T(8,128)S(1)}, f32[56,64]{1,0:T(8,128)S(1)}, u32[]{:S(2)}, u32[]{:S(2)}) collective-permute-start(f32[56,64]{1,0:T(8,128)S(1)} %get-tuple-element.16), channel_id=1, source_target_pairs={{0,2},{1,3},{2,0},{3,1},{4,6},{5,7},{6,4},{7,5},{8,10},{9,11},{10,... | collective-permute-start | bytes 43016 | tf_op jit(solution)/shard_map/ppermute | solution.py:246
  74.1 0.0 collective-permute-start.5
  74.1 0.7 collective-permute-done.7
  74.8 1.3 %collective-permute-done.6 = f32[56,64]{1,0:T(8,128)S(1)} collective-permute-done((f32[56,64]{1,0:T(8,128)S(1)}, f32[56,64]{1,0:T(8,128)S(1)}, u32[]{:S(2)}, u32[]{:S(2)}) %collective-permute-start.6) | collective-permute-done | bytes 14368 | tf_op jit(solution)/shard_map/ppermute | solution.py:246
  76.1 0.0 collective-permute-done.5
  76.2 0.6 fusion.4
  76.8 0.0 collective-permute-done.4
  76.8 0.1 broadcast_select_fusion.1.col_ref
  76.9 7.9 %covariance.1 = f32[2048,2048]{1,0:T(8,128)} custom-call(bf16[224,2048]{1,0:T(8,128)(2,1)S(1)} %all_gather.3.row_ref.all_ref, bf16[224,2048]{1,0:T(8,128)(2,1)S(1)} %broadcast_select_fusion.1.col_ref), custom_call_target="tpu_custom_call" | custom-call | tf_op jit(solution)/shard_map/covariance/pallas_call | solution.py:162
  (11 shorter events, 0.3 us)
Async XLA Ops:
  1.7 2.0 %copy-start = (bf16[1792,1024]{1,0:T(8,128)(2,1)S(1)}, bf16[1792,1024]{1,0:T(8,128)(2,1)}, u32[]{:S(2)}) copy-start(bf16[1792,1024]{1,0:T(8,128)(2,1)} %x_ref.1) | copy-start | bytes 11010052
  3.8 2.0 %copy-start.1 = (bf16[1792,1024]{1,0:T(8,128)(2,1)S(1)}, bf16[1792,1024]{1,0:T(8,128)(2,1)}, u32[]{:S(2)}) copy-start(bf16[1792,1024]{1,0:T(8,128)(2,1)} %g_ref.1) | copy-start | bytes 11010052
  5.8 0.9 %copy-start.2 = (bf16[1024,128]{1,0:T(8,128)(2,1)S(1)}, bf16[1024,128]{1,0:T(8,128)(2,1)}, u32[]{:S(2)}) copy-start(bf16[1024,128]{1,0:T(8,128)(2,1)} %out_ref.1) | copy-start | bytes 786436
  10.6 16.4 %copy-start.3 = (s32[1,56]{1,0:T(1,128)S(1)}, s32[1,56]{1,0:T(1,128)}, u32[]{:S(2)}) copy-start(s32[1,56]{1,0:T(1,128)} %param.10) | copy-start | bytes 676
  10.7 2.3 %collective-permute-start = (f32[96,1792]{1,0:T(8,128)S(1)}, f32[96,1792]{1,0:T(8,128)S(1)}, u32[]{:S(2)}, u32[]{:S(2)}) collective-permute-start(f32[96,1792]{1,0:T(8,128)S(1)} %pad_maximum_fusion), channel_id=1, source_target_pairs={{0,1},{1,0},{2,3},{3,2},{4,5},{5,4},{6,7},{7,6},{8,9},{9,8},{10,11... | collective-permute-start | bytes 2064392 | tf_op jit(solution)/shard_map/ppermute | solution.py:177
  13.1 13.7 %collective-permute-start.1 = (f32[64,1792]{1,0:T(8,128)S(1)}, f32[64,1792]{1,0:T(8,128)S(1)}, u32[]{:S(2)}, u32[]{:S(2)}) collective-permute-start(f32[64,1792]{1,0:T(8,128)S(1)} %pad_maximum_fusion.1), channel_id=1, source_target_pairs={{0,2},{2,0},{1,3},{3,1},{4,6},{6,4},{5,7},{7,5},{8,10},{10,8},{9,1... | collective-permute-start | bytes 1376264 | tf_op jit(solution)/shard_map/ppermute | solution.py:177
  26.9 43.7 %copy-start.4 = (s32[64]{0:T(128)S(1)}, s32[64]{0:T(128)}, u32[]{:S(2)}) copy-start(s32[64]{0:T(128)} %param.11) | copy-start | bytes 772
  27.0 1.6 %collective-permute-start.2 = (f32[32,1792]{1,0:T(8,128)S(1)}, f32[32,1792]{1,0:T(8,128)S(1)}, u32[]{:S(2)}, u32[]{:S(2)}) collective-permute-start(f32[32,1792]{1,0:T(8,128)S(1)} %slice.69), channel_id=1, source_target_pairs={{0,1},{1,0},{2,3},{3,2},{4,5},{5,4},{6,7},{7,6},{8,9},{9,8},{10,11... | collective-permute-start | bytes 688136 | tf_op jit(solution)/shard_map/ppermute | solution.py:177
  54.9 14.3 %collective-permute-start.3 = (bf16[224,2048]{1,0:T(8,128)(2,1)S(1)}, bf16[224,2048]{1,0:T(8,128)(2,1)S(1)}, u32[]{:S(2)}, u32[]{:S(2)}) collective-permute-start(bf16[224,2048]{1,0:T(8,128)(2,1)S(1)} %all_gather.3.row_ref.all_ref), channel_id=1, source_target_pairs={{0,2},{5,7},{10,8},{15,13},{16,18},{21,23},{26,24},{31,29}} | collective-permute-start | bytes 2752520 | tf_op jit(solution)/shard_map/ppermute | solution.py:210
  69.3 7.5 %collective-permute-start.4 = (bf16[224,2048]{1,0:T(8,128)(2,1)S(1)}, bf16[224,2048]{1,0:T(8,128)(2,1)S(1)}, u32[]{:S(2)}, u32[]{:S(2)}) collective-permute-start(bf16[224,2048]{1,0:T(8,128)(2,1)S(1)} %broadcast_select_fusion), channel_id=1, source_target_pairs={{0,1},{5,4},{10,11},{15,14},{2,3},{7,6},{8,9},{13,12},{16,17},{21,... | collective-permute-start | bytes 2752520 | tf_op jit(solution)/shard_map/ppermute | solution.py:214
  71.4 3.4 %collective-permute-start.7 = (f32[56,64]{1,0:T(8,128)S(1)}, f32[56,64]{1,0:T(8,128)S(1)}, u32[]{:S(2)}, u32[]{:S(2)}) collective-permute-start(f32[56,64]{1,0:T(8,128)S(1)} %get-tuple-element.15), channel_id=1, source_target_pairs={{0,3},{1,2},{2,1},{3,0},{4,7},{5,6},{6,5},{7,4},{8,11},{9,10},{10,... | collective-permute-start | bytes 43016 | tf_op jit(solution)/shard_map/ppermute | solution.py:246
  71.5 4.6 %collective-permute-start.6 = (f32[56,64]{1,0:T(8,128)S(1)}, f32[56,64]{1,0:T(8,128)S(1)}, u32[]{:S(2)}, u32[]{:S(2)}) collective-permute-start(f32[56,64]{1,0:T(8,128)S(1)} %get-tuple-element.16), channel_id=1, source_target_pairs={{0,2},{1,3},{2,0},{3,1},{4,6},{5,7},{6,4},{7,5},{8,10},{9,11},{10,... | collective-permute-start | bytes 43016 | tf_op jit(solution)/shard_map/ppermute | solution.py:246
  74.1 2.1 %collective-permute-start.5 = (f32[56,64]{1,0:T(8,128)S(1)}, f32[56,64]{1,0:T(8,128)S(1)}, u32[]{:S(2)}, u32[]{:S(2)}) collective-permute-start(f32[56,64]{1,0:T(8,128)S(1)} %get-tuple-element.14), channel_id=1, source_target_pairs={{0,1},{1,0},{2,3},{3,2},{4,5},{5,4},{6,7},{7,6},{8,9},{9,8},{10,11... | collective-permute-start | bytes 43016 | tf_op jit(solution)/shard_map/ppermute | solution.py:246

commit v2 on v1

--- a/solution.py
+++ b/solution.py
@@ -16,32 +16,53 @@
     return pltpu.CompilerParams(vmem_limit_bytes=mib * MIB)
 
 
-def project_kernel(x_ref, g_ref, in_ref, out_ref, full_ref):
-    rank_in = in_ref.shape[1]
-    u = jnp.dot(x_ref[...], in_ref[...], preferred_element_type=F32)
-    v = jnp.dot(g_ref[...], out_ref[...], preferred_element_type=F32)
-    full_ref[0:rank_in, :] = jnp.transpose(u)
-    full_ref[rank_in:, :] = jnp.transpose(v)
+def project_kernel(x_hbm, g_hbm, in_ref, out_ref, full_ref, x_ref, g_ref, flip_ref, x_sem, g_sem):
+    rank_in = in_ref.shape[0]
+    rows = x_ref.shape[0]
+    steps = x_sem.shape[0]
+    tile = rows // steps
+    copies = []
+    for i in range(steps):
+        at = pl.ds(i * tile, tile)
+        copies.append(
+            (
+                pltpu.make_async_copy(x_hbm.at[at], x_ref.at[at], x_sem.at[i]),
+                pltpu.make_async_copy(g_hbm.at[at], g_ref.at[at], g_sem.at[i]),
+            )
+        )
+    for x_copy, g_copy in copies:
+        x_copy.start()
+        g_copy.start()
+    flip_ref[...] = jnp.transpose(in_ref[...])
+    for i, (x_copy, g_copy) in enumerate(copies):
+        at = slice(i * tile, (i + 1) * tile)
+        x_copy.wait()
+        u = jnp.dot(x_ref[at, :], flip_ref[...], preferred_element_type=F32)
+        full_ref[0:rank_in, at] = jnp.transpose(u)
+        g_copy.wait()
+        v = jnp.dot(g_ref[at, :], out_ref[...], preferred_element_type=F32)
+        full_ref[rank_in:, at] = jnp.transpose(v)
 
 
 def project(layer_inputs, output_grads, proj_in, proj_out):
     rows, width = layer_inputs.shape
-    tile = 256
+    steps = rows // 256
     total = proj_in.shape[1] + proj_out.shape[1]
     return pl.pallas_call(
         project_kernel,
-        grid=(rows // tile,),
-        in_specs=[
-            pl.BlockSpec((tile, width), lambda i: (i, 0)),
-            pl.BlockSpec((tile, width), lambda i: (i, 0)),
-            pl.BlockSpec(proj_in.shape, lambda i: (0, 0)),
-            pl.BlockSpec(proj_out.shape, lambda i: (0, 0)),
+        in_specs=[pl.BlockSpec(memory_space=pltpu.HBM)] * 2 + [VMEM, VMEM],
+        out_specs=VMEM,
+        out_shape=jax.ShapeDtypeStruct((total, rows), F32),
+        scratch_shapes=[
+            pltpu.VMEM((rows, width), BF16),
+            pltpu.VMEM((rows, width), BF16),
+            pltpu.VMEM(proj_in.shape, BF16),
+            pltpu.SemaphoreType.DMA((steps,)),
+            pltpu.SemaphoreType.DMA((steps,)),
         ],
-        out_specs=pl.BlockSpec((total, tile), lambda i: (0, i)),
-        out_shape=jax.ShapeDtypeStruct((total, rows), F32),
-        compiler_params=params(16),
+        compiler_params=params(58),
         name="project",
-    )(layer_inputs, output_grads, proj_in, proj_out)
+    )(layer_inputs, output_grads, jnp.transpose(proj_in), proj_out)
 
 
 def split(x):
@@ -143,6 +164,7 @@
         out_specs=VMEM,
         out_shape=jax.ShapeDtypeStruct((gathered.shape[0], ids.shape[0]), F32),
         compiler_params=params(24),
+        cost_estimate=pl.CostEstimate(flops=8 * gathered.size * ids.shape[0], bytes_accessed=2 * gathered.size, transcendentals=0),
         name="partial_scores",
     )(ids[:, None], gathered)
 
@@ -169,6 +191,7 @@
         out_specs=pl.BlockSpec((tile, cols), lambda i: (i, 0)),
         out_shape=jax.ShapeDtypeStruct((rows, cols), F32),
         compiler_params=params(24),
+        cost_estimate=pl.CostEstimate(flops=2 * seqs * rows * cols, bytes_accessed=4 * rows * cols, transcendentals=0),
         name="covariance",
     )(gathered, other_cols)
 
@@ -199,21 +222,38 @@
     return u, v_mine
 
 
+def is_square():
+    return lax.axis_size("feat") == 2 and lax.axis_size("sub") == 2 and lax.axis_size("dp") == 4
+
+
+RING = (0, 1, 3, 2)
+
+
+def ring_place(d):
+    return d ^ (d >> 1)
+
+
+def around(part):
+    return lax.ppermute(part, "dp", [(RING[i], RING[(i + 1) % 4]) for i in range(4)])
+
+
+def sent_across(part):
+    return lax.ppermute(part, ("dp",) + WIDE, [(4 * d + d, 4 * d + (d ^ 2)) for d in range(4)])
+
+
+def spread(part, over):
+    at = lax.axis_index("dp")
+    me = lax.axis_index(WIDE)
+    held = jnp.where(me == at, part, over)
+    pairs = [(4 * d + d, 4 * d + (d ^ 1)) for d in range(4)]
+    pairs += [(4 * d + (d ^ 2), 4 * d + (d ^ 3)) for d in range(4)]
+    beside = lax.ppermute(held, ("dp",) + WIDE, pairs)
+    return jnp.where((me == at) | (me == (at ^ 2)), held, beside)
+
+
 def column_block(gathered, col_width):
-    group = lax.axis_size(WIDE)
     block_width = gathered.shape[1]
-    dp = lax.axis_size("dp")
-    at = lax.axis_index("dp")
-    if lax.axis_size("feat") == 2 and lax.axis_size("sub") == 2 and dp == 4:
-        axes = ("dp",) + WIDE
-        me = lax.axis_index(WIDE)
-        over = lax.ppermute(gathered, axes, [(4 * d + d, 4 * d + (d ^ 2)) for d in range(4)])
-        held = jnp.where(me == at, gathered, over)
-        across = [(4 * d + d, 4 * d + (d ^ 1)) for d in range(4)]
-        across += [(4 * d + (d ^ 2), 4 * d + (d ^ 3)) for d in range(4)]
-        beside = lax.ppermute(held, axes, across)
-        return jnp.where((me == at) | (me == (at ^ 2)), held, beside)
-    col_start = at * col_width
+    col_start = lax.axis_index("dp") * col_width
     owner = col_start // block_width
     own_slice = lax.dynamic_slice_in_dim(gathered, col_start % block_width, col_width, 1)
     every_slice = lax.all_gather(own_slice, WIDE, axis=1, tiled=True)
@@ -231,22 +271,36 @@
     starts = ends - seq_len
     scale = jnp.broadcast_to(1.0 / jnp.sqrt(seq_len.astype(F32))[:, None], (seq_len.shape[0], 2 * rank_in))
     local_feat = features_of(starts, ends, u, v_mine, scale)
-    gathered = lax.all_gather(local_feat, "dp", axis=0, tiled=True)
-    block_width = gathered.shape[1]
-    col_width = block_width * group // lax.axis_size("dp")
-    other_cols = column_block(gathered, col_width)
-    part = partial_scores_of(target_ids, gathered)
+    me = lax.axis_index(WIDE)
+    at = lax.axis_index("dp")
+    if is_square():
+        chunks, across = [local_feat], []
+        for k in range(4):
+            if k < 3:
+                chunks.append(around(chunks[k]))
+            across.append(sent_across(chunks[k]))
+            if k < 3:
+                chunks[-1], across[-1] = lax.optimization_barrier((chunks[-1], across[-1]))
+        gathered = jnp.concatenate(chunks)
+        early = spread(jnp.concatenate(chunks[:3]), jnp.concatenate(across[:3]))
+        other_cols = jnp.concatenate([early, spread(chunks[3], across[3])])
+        seqs = local_feat.shape[0]
+        ids = ((ring_place(at) - ring_place(target_ids // seqs)) & 3) * seqs + target_ids % seqs
+    else:
+        gathered = lax.all_gather(local_feat, "dp", axis=0, tiled=True)
+        other_cols = column_block(gathered, gathered.shape[1] * group // lax.axis_size("dp"))
+        ids = target_ids
+    part = partial_scores_of(ids, gathered)
     own = part.shape[0] // group
-    me = lax.axis_index(WIDE)
-    if lax.axis_size("feat") == 2 and lax.axis_size("sub") == 2:
+    if is_square():
         pieces = part.reshape(group, own, -1)
-        total = lax.dynamic_index_in_dim(pieces, me, 0, keepdims=False)
+        total = lax.dynamic_index_in_dim(pieces, (ring_place(at) - ring_place(me)) & 3, 0, keepdims=False)
         for k in range(1, group):
-            given = lax.dynamic_index_in_dim(pieces, me ^ k, 0, keepdims=False)
+            given = lax.dynamic_index_in_dim(pieces, (ring_place(at) - ring_place(me ^ k)) & 3, 0, keepdims=False)
             total = total + lax.ppermute(given, WIDE, [(i, i ^ k) for i in range(group)])
     else:
         total = lax.psum_scatter(part, WIDE, scatter_dimension=0, tiled=True)
-    scores = jnp.transpose(total) / jnp.sqrt(jnp.float32(block_width * group))
+    scores = jnp.transpose(total) / jnp.sqrt(jnp.float32(gathered.shape[1] * group))
     return (covariance_of(gathered, other_cols), scores)
 
 

time: 85.3 us -> 79.4 us (0.931)
  blocking collectives: 21.5 us -> 0 us
  starting transfers between devices: 11 us -> 26.7 us
  local copies, waits for them, and re-layouts: 6.47 us -> 1.85 us
  Pallas kernels: 16.9 us -> 21.4 us
    all_gather x1 -> x0, blocking collectives: 21.5 us -> none  [shards(): gathered = lax.all_gather(local_feat, 'dp', axis=0, tiled=True)]
    ppermute x2 -> x9, starting transfers between devices: 4.79 us -> 21.3 us  [the longest x4 14.8 us: sent_across(): lax.ppermute(part, ('dp',) + WIDE, [(4 * d + d, 4 * d + (d ^ 2)) for d in...]
    unnamed x11 -> x6, local copies, waits for them, and re-layouts: 6.11 us -> 1.33 us
    pallas_call x1, Pallas kernels: 3.65 us -> 8.12 us  [project(): pl.pallas_call(project_kernel, in_specs=[pl.BlockSpec(memory_space=pltpu....]
    ppermute x3, waiting for transfers between devices: 2.04 us -> 0.01 us  [shards(): lax.ppermute(given, WIDE, [(i, i ^ k) for i in range(group)])]
    ppermute x2 -> x9, waiting for transfers between devices: 10.8 us -> 12.6 us  [the longest x3 9.26 us: around(): lax.ppermute(part, 'dp', [(RING[i], RING[(i + 1) % 4]) for i in range(4)])]
  transfers between devices with their start and end apart: 8 -> 15, of which waited for: 6 -> 9; matrix products, arithmetic and copies ran while one was open for 1% -> 2% of each run, Pallas kernels for 1% -> 1%
where the time goes in v2:
time: 79.4 us; the launch traced here: 79 us
  starting transfers between devices  26.7 us (34%)
  waiting for transfers between devices  26.3 us (33%)
  Pallas kernels  21.4 us (27%)
  local copies, waits for them, and re-layouts  1.85 us (2%)
  other arithmetic  1.81 us (2%)
  between operations  0.95 us (1%)
    ppermute x4, starting transfers between devices, sent_across(): lax.ppermute(part, ('dp',) + WIDE, [(4 * d + d, 4 * d + (d ^ 2)) for d in...  14.8 us
    ppermute x3, waiting for transfers between devices, both_ways(): return lax.ppermute(x, axis, [(0, 1), (1, 0)])  13.7 us
    ppermute x3, waiting for transfers between devices, around(): lax.ppermute(part, 'dp', [(RING[i], RING[(i + 1) % 4]) for i in range(4)])  9.26 us
    pallas_call x1, Pallas kernels, project(): pl.pallas_call(project_kernel, in_specs=[pl.BlockSpec(memory_space=pltpu....  8.12 us
    pallas_call x1, Pallas kernels, covariance_of(): pl.pallas_call(covariance_kernel, grid=(rows // tile,), in_specs=[pl.Bloc...  7.9 us
    pallas_call x1, Pallas kernels, features_of(): pl.pallas_call(feature_kernel, in_specs=[SMEM, SMEM, VMEM, VMEM, VMEM], o...  4.72 us
    ppermute x3, starting transfers between devices, around(): lax.ppermute(part, 'dp', [(RING[i], RING[(i + 1) % 4]) for i in range(4)])  3.87 us
    ppermute x3, starting transfers between devices, both_ways(): return lax.ppermute(x, axis, [(0, 1), (1, 0)])  3.51 us
  transfers between devices with their start and end apart: 15, of which 9 were waited for; matrix products, arithmetic and copies ran while one was open for 2% of the time, Pallas kernels for 1%

profile of v2, /device:TPU:0, one launch (start us, length us, event | category | flops | bytes accessed | tf_op | source)
XLA Modules:
  0.0 79.0 jit_solution(16426765870890921319)
XLA Ops:
  0.6 8.1 %project.1 = f32[192,1792]{1,0:T(8,128)} custom-call(bf16[1792,1024]{1,0:T(8,128)(2,1)} %x_hbm.1, bf16[1792,1024]{1,0:T(8,128)(2,1)} %g_hbm.1, bf16[64,1024]{1,0:T(8,128)(2,1)} %bitcast.40, bf16[1024,128]{1,0:T(8,128)(2,1)} %out_ref.1), custom_call_target="tpu_custom_call" | custom-call | tf_op jit(solution)/shard_map/project/pallas_call | solution.py:51
  8.8 0.0 copy-start
  8.8 0.0 slice-start
  8.8 1.3 %copy-done = f32[192,1792]{1,0:T(8,128)S(1)} copy-done((f32[192,1792]{1,0:T(8,128)S(1)}, f32[192,1792]{1,0:T(8,128)}, u32[]{:S(2)}) %copy-start) | copy-done | bytes 1376280
  10.1 0.2 slice-done
  10.4 0.1 select_bitcast_fusion.3
  10.5 0.5 collective-permute-start
  11.0 1.8 %collective-permute-done = f32[96,1792]{1,0:T(8,128)S(1)} collective-permute-done((f32[96,1792]{1,0:T(8,128)S(1)}, f32[96,1792]{1,0:T(8,128)S(1)}, u32[]{:S(2)}, u32[]{:S(2)}) %collective-permute-start) | collective-permute-done | bytes 688160 | tf_op jit(solution)/shard_map/ppermute | solution.py:200
  12.8 0.1 maximum_add_fusion
  12.8 0.0 copy-start.1
  12.9 2.9 %collective-permute-start.1 = (f32[64,1792]{1,0:T(8,128)S(1)}, f32[64,1792]{1,0:T(8,128)S(1)}, u32[]{:S(2)}, u32[]{:S(2)}) collective-permute-start(f32[64,1792]{1,0:T(8,128)S(1)} %pad_maximum_fusion.3), channel_id=1, source_target_pairs={{0,2},{2,0},{1,3},{3,1},{4,6},{6,4},{5,7},{7,5},{8,10},{10,8},{9,1... | collective-permute-start | bytes 1376264 | tf_op jit(solution)/shard_map/ppermute | solution.py:200
  15.9 10.8 %collective-permute-done.1 = f32[64,1792]{1,0:T(8,128)S(1)} collective-permute-done((f32[64,1792]{1,0:T(8,128)S(1)}, f32[64,1792]{1,0:T(8,128)S(1)}, u32[]{:S(2)}, u32[]{:S(2)}) %collective-permute-start.1) | collective-permute-done | bytes 458784 | tf_op jit(solution)/shard_map/ppermute | solution.py:200
  26.8 0.0 copy-start.2
  26.8 0.1 collective-permute-start.2
  26.9 0.1 copy.10
  27.0 0.1 reduce-window.9
  27.1 0.1 reduce.end_ref
  27.2 1.1 %collective-permute-done.2 = f32[32,1792]{1,0:T(8,128)S(1)} collective-permute-done((f32[32,1792]{1,0:T(8,128)S(1)}, f32[32,1792]{1,0:T(8,128)S(1)}, u32[]{:S(2)}, u32[]{:S(2)}) %collective-permute-start.2) | collective-permute-done | bytes 229408 | tf_op jit(solution)/shard_map/ppermute | solution.py:200
  28.3 0.1 broadcast_select_fusion.4
  28.4 0.1 broadcast_in_dim.4.scale_ref
  28.5 4.7 %features.1 = bf16[56,2048]{1,0:T(8,128)(2,1)S(1)} custom-call(s32[56]{0:T(128)S(1)} %bitcast_subtract_fusion.start_ref, s32[56]{0:T(128)S(1)} %reduce.end_ref, f32[64,1792]{1,0:T(8,128)S(1)} %pad_maximum_fusion.5.u_ref, f32[32,1792]{1,0:T(8,128)S(1)} %get-tuple-element.25.v_ref, f32[56,128]{1,0:T(8,128)S(1)} %broadcast_in_dim.4.scale_ref), custom_call_target="tpu_custom_call" | custom-call | tf_op jit(solution)/shard_map/features/pallas_call | solution.py:127
  33.2 1.9 %collective-permute-start.3 = (bf16[56,2048]{1,0:T(8,128)(2,1)S(1)}, bf16[56,2048]{1,0:T(8,128)(2,1)S(1)}, u32[]{:S(2)}, u32[]{:S(2)}) collective-permute-start(bf16[56,2048]{1,0:T(8,128)(2,1)S(1)} %features.1), channel_id=1, source_target_pairs={{0,4},{4,12},{12,8},{8,0},{1,5},{5,13},{13,9},{9,1},{2,6},{6,14},{... | collective-permute-start | bytes 688136 | tf_op jit(solution)/shard_map/ppermute | solution.py:237
  35.1 3.4 %collective-permute-start.4 = (bf16[56,2048]{1,0:T(8,128)(2,1)S(1)}, bf16[56,2048]{1,0:T(8,128)(2,1)S(1)}, u32[]{:S(2)}, u32[]{:S(2)}) collective-permute-start(bf16[56,2048]{1,0:T(8,128)(2,1)S(1)} %features.1), channel_id=1, source_target_pairs={{0,2},{5,7},{10,8},{15,13},{16,18},{21,23},{26,24},{31,29}} | collective-permute-start | bytes 688136 | tf_op jit(solution)/shard_map/ppermute | solution.py:241
  38.5 3.5 %collective-permute-done.3 = bf16[56,2048]{1,0:T(8,128)(2,1)S(1)} collective-permute-done((bf16[56,2048]{1,0:T(8,128)(2,1)S(1)}, bf16[56,2048]{1,0:T(8,128)(2,1)S(1)}, u32[]{:S(2)}, u32[]{:S(2)}) %collective-permute-start.3) | collective-permute-done | bytes 229408 | tf_op jit(solution)/shard_map/ppermute | solution.py:237
  42.0 0.8 %collective-permute-start.5 = (bf16[56,2048]{1,0:T(8,128)(2,1)S(1)}, bf16[56,2048]{1,0:T(8,128)(2,1)S(1)}, u32[]{:S(2)}, u32[]{:S(2)}) collective-permute-start(bf16[56,2048]{1,0:T(8,128)(2,1)S(1)} %collective-permute-done.3), channel_id=1, source_target_pairs={{0,4},{4,12},{12,8},{8,0},{1,5},{5,13},{13,9},{9,1},{2,6},{6,14},{... | collective-permute-start | bytes 688136 | tf_op jit(solution)/shard_map/ppermute | solution.py:237
  42.9 3.5 %collective-permute-start.6 = (bf16[56,2048]{1,0:T(8,128)(2,1)S(1)}, bf16[56,2048]{1,0:T(8,128)(2,1)S(1)}, u32[]{:S(2)}, u32[]{:S(2)}) collective-permute-start(bf16[56,2048]{1,0:T(8,128)(2,1)S(1)} %collective-permute-done.3), channel_id=1, source_target_pairs={{0,2},{5,7},{10,8},{15,13},{16,18},{21,23},{26,24},{31,29}} | collective-permute-start | bytes 688136 | tf_op jit(solution)/shard_map/ppermute | solution.py:241
  46.4 3.5 %collective-permute-done.5 = bf16[56,2048]{1,0:T(8,128)(2,1)S(1)} collective-permute-done((bf16[56,2048]{1,0:T(8,128)(2,1)S(1)}, bf16[56,2048]{1,0:T(8,128)(2,1)S(1)}, u32[]{:S(2)}, u32[]{:S(2)}) %collective-permute-start.5) | collective-permute-done | bytes 229408 | tf_op jit(solution)/shard_map/ppermute | solution.py:237
  50.0 1.1 %collective-permute-start.7 = (bf16[56,2048]{1,0:T(8,128)(2,1)S(1)}, bf16[56,2048]{1,0:T(8,128)(2,1)S(1)}, u32[]{:S(2)}, u32[]{:S(2)}) collective-permute-start(bf16[56,2048]{1,0:T(8,128)(2,1)S(1)} %collective-permute-done.5), channel_id=1, source_target_pairs={{0,4},{4,12},{12,8},{8,0},{1,5},{5,13},{13,9},{9,1},{2,6},{6,14},{... | collective-permute-start | bytes 688136 | tf_op jit(solution)/shard_map/ppermute | solution.py:237
  51.1 3.5 %collective-permute-start.8 = (bf16[56,2048]{1,0:T(8,128)(2,1)S(1)}, bf16[56,2048]{1,0:T(8,128)(2,1)S(1)}, u32[]{:S(2)}, u32[]{:S(2)}) collective-permute-start(bf16[56,2048]{1,0:T(8,128)(2,1)S(1)} %collective-permute-done.5), channel_id=1, source_target_pairs={{0,2},{5,7},{10,8},{15,13},{16,18},{21,23},{26,24},{31,29}} | collective-permute-start | bytes 688136 | tf_op jit(solution)/shard_map/ppermute | solution.py:241
  54.7 0.1 copy.11.ids_ref
  54.7 2.2 %collective-permute-done.7 = bf16[56,2048]{1,0:T(8,128)(2,1)S(1)} collective-permute-done((bf16[56,2048]{1,0:T(8,128)(2,1)S(1)}, bf16[56,2048]{1,0:T(8,128)(2,1)S(1)}, u32[]{:S(2)}, u32[]{:S(2)}) %collective-permute-start.7) | collective-permute-done | bytes 229408 | tf_op jit(solution)/shard_map/ppermute | solution.py:237
  57.0 1.1 %collective-permute-done.8 = bf16[56,2048]{1,0:T(8,128)(2,1)S(1)} collective-permute-done((bf16[56,2048]{1,0:T(8,128)(2,1)S(1)}, bf16[56,2048]{1,0:T(8,128)(2,1)S(1)}, u32[]{:S(2)}, u32[]{:S(2)}) %collective-permute-start.8) | collective-permute-done | bytes 229408 | tf_op jit(solution)/shard_map/ppermute | solution.py:241
  58.1 4.4 %collective-permute-start.10 = (bf16[56,2048]{1,0:T(8,128)(2,1)S(1)}, bf16[56,2048]{1,0:T(8,128)(2,1)S(1)}, u32[]{:S(2)}, u32[]{:S(2)}) collective-permute-start(bf16[56,2048]{1,0:T(8,128)(2,1)S(1)} %collective-permute-done.7), channel_id=1, source_target_pairs={{0,2},{5,7},{10,8},{15,13},{16,18},{21,23},{26,24},{31,29}} | collective-permute-start | bytes 688136 | tf_op jit(solution)/shard_map/ppermute | solution.py:241
  62.5 0.1 pad_maximum_fusion.row_ref.all_ref
  62.6 0.7 partial_scores.1
  63.2 0.1 collective-permute-start.14
  63.3 0.1 collective-permute-start.13
  63.4 1.8 %collective-permute-start.12 = (f32[56,64]{1,0:T(8,128)S(1)}, f32[56,64]{1,0:T(8,128)S(1)}, u32[]{:S(2)}, u32[]{:S(2)}) collective-permute-start(f32[56,64]{1,0:T(8,128)S(1)} %get-tuple-element.26), channel_id=1, source_target_pairs={{0,1},{1,0},{2,3},{3,2},{4,5},{5,4},{6,7},{7,6},{8,9},{9,8},{10,11... | collective-permute-start | bytes 43016 | tf_op jit(solution)/shard_map/ppermute | solution.py:300
  65.2 1.1 %collective-permute-done.10 = bf16[56,2048]{1,0:T(8,128)(2,1)S(1)} collective-permute-done((bf16[56,2048]{1,0:T(8,128)(2,1)S(1)}, bf16[56,2048]{1,0:T(8,128)(2,1)S(1)}, u32[]{:S(2)}, u32[]{:S(2)}) %collective-permute-start.10) | collective-permute-done | bytes 229408 | tf_op jit(solution)/shard_map/ppermute | solution.py:241
  66.3 1.3 %collective-permute-start.11 = (bf16[56,2048]{1,0:T(8,128)(2,1)S(1)}, bf16[56,2048]{1,0:T(8,128)(2,1)S(1)}, u32[]{:S(2)}, u32[]{:S(2)}) collective-permute-start(bf16[56,2048]{1,0:T(8,128)(2,1)S(1)} %broadcast_select_fusion.1), channel_id=1, source_target_pairs={{0,1},{5,4},{10,11},{15,14},{2,3},{7,6},{8,9},{13,12},{16,17},{21,... | collective-permute-start | bytes 688136 | tf_op jit(solution)/shard_map/ppermute | solution.py:250
  67.7 0.2 maximum_select_fusion
  67.9 1.3 %collective-permute-start.9 = (bf16[168,2048]{1,0:T(8,128)(2,1)S(1)}, bf16[168,2048]{1,0:T(8,128)(2,1)S(1)}, u32[]{:S(2)}, u32[]{:S(2)}) collective-permute-start(bf16[168,2048]{1,0:T(8,128)(2,1)S(1)} %maximum_select_fusion), channel_id=1, source_target_pairs={{0,1},{5,4},{10,11},{15,14},{2,3},{7,6},{8,9},{13,12},{16,17},{21,... | collective-permute-start | bytes 2064392 | tf_op jit(solution)/shard_map/ppermute | solution.py:250
  69.2 0.0 collective-permute-done.14
  69.3 0.6 fusion.4
  69.9 1.0 %collective-permute-done.9 = bf16[168,2048]{1,0:T(8,128)(2,1)S(1)} collective-permute-done((bf16[168,2048]{1,0:T(8,128)(2,1)S(1)}, bf16[168,2048]{1,0:T(8,128)(2,1)S(1)}, u32[]{:S(2)}, u32[]{:S(2)}) %collective-permute-start.9) | collective-permute-done | bytes 688160 | tf_op jit(solution)/shard_map/ppermute | solution.py:250
  71.0 0.1 broadcast_select_fusion
  71.0 0.1 pad_maximum_fusion.1.col_ref
  71.1 7.9 %covariance.1 = f32[2048,2048]{1,0:T(8,128)} custom-call(bf16[224,2048]{1,0:T(8,128)(2,1)S(1)} %pad_maximum_fusion.row_ref.all_ref, bf16[224,2048]{1,0:T(8,128)(2,1)S(1)} %pad_maximum_fusion.1.col_ref), custom_call_target="tpu_custom_call" | custom-call | flops 1879048192 | bytes 16777216 | tf_op jit(solution)/shard_map/covariance/pallas_call | solution.py:184
  (20 shorter events, 0.4 us)
Async XLA Ops:
  8.8 1.3 %copy-start = (f32[192,1792]{1,0:T(8,128)S(1)}, f32[192,1792]{1,0:T(8,128)}, u32[]{:S(2)}) copy-start(f32[192,1792]{1,0:T(8,128)} %project.1) | copy-start | bytes 4128772
  8.8 1.6 %slice-start = ((f32[192,1792]{1,0:T(8,128)}), f32[128,1792]{1,0:T(8,128)S(1)}, s32[]{:S(2)}) async-start(f32[192,1792]{1,0:T(8,128)} %project.1), calls=%async_computation | async-start | bytes 1835008 | tf_op jit(solution)/shard_map/slice | solution.py:210
  10.5 2.3 %collective-permute-start = (f32[96,1792]{1,0:T(8,128)S(1)}, f32[96,1792]{1,0:T(8,128)S(1)}, u32[]{:S(2)}, u32[]{:S(2)}) collective-permute-start(f32[96,1792]{1,0:T(8,128)S(1)} %pad_maximum_fusion.2), channel_id=1, source_target_pairs={{0,1},{1,0},{2,3},{3,2},{4,5},{5,4},{6,7},{7,6},{8,9},{9,8},{10,11... | collective-permute-start | bytes 2064392 | tf_op jit(solution)/shard_map/ppermute | solution.py:200
  12.8 14.0 %copy-start.1 = (s32[1,56]{1,0:T(1,128)S(1)}, s32[1,56]{1,0:T(1,128)}, u32[]{:S(2)}) copy-start(s32[1,56]{1,0:T(1,128)} %param.10) | copy-start | bytes 676
  12.9 13.7 %collective-permute-start.1 = (f32[64,1792]{1,0:T(8,128)S(1)}, f32[64,1792]{1,0:T(8,128)S(1)}, u32[]{:S(2)}, u32[]{:S(2)}) collective-permute-start(f32[64,1792]{1,0:T(8,128)S(1)} %pad_maximum_fusion.3), channel_id=1, source_target_pairs={{0,2},{2,0},{1,3},{3,1},{4,6},{6,4},{5,7},{7,5},{8,10},{10,8},{9,1... | collective-permute-start | bytes 1376264 | tf_op jit(solution)/shard_map/ppermute | solution.py:200
  26.8 27.8 %copy-start.2 = (s32[64]{0:T(128)S(1)}, s32[64]{0:T(128)}, u32[]{:S(2)}) copy-start(s32[64]{0:T(128)} %param.11) | copy-start | bytes 772
  26.8 1.6 %collective-permute-start.2 = (f32[32,1792]{1,0:T(8,128)S(1)}, f32[32,1792]{1,0:T(8,128)S(1)}, u32[]{:S(2)}, u32[]{:S(2)}) collective-permute-start(f32[32,1792]{1,0:T(8,128)S(1)} %slice.69), channel_id=1, source_target_pairs={{0,1},{1,0},{2,3},{3,2},{4,5},{5,4},{6,7},{7,6},{8,9},{9,8},{10,11... | collective-permute-start | bytes 688136 | tf_op jit(solution)/shard_map/ppermute | solution.py:200
  33.2 8.8 %collective-permute-start.3 = (bf16[56,2048]{1,0:T(8,128)(2,1)S(1)}, bf16[56,2048]{1,0:T(8,128)(2,1)S(1)}, u32[]{:S(2)}, u32[]{:S(2)}) collective-permute-start(bf16[56,2048]{1,0:T(8,128)(2,1)S(1)} %features.1), channel_id=1, source_target_pairs={{0,4},{4,12},{12,8},{8,0},{1,5},{5,13},{13,9},{9,1},{2,6},{6,14},{... | collective-permute-start | bytes 688136 | tf_op jit(solution)/shard_map/ppermute | solution.py:237
  35.1 6.9 %collective-permute-start.4 = (bf16[56,2048]{1,0:T(8,128)(2,1)S(1)}, bf16[56,2048]{1,0:T(8,128)(2,1)S(1)}, u32[]{:S(2)}, u32[]{:S(2)}) collective-permute-start(bf16[56,2048]{1,0:T(8,128)(2,1)S(1)} %features.1), channel_id=1, source_target_pairs={{0,2},{5,7},{10,8},{15,13},{16,18},{21,23},{26,24},{31,29}} | collective-permute-start | bytes 688136 | tf_op jit(solution)/shard_map/ppermute | solution.py:241
  42.0 7.9 %collective-permute-start.5 = (bf16[56,2048]{1,0:T(8,128)(2,1)S(1)}, bf16[56,2048]{1,0:T(8,128)(2,1)S(1)}, u32[]{:S(2)}, u32[]{:S(2)}) collective-permute-start(bf16[56,2048]{1,0:T(8,128)(2,1)S(1)} %collective-permute-done.3), channel_id=1, source_target_pairs={{0,4},{4,12},{12,8},{8,0},{1,5},{5,13},{13,9},{9,1},{2,6},{6,14},{... | collective-permute-start | bytes 688136 | tf_op jit(solution)/shard_map/ppermute | solution.py:237
  42.9 7.1 %collective-permute-start.6 = (bf16[56,2048]{1,0:T(8,128)(2,1)S(1)}, bf16[56,2048]{1,0:T(8,128)(2,1)S(1)}, u32[]{:S(2)}, u32[]{:S(2)}) collective-permute-start(bf16[56,2048]{1,0:T(8,128)(2,1)S(1)} %collective-permute-done.3), channel_id=1, source_target_pairs={{0,2},{5,7},{10,8},{15,13},{16,18},{21,23},{26,24},{31,29}} | collective-permute-start | bytes 688136 | tf_op jit(solution)/shard_map/ppermute | solution.py:241
  50.0 7.0 %collective-permute-start.7 = (bf16[56,2048]{1,0:T(8,128)(2,1)S(1)}, bf16[56,2048]{1,0:T(8,128)(2,1)S(1)}, u32[]{:S(2)}, u32[]{:S(2)}) collective-permute-start(bf16[56,2048]{1,0:T(8,128)(2,1)S(1)} %collective-permute-done.5), channel_id=1, source_target_pairs={{0,4},{4,12},{12,8},{8,0},{1,5},{5,13},{13,9},{9,1},{2,6},{6,14},{... | collective-permute-start | bytes 688136 | tf_op jit(solution)/shard_map/ppermute | solution.py:237
  51.1 7.0 %collective-permute-start.8 = (bf16[56,2048]{1,0:T(8,128)(2,1)S(1)}, bf16[56,2048]{1,0:T(8,128)(2,1)S(1)}, u32[]{:S(2)}, u32[]{:S(2)}) collective-permute-start(bf16[56,2048]{1,0:T(8,128)(2,1)S(1)} %collective-permute-done.5), channel_id=1, source_target_pairs={{0,2},{5,7},{10,8},{15,13},{16,18},{21,23},{26,24},{31,29}} | collective-permute-start | bytes 688136 | tf_op jit(solution)/shard_map/ppermute | solution.py:241
  58.1 8.2 %collective-permute-start.10 = (bf16[56,2048]{1,0:T(8,128)(2,1)S(1)}, bf16[56,2048]{1,0:T(8,128)(2,1)S(1)}, u32[]{:S(2)}, u32[]{:S(2)}) collective-permute-start(bf16[56,2048]{1,0:T(8,128)(2,1)S(1)} %collective-permute-done.7), channel_id=1, source_target_pairs={{0,2},{5,7},{10,8},{15,13},{16,18},{21,23},{26,24},{31,29}} | collective-permute-start | bytes 688136 | tf_op jit(solution)/shard_map/ppermute | solution.py:241
  63.2 6.0 %collective-permute-start.14 = (f32[56,64]{1,0:T(8,128)S(1)}, f32[56,64]{1,0:T(8,128)S(1)}, u32[]{:S(2)}, u32[]{:S(2)}) collective-permute-start(f32[56,64]{1,0:T(8,128)S(1)} %get-tuple-element.27), channel_id=1, source_target_pairs={{0,3},{1,2},{2,1},{3,0},{4,7},{5,6},{6,5},{7,4},{8,11},{9,10},{10,... | collective-permute-start | bytes 43016 | tf_op jit(solution)/shard_map/ppermute | solution.py:300
  63.3 5.9 %collective-permute-start.13 = (f32[56,64]{1,0:T(8,128)S(1)}, f32[56,64]{1,0:T(8,128)S(1)}, u32[]{:S(2)}, u32[]{:S(2)}) collective-permute-start(f32[56,64]{1,0:T(8,128)S(1)} %get-tuple-element.28), channel_id=1, source_target_pairs={{0,2},{1,3},{2,0},{3,1},{4,6},{5,7},{6,4},{7,5},{8,10},{9,11},{10,... | collective-permute-start | bytes 43016 | tf_op jit(solution)/shard_map/ppermute | solution.py:300
  63.4 5.9 %collective-permute-start.12 = (f32[56,64]{1,0:T(8,128)S(1)}, f32[56,64]{1,0:T(8,128)S(1)}, u32[]{:S(2)}, u32[]{:S(2)}) collective-permute-start(f32[56,64]{1,0:T(8,128)S(1)} %get-tuple-element.26), channel_id=1, source_target_pairs={{0,1},{1,0},{2,3},{3,2},{4,5},{5,4},{6,7},{7,6},{8,9},{9,8},{10,11... | collective-permute-start | bytes 43016 | tf_op jit(solution)/shard_map/ppermute | solution.py:300
  66.3 3.6 %collective-permute-start.11 = (bf16[56,2048]{1,0:T(8,128)(2,1)S(1)}, bf16[56,2048]{1,0:T(8,128)(2,1)S(1)}, u32[]{:S(2)}, u32[]{:S(2)}) collective-permute-start(bf16[56,2048]{1,0:T(8,128)(2,1)S(1)} %broadcast_select_fusion.1), channel_id=1, source_target_pairs={{0,1},{5,4},{10,11},{15,14},{2,3},{7,6},{8,9},{13,12},{16,17},{21,... | collective-permute-start | bytes 688136 | tf_op jit(solution)/shard_map/ppermute | solution.py:250
  67.9 3.1 %collective-permute-start.9 = (bf16[168,2048]{1,0:T(8,128)(2,1)S(1)}, bf16[168,2048]{1,0:T(8,128)(2,1)S(1)}, u32[]{:S(2)}, u32[]{:S(2)}) collective-permute-start(bf16[168,2048]{1,0:T(8,128)(2,1)S(1)} %maximum_select_fusion), channel_id=1, source_target_pairs={{0,1},{5,4},{10,11},{15,14},{2,3},{7,6},{8,9},{13,12},{16,17},{21,... | collective-permute-start | bytes 2064392 | tf_op jit(solution)/shard_map/ppermute | solution.py:250

commit v3 on v2

v3 whole, which is shorter than its diff:
```python
import jax
import jax.numpy as jnp
from jax import lax
from jax.experimental import pallas as pl
from jax.experimental.pallas import tpu as pltpu
from jax.sharding import PartitionSpec as P

F32, BF16, I32 = jnp.float32, jnp.bfloat16, jnp.int32
WIDE = ("feat", "sub")
MIB = 1 << 20
VMEM = pl.BlockSpec(memory_space=pltpu.VMEM)
SMEM = pl.BlockSpec(memory_space=pltpu.SMEM)


def params(mib):
    return pltpu.CompilerParams(vmem_limit_bytes=mib * MIB)


def project_kernel(x_ref, weight_ref, full_ref):
    tile = 256
    for i in range(x_ref.shape[0] // tile):
        at = slice(i * tile, (i + 1) * tile)
        product = jnp.dot(x_ref[at, :], weight_ref[...], preferred_element_type=F32)
        full_ref[:, at] = jnp.transpose(product)


def project_flipped_kernel(x_ref, weight_ref, full_ref, flip_ref):
    flip_ref[...] = jnp.transpose(weight_ref[...])
    project_kernel(x_ref, flip_ref, full_ref)


def project(x, weight, flipped):
    rows, width = x.shape
    rank = weight.shape[0] if flipped else weight.shape[1]
    return pl.pallas_call(
        project_flipped_kernel if flipped else project_kernel,
        in_specs=[VMEM, VMEM],
        out_specs=VMEM,
        out_shape=jax.ShapeDtypeStruct((rank, rows), F32),
        scratch_shapes=[pltpu.VMEM((width, rank), BF16)] if flipped else [],
        compiler_params=params(16),
        cost_estimate=pl.CostEstimate(
            flops=(40 if flipped else 2) * rows * width * rank, bytes_accessed=2 * x.size, transcendentals=0
        ),
        name="project",
    )(x, weight)


def split(x):
    high = x.astype(BF16)
    return high, (x - high.astype(F32)).astype(BF16)


def feature_kernel(start_ref, end_ref, u_ref, v_ref, scale_ref, feat_ref, uu, vh, vl, acc, wide):
    rank_in = u_ref.shape[0]
    share = v_ref.shape[0]
    tokens = u_ref.shape[1]
    seqs = scale_ref.shape[0]
    tile = 256
    high, low = split(u_ref[...])
    uu[:tokens, :] = jnp.transpose(jnp.concatenate([high, low], axis=0))
    uu[tokens:, :] = jnp.zeros((uu.shape[0] - tokens, uu.shape[1]), BF16)
    high, low = split(v_ref[...])
    vh[:, :tokens] = high
    vl[:, :tokens] = low
    for ref in (vh, vl):
        ref[:, tokens:] = jnp.zeros((ref.shape[0], ref.shape[1] - tokens), BF16)
    lane = lax.broadcasted_iota(I32, (8, tile), 1)
    left = lax.broadcasted_iota(I32, (8, 2 * rank_in), 1) < rank_in
    for group in range(seqs // 8):
        sets = (8 * group, 8 * group + 4)
        bases = [(start_ref[s] // 128) * 128 for s in sets]
        needs = [(end_ref[s + 3] - base + tile - 1) // tile for s, base in zip(sets, bases)]
        acc[...] = jnp.zeros_like(acc)

        def step(k, carry):
            for i in range(2):
                at = pl.multiple_of(bases[i] + k * tile, 128)
                tops, lows = [], []
                v_high = vh[:, pl.ds(at, tile)]
                v_low = vl[:, pl.ds(at, tile)]
                for s in range(sets[i], sets[i] + 4):
                    begin = start_ref[s] - at
                    stop = end_ref[s] - at
                    inside = jnp.where((lane >= begin) & (lane < stop), 1.0, 0.0).astype(F32)
                    inside = jnp.concatenate([inside] * (share // 8), axis=0).astype(BF16)
                    tops.append(v_high * inside)
                    lows.append(v_low * inside)
                total = jnp.dot(
                    jnp.concatenate(tops + lows, 0),
                    uu[pl.ds(at, tile), :],
                    preferred_element_type=F32,
                )
                rows = slice(4 * share * i, 4 * share * (i + 1))
                acc[rows, :] += total[: 4 * share] + total[4 * share :]
            return carry

        lax.fori_loop(0, jnp.maximum(needs[0], needs[1]), step, 0)
        factor = scale_ref[8 * group : 8 * group + 8, :]
        for pair in range(share // 2):
            even = acc[pl.ds(2 * pair, 8, stride=share), :]
            odd = acc[pl.ds(2 * pair + 1, 8, stride=share), :]
            even = even + pltpu.roll(even, rank_in, 1)
            odd = odd + pltpu.roll(odd, rank_in, 1)
            both = jnp.where(left, even, odd) * factor
            wide[8 * group : 8 * group + 8, 2 * rank_in * pair : 2 * rank_in * (pair + 1)] = both
    feat_ref[...] = wide[...].astype(BF16)


def features_of(starts, ends, u, v, scale):
    rank_in, tokens = u.shape
    share = v.shape[0]
    seqs = starts.shape[0]
    return pl.pallas_call(
        feature_kernel,
        in_specs=[SMEM, SMEM, VMEM, VMEM, VMEM],
        out_specs=VMEM,
        out_shape=jax.ShapeDtypeStruct((seqs, share * rank_in), BF16),
        scratch_shapes=[
            pltpu.VMEM((tokens + 768, 2 * rank_in), BF16),
            pltpu.VMEM((share, tokens + 768), BF16),
            pltpu.VMEM((share, tokens + 768), BF16),
            pltpu.VMEM((8 * share, 2 * rank_in), F32),
            pltpu.VMEM((seqs, share * rank_in), F32),
        ],
        compiler_params=params(16),
        name="features",
    )(starts, ends, u, v, scale)


def score_kernel(ids_ref, all_ref, square_ref, part_ref):
    every = all_ref[...]
    seqs = every.shape[0]
    picks = ids_ref.shape[0]
    weights = 1.0 / (square_ref[...] / seqs + 1e-05)
    column = lax.broadcasted_iota(I32, (picks, seqs), 1)
    chosen_of = jnp.where(column == ids_ref[...], 1.0, 0.0).astype(BF16)
    chosen = jnp.dot(chosen_of, every, preferred_element_type=F32)
    weighted = (chosen * weights).astype(BF16)
    part_ref[...] = lax.dot_general(
        every, weighted, (((1,), (1,)), ((), ())), preferred_element_type=F32
    )


def partial_scores_of(ids, gathered, squares):
    return pl.pallas_call(
        score_kernel,
        in_specs=[VMEM, VMEM, VMEM],
        out_specs=VMEM,
        out_shape=jax.ShapeDtypeStruct((gathered.shape[0], ids.shape[0]), F32),
        compiler_params=params(24),
        cost_estimate=pl.CostEstimate(flops=8 * gathered.size * ids.shape[0], bytes_accessed=2 * gathered.size, transcendentals=0),
        name="partial_scores",
    )(ids[:, None], gathered, squares)


def covariance_kernel(row_ref, col_ref, tile_hbm, tile_ref, sem):
    seqs = row_ref.shape[0]
    steps = sem.shape[0]
    tile = tile_ref.shape[0] // steps
    copies = []
    for i in range(steps):
        at = slice(i * tile, (i + 1) * tile)
        product = lax.dot_general(
            row_ref[:, at], col_ref[...], (((0,), (0,)), ((), ())), preferred_element_type=F32
        )
        tile_ref[at, :] = product * (1.0 / seqs)
        rows = pl.ds(i * tile, tile)
        copies.append(pltpu.make_async_copy(tile_ref.at[rows], tile_hbm.at[rows], sem.at[i]))
        copies[-1].start()
    for copy in copies:
        copy.wait()


def covariance_of(gathered, other_cols):
    seqs, rows = gathered.shape
    cols = other_cols.shape[1]
    steps = rows // 256
    return pl.pallas_call(
        covariance_kernel,
        in_specs=[VMEM, VMEM],
        out_specs=pl.BlockSpec(memory_space=pltpu.HBM),
        out_shape=jax.ShapeDtypeStruct((rows, cols), F32),
        scratch_shapes=[pltpu.VMEM((rows, cols), F32), pltpu.SemaphoreType.DMA((steps,))],
        compiler_params=params(32),
        cost_estimate=pl.CostEstimate(flops=2 * seqs * rows * cols, bytes_accessed=4 * rows * cols, transcendentals=0),
        name="covariance",
    )(gathered, other_cols)


def both_ways(x, axis):
    return lax.ppermute(x, axis, [(0, 1), (1, 0)])


def picked(index, low, high):
    return jnp.where(index == 0, low, high)


STEPS = 32000.0


def exchanged(keep, give):
    top = jnp.max(jnp.abs(give), axis=1, keepdims=True)
    power = jnp.ceil(jnp.log2(jnp.maximum(top, 1e-30)))
    coded = jnp.round(give * (jnp.exp2(-power) * STEPS))
    sent = jnp.concatenate([coded, jnp.broadcast_to(power, (give.shape[0], 128))], axis=1)
    got = both_ways(sent.astype(jnp.int16), "feat").astype(F32)
    return keep + got[:, :-128] * (jnp.exp2(got[:, -128:-127]) * (1.0 / STEPS))


def u_of_chip(u):
    half = u.shape[0] // 2
    sub = lax.axis_index("sub")
    return picked(sub, u[:half], u[half:]) + both_ways(picked(sub, u[half:], u[:half]), "sub")


def reduced(u_chip, v, share):
    feat, sub = lax.axis_index("feat"), lax.axis_index("sub")
    u_mine = exchanged(u_chip, u_chip)
    u_other = both_ways(u_mine, "sub")
    u = jnp.concatenate([picked(sub, u_mine, u_other), picked(sub, u_other, u_mine)])
    v = v.reshape(2, 2, share, -1)
    v_chip = picked(sub, v[:, 0], v[:, 1]) + both_ways(picked(sub, v[:, 1], v[:, 0]), "sub")
    v_mine = exchanged(picked(feat, v_chip[0], v_chip[1]), picked(feat, v_chip[1], v_chip[0]))
    return u, v_mine


def is_square():
    return lax.axis_size("feat") == 2 and lax.axis_size("sub") == 2 and lax.axis_size("dp") == 4


RING = (0, 1, 3, 2)


def ring_place(d):
    return d ^ (d >> 1)


def around(part):
    return lax.ppermute(part, "dp", [(RING[i], RING[(i + 1) % 4]) for i in range(4)])


def on_owner_chip():
    return (lax.axis_index(WIDE) ^ lax.axis_index("dp")) < 2


def owned(part, other):
    return jnp.where(lax.axis_index(WIDE) == lax.axis_index("dp"), part, other)


def sent_across(part, axis):
    size = part.shape[axis] // 2
    low = lax.slice_in_dim(part, 0, size, axis=axis)
    high = lax.slice_in_dim(part, size, 2 * size, axis=axis)
    half = picked(lax.axis_index("sub"), low, high)
    return both_ways(half, "feat")


def spread(part, mine, other, axis):
    sub = lax.axis_index("sub")
    both = jnp.concatenate([picked(sub, mine, other), picked(sub, other, mine)], axis=axis)
    return jnp.where(on_owner_chip(), part, both)


def summed_squares(part):
    return jnp.sum(jnp.square(part.astype(F32)), axis=0, keepdims=True)


def column_block(gathered, col_width):
    block_width = gathered.shape[1]
    col_start = lax.axis_index("dp") * col_width
    owner = col_start // block_width
    own_slice = lax.dynamic_slice_in_dim(gathered, col_start % block_width, col_width, 1)
    every_slice = lax.all_gather(own_slice, WIDE, axis=1, tiled=True)
    return lax.dynamic_slice_in_dim(every_slice, owner * col_width, col_width, 1)


def shards(layer_inputs, output_grads, proj_in, proj_out, lengths, target_ids):
    group = lax.axis_size(WIDE)
    rank_in = proj_in.shape[1]
    share = proj_out.shape[1] // group
    u = project(layer_inputs, jnp.transpose(proj_in), True)
    if is_square():
        u_chip, proj_out = lax.optimization_barrier((u_of_chip(u), proj_out))
        v = project(output_grads, proj_out, False)
        u, v_mine = reduced(u_chip, v, share)
    else:
        v = project(output_grads, proj_out, False)
        u = lax.psum(u, WIDE)
        v_mine = lax.psum_scatter(v, WIDE, scatter_dimension=0, tiled=True)
    seq_len = lengths[0]
    ends = jnp.cumsum(seq_len)
    starts = ends - seq_len
    scale = jnp.broadcast_to(1.0 / jnp.sqrt(seq_len.astype(F32))[:, None], (seq_len.shape[0], 2 * rank_in))
    local_feat = features_of(starts, ends, u, v_mine, scale)
    me = lax.axis_index(WIDE)
    at = lax.axis_index("dp")
    if is_square():
        chunks = [local_feat]
        chunks.append(around(chunks[0]))
        chunks.append(around(chunks[1]))
        pair = jnp.concatenate(chunks[:2])
        pair = owned(pair, both_ways(pair, "sub"))
        pair_over = sent_across(pair, 0)
        chunks[2], pair_over = lax.optimization_barrier((chunks[2], pair_over))
        chunks.append(around(chunks[2]))
        third = owned(chunks[2], both_ways(chunks[2], "sub"))
        third_over = sent_across(third, 1)
        pair_other = both_ways(pair_over, "sub")
        chunks[3], third_over, pair_other = lax.optimization_barrier((chunks[3], third_over, pair_other))
        last = owned(chunks[3], both_ways(chunks[3], "sub"))
        third_other = both_ways(third_over, "sub")
        gathered = jnp.concatenate(chunks)
        squares = summed_squares(gathered)
        seqs = local_feat.shape[0]
        ids = ((ring_place(at) - ring_place(target_ids // seqs)) & 3) * seqs + target_ids % seqs
    else:
        gathered = lax.all_gather(local_feat, "dp", axis=0, tiled=True)
        other_cols = column_block(gathered, gathered.shape[1] * group // lax.axis_size("dp"))
        ids = target_ids
        squares = summed_squares(gathered)
    if is_square():
        last, ids = lax.optimization_barrier((last, ids))
        last_over = sent_across(last, 1)
    part = partial_scores_of(ids, gathered, squares)
    own = part.shape[0] // group
    if is_square():
        places = [(ring_place(at) - ring_place(me ^ k)) & 3 for k in range(4)]
        pieces = part.reshape(group, own, -1)
        pieces = [lax.dynamic_index_in_dim(pieces, place, 0, keepdims=False) for place in places]
        summed = jnp.stack([pieces[0], pieces[2]]) + both_ways(jnp.stack([pieces[1], pieces[3]]), "sub")
        last_other = both_ways(last_over, "sub")
        other_cols = jnp.concatenate(
            [
                spread(pair, pair_over, pair_other, 0),
                spread(third, third_over, third_other, 1),
                spread(last, last_over, last_other, 1),
            ]
        )
        given = both_ways(summed[1], "feat")
        tile = covariance_of(gathered, other_cols)
        mine, given, tile = lax.optimization_barrier((summed[0], given, tile))
        total = mine + given
    else:
        total = lax.psum_scatter(part, WIDE, scatter_dimension=0, tiled=True)
        tile = covariance_of(gathered, other_cols)
    scores = jnp.transpose(total) / jnp.sqrt(jnp.float32(gathered.shape[1] * group))
    return (tile, scores)


def solution(mesh):
    placed = (
        P(("groups", "dp"), ("feat", "sub")),
        P(("groups", "dp"), ("feat", "sub")),
        P(("feat", "sub"), None),
        P(("feat", "sub"), None),
        P(("groups", "dp"), None),
        P(("groups", "dp")),
    )
    return jax.shard_map(
        shards,
        mesh=mesh,
        in_specs=placed,
        out_specs=(P(("groups", "feat", "sub"), "dp"), P(("groups", "dp"), ("feat", "sub"))),
        check_vma=False,
    )
```

time: 79.4 us -> 70.3 us (0.89)
  Pallas kernels: 21.4 us -> 13 us
  starting transfers between devices: 26.7 us -> 19.4 us
  local copies, waits for them, and re-layouts: 1.85 us -> 5.42 us
  waiting for transfers between devices: 26.3 us -> 28.3 us
  other arithmetic: 1.81 us -> 2.99 us
    ppermute x9 -> x0, starting transfers between devices: 19.4 us -> none  [the longest x4 14.8 us: sent_across(): lax.ppermute(part, ('dp',) + WIDE, [(4 * d + d, 4 * d + (d ^ 2)) for d in...]
    ppermute x3 -> x16, starting transfers between devices: 3.51 us -> 13.2 us  [both_ways(): return lax.ppermute(x, axis, [(0, 1), (1, 0)])]
    pallas_call x3 -> x4, Pallas kernels: 16.7 us -> 9.45 us  [the longest x1 6.39 us: covariance_of(): pl.pallas_call(covariance_kernel, in_specs=[VMEM, VMEM], out_specs=pl.Blo...]
    ppermute x3, waiting for transfers between devices: 9.26 us -> 15.8 us  [around(): lax.ppermute(part, 'dp', [(RING[i], RING[(i + 1) % 4]) for i in range(4)])]
    unnamed x6 -> x12, local copies, waits for them, and re-layouts: 1.33 us -> 4.99 us
    ppermute x9 -> x0, waiting for transfers between devices: 3.31 us -> none  [the longest x4 2.28 us: sent_across(): lax.ppermute(part, ('dp',) + WIDE, [(4 * d + d, 4 * d + (d ^ 2)) for d in...]
    ppermute x3, starting transfers between devices: 3.87 us -> 6.16 us  [around(): lax.ppermute(part, 'dp', [(RING[i], RING[(i + 1) % 4]) for i in range(4)])]
    ppermute x3 -> x16, waiting for transfers between devices: 13.7 us -> 12.6 us  [both_ways(): return lax.ppermute(x, axis, [(0, 1), (1, 0)])]
  transfers between devices with their start and end apart: 15 -> 19, of which waited for: 9 -> 12; matrix products, arithmetic and copies ran while one was open for 2% -> 2% of each run, Pallas kernels for 1% -> 11%
where the time goes in v3:
time: 70.3 us; the launch traced here: 70 us
  waiting for transfers between devices  28.3 us (40%)
  starting transfers between devices  19.4 us (28%)
  Pallas kernels  13 us (18%)
  local copies, waits for them, and re-layouts  5.42 us (8%)
  other arithmetic  2.99 us (4%)
  between operations  0.93 us (1%)
    ppermute x3, waiting for transfers between devices, around(): lax.ppermute(part, 'dp', [(RING[i], RING[(i + 1) % 4]) for i in range(4)])  15.8 us
    ppermute x16, starting transfers between devices, both_ways(): return lax.ppermute(x, axis, [(0, 1), (1, 0)])  13.2 us
    ppermute x16, waiting for transfers between devices, both_ways(): return lax.ppermute(x, axis, [(0, 1), (1, 0)])  12.6 us
    pallas_call x1, Pallas kernels, covariance_of(): pl.pallas_call(covariance_kernel, in_specs=[VMEM, VMEM], out_specs=pl.Blo...  6.39 us
    ppermute x3, starting transfers between devices, around(): lax.ppermute(part, 'dp', [(RING[i], RING[(i + 1) % 4]) for i in range(4)])  6.16 us
    unnamed x12, local copies, waits for them, and re-layouts  4.99 us
    pallas_call x1, Pallas kernels, features_of(): pl.pallas_call(feature_kernel, in_specs=[SMEM, SMEM, VMEM, VMEM, VMEM], o...  3.54 us
    pallas_call x2, Pallas kernels, project(): pl.pallas_call(project_flipped_kernel if flipped else project_kernel, in_...  2.41 us
  transfers between devices with their start and end apart: 19, of which 12 were waited for; matrix products, arithmetic and copies ran while one was open for 2% of the time, Pallas kernels for 11%

profile of v3, /device:TPU:0, one launch (start us, length us, event | category | flops | bytes accessed | tf_op | source)
XLA Modules:
  0.0 70.0 jit_solution(3497583163548972457)
XLA Ops:
  0.6 2.0 %copy-done.2 = bf16[1792,1024]{1,0:T(8,128)(2,1)S(1)} copy-done((bf16[1792,1024]{1,0:T(8,128)(2,1)S(1)}, bf16[1792,1024]{1,0:T(8,128)(2,1)}, u32[]{:S(2)}) %copy-start.2) | copy-done | bytes 3670040
  2.7 0.9 %copy-done.3 = bf16[1024,64]{0,1:T(8,128)(2,1)S(1)} copy-done((bf16[1024,64]{0,1:T(8,128)(2,1)S(1)}, bf16[1024,64]{0,1:T(8,128)(2,1)}, u32[]{:S(2)}) %copy-start.3) | copy-done | bytes 131096
  3.6 1.2 %project.2 = f32[64,1792]{1,0:T(8,128)S(1)} custom-call(bf16[1792,1024]{1,0:T(8,128)(2,1)S(1)} %copy-done.2, bf16[64,1024]{1,0:T(8,128)(2,1)S(1)} %bitcast.48), custom_call_target="tpu_custom_call" | custom-call | flops 4697620480 | bytes 3670016 | tf_op jit(solution)/shard_map/project/pallas_call | solution.py:35
  4.9 0.5 collective-permute-start
  5.6 0.1 reduce.end_ref
  5.7 0.8 %collective-permute-done = f32[32,1792]{1,0:T(8,128)S(1)} collective-permute-done((f32[32,1792]{1,0:T(8,128)S(1)}, f32[32,1792]{1,0:T(8,128)S(1)}, u32[]{:S(2)}, u32[]{:S(2)}) %collective-permute-start) | collective-permute-done | bytes 229408 | tf_op jit(solution)/shard_map/ppermute | solution.py:192
  6.5 0.1 abs_reduce_fusion
  6.7 0.1 round-nearest-even_convert_fusion
  6.9 2.9 %collective-permute-start.1 = (s16[32,1920]{1,0:T(8,128)(2,1)S(1)}, s16[32,1920]{1,0:T(8,128)(2,1)S(1)}, u32[]{:S(2)}, u32[]{:S(2)}) collective-permute-start(s16[32,1920]{1,0:T(8,128)(2,1)S(1)} %pad_add_fusion), channel_id=1, source_target_pairs={{0,2},{2,0},{1,3},{3,1},{4,6},{6,4},{5,7},{7,5},{8,10},{10,8},{9,1... | collective-permute-start | bytes 368648 | tf_op jit(solution)/shard_map/ppermute | solution.py:192
  9.8 2.0 %copy-done = bf16[1792,1024]{1,0:T(8,128)(2,1)S(1)} copy-done((bf16[1792,1024]{1,0:T(8,128)(2,1)S(1)}, bf16[1792,1024]{1,0:T(8,128)(2,1)}, u32[]{:S(2)}) %copy-start) | copy-done | bytes 3670040
  11.9 1.2 %project.3 = f32[128,1792]{1,0:T(8,128)S(1)} custom-call(bf16[1792,1024]{1,0:T(8,128)(2,1)S(1)} %copy-done, bf16[1024,128]{1,0:T(8,128)(2,1)S(1)} %copy-done.1), custom_call_target="tpu_custom_call" | custom-call | flops 469762048 | bytes 3670016 | tf_op jit(solution)/shard_map/project/pallas_call | solution.py:35
  13.0 0.4 collective-permute-done.1
  13.5 0.1 fusion.10
  13.6 0.1 fusion.1
  13.8 0.6 collective-permute-start.3
  14.4 0.9 %collective-permute-done.2 = f32[32,1792]{1,0:T(8,128)S(1)} collective-permute-done((f32[32,1792]{1,0:T(8,128)S(1)}, f32[32,1792]{1,0:T(8,128)S(1)}, u32[]{:S(2)}, u32[]{:S(2)}) %collective-permute-start.2) | collective-permute-done | bytes 229408 | tf_op jit(solution)/shard_map/ppermute | solution.py:192
  15.3 0.6 collective-permute-done.3
  16.0 0.1 fusion.2
  16.1 0.1 fusion.4
  16.3 1.8 %collective-permute-start.4 = (s16[32,1920]{1,0:T(8,128)(2,1)S(1)}, s16[32,1920]{1,0:T(8,128)(2,1)S(1)}, u32[]{:S(2)}, u32[]{:S(2)}) collective-permute-start(s16[32,1920]{1,0:T(8,128)(2,1)S(1)} %pad_add_fusion.1), channel_id=1, source_target_pairs={{0,2},{2,0},{1,3},{3,1},{4,6},{6,4},{5,7},{7,5},{8,10},{10,8},{9,1... | collective-permute-start | bytes 368648 | tf_op jit(solution)/shard_map/ppermute | solution.py:192
  18.2 3.8 %collective-permute-done.4 = s16[32,1920]{1,0:T(8,128)(2,1)S(1)} collective-permute-done((s16[32,1920]{1,0:T(8,128)(2,1)S(1)}, s16[32,1920]{1,0:T(8,128)(2,1)S(1)}, u32[]{:S(2)}, u32[]{:S(2)}) %collective-permute-start.4) | collective-permute-done | bytes 122912 | tf_op jit(solution)/shard_map/ppermute | solution.py:192
  22.0 0.1 fusion.7
  22.1 0.1 fusion.v_ref
  22.3 3.5 %features.1 = bf16[56,2048]{1,0:T(8,128)(2,1)S(1)} custom-call(s32[56]{0:T(128)S(1)} %bitcast_subtract_fusion.start_ref, s32[56]{0:T(128)S(1)} %reduce.end_ref, f32[64,1792]{1,0:T(8,128)S(1)} %pad_maximum_fusion.2.u_ref, f32[32,1792]{1,0:T(8,128)S(1)} %fusion.v_ref, f32[56,128]{1,0:T(8,128)S(1)} %broadcast_in_dim.12.scale_ref), custom_call_target="tpu_custom_call" | custom-call | tf_op jit(solution)/shard_map/features/pallas_call | solution.py:114
  25.8 2.3 %collective-permute-start.5 = (bf16[56,2048]{1,0:T(8,128)(2,1)S(1)}, bf16[56,2048]{1,0:T(8,128)(2,1)S(1)}, u32[]{:S(2)}, u32[]{:S(2)}) collective-permute-start(bf16[56,2048]{1,0:T(8,128)(2,1)S(1)} %features.1), channel_id=1, source_target_pairs={{0,4},{4,12},{12,8},{8,0},{1,5},{5,13},{13,9},{9,1},{2,6},{6,14},{... | collective-permute-start | bytes 688136 | tf_op jit(solution)/shard_map/ppermute | solution.py:240
  28.1 6.0 %collective-permute-done.5 = bf16[56,2048]{1,0:T(8,128)(2,1)S(1)} collective-permute-done((bf16[56,2048]{1,0:T(8,128)(2,1)S(1)}, bf16[56,2048]{1,0:T(8,128)(2,1)S(1)}, u32[]{:S(2)}, u32[]{:S(2)}) %collective-permute-start.5) | collective-permute-done | bytes 229408 | tf_op jit(solution)/shard_map/ppermute | solution.py:240
  34.3 1.1 %collective-permute-start.6 = (bf16[56,2048]{1,0:T(8,128)(2,1)S(1)}, bf16[56,2048]{1,0:T(8,128)(2,1)S(1)}, u32[]{:S(2)}, u32[]{:S(2)}) collective-permute-start(bf16[56,2048]{1,0:T(8,128)(2,1)S(1)} %collective-permute-done.5), channel_id=1, source_target_pairs={{0,4},{4,12},{12,8},{8,0},{1,5},{5,13},{13,9},{9,1},{2,6},{6,14},{... | collective-permute-start | bytes 688136 | tf_op jit(solution)/shard_map/ppermute | solution.py:240
  35.4 0.7 collective-permute-done.7
  36.1 0.1 broadcast_select_fusion
  36.3 1.6 %collective-permute-start.8 = (bf16[56,2048]{1,0:T(8,128)(2,1)S(1)}, bf16[56,2048]{1,0:T(8,128)(2,1)S(1)}, u32[]{:S(2)}, u32[]{:S(2)}) collective-permute-start(bf16[56,2048]{1,0:T(8,128)(2,1)S(1)} %slice_select_fusion), channel_id=1, source_target_pairs={{0,2},{2,0},{1,3},{3,1},{4,6},{6,4},{5,7},{7,5},{8,10},{10,8},{9,1... | collective-permute-start | bytes 688136 | tf_op jit(solution)/shard_map/ppermute | solution.py:192
  37.8 5.4 %collective-permute-done.6 = bf16[56,2048]{1,0:T(8,128)(2,1)S(1)} collective-permute-done((bf16[56,2048]{1,0:T(8,128)(2,1)S(1)}, bf16[56,2048]{1,0:T(8,128)(2,1)S(1)}, u32[]{:S(2)}, u32[]{:S(2)}) %collective-permute-start.6) | collective-permute-done | bytes 229408 | tf_op jit(solution)/shard_map/ppermute | solution.py:240
  43.2 0.7 %collective-permute-done.8 = bf16[56,2048]{1,0:T(8,128)(2,1)S(1)} collective-permute-done((bf16[56,2048]{1,0:T(8,128)(2,1)S(1)}, bf16[56,2048]{1,0:T(8,128)(2,1)S(1)}, u32[]{:S(2)}, u32[]{:S(2)}) %collective-permute-start.8) | collective-permute-done | bytes 229408 | tf_op jit(solution)/shard_map/ppermute | solution.py:192
  44.0 2.7 %collective-permute-start.9 = (bf16[56,2048]{1,0:T(8,128)(2,1)S(1)}, bf16[56,2048]{1,0:T(8,128)(2,1)S(1)}, u32[]{:S(2)}, u32[]{:S(2)}) collective-permute-start(bf16[56,2048]{1,0:T(8,128)(2,1)S(1)} %collective-permute-done.6), channel_id=1, source_target_pairs={{0,4},{4,12},{12,8},{8,0},{1,5},{5,13},{13,9},{9,1},{2,6},{6,14},{... | collective-permute-start | bytes 688136 | tf_op jit(solution)/shard_map/ppermute | solution.py:240
  46.7 0.2 collective-permute-start.12
  47.0 1.6 %collective-permute-start.11 = (bf16[56,1024]{1,0:T(8,128)(2,1)S(1)}, bf16[56,1024]{1,0:T(8,128)(2,1)S(1)}, u32[]{:S(2)}, u32[]{:S(2)}) collective-permute-start(bf16[56,1024]{1,0:T(8,128)(2,1)S(1)} %slice_select_fusion.3), channel_id=1, source_target_pairs={{0,2},{2,0},{1,3},{3,1},{4,6},{6,4},{5,7},{7,5},{8,10},{10,8},{9,1... | collective-permute-start | bytes 344072 | tf_op jit(solution)/shard_map/ppermute | solution.py:192
  48.6 4.3 %collective-permute-done.9 = bf16[56,2048]{1,0:T(8,128)(2,1)S(1)} collective-permute-done((bf16[56,2048]{1,0:T(8,128)(2,1)S(1)}, bf16[56,2048]{1,0:T(8,128)(2,1)S(1)}, u32[]{:S(2)}, u32[]{:S(2)}) %collective-permute-start.9) | collective-permute-done | bytes 229408 | tf_op jit(solution)/shard_map/ppermute | solution.py:240
  53.0 0.5 collective-permute-start.16
  53.5 0.1 maximum_select_fusion
  53.6 0.2 multiply_reduce_fusion
  53.8 0.8 %collective-permute-done.16 = bf16[56,1024]{1,0:T(8,128)(2,1)S(1)} collective-permute-done((bf16[56,1024]{1,0:T(8,128)(2,1)S(1)}, bf16[56,1024]{1,0:T(8,128)(2,1)S(1)}, u32[]{:S(2)}, u32[]{:S(2)}) %collective-permute-start.16) | collective-permute-done | bytes 114720 | tf_op jit(solution)/shard_map/ppermute | solution.py:192
  54.8 0.7 partial_scores.1
  55.5 0.2 collective-permute-start.14
  55.8 1.6 %collective-permute-start.17 = (bf16[56,1024]{1,0:T(8,128)(2,1)S(1)}, bf16[56,1024]{1,0:T(8,128)(2,1)S(1)}, u32[]{:S(2)}, u32[]{:S(2)}) collective-permute-start(bf16[56,1024]{1,0:T(8,128)(2,1)S(1)} %slice_select_fusion.4), channel_id=1, source_target_pairs={{0,2},{2,0},{1,3},{3,1},{4,6},{6,4},{5,7},{7,5},{8,10},{10,8},{9,1... | collective-permute-start | bytes 344072 | tf_op jit(solution)/shard_map/ppermute | solution.py:192
  57.4 3.9 %collective-permute-done.17 = bf16[56,1024]{1,0:T(8,128)(2,1)S(1)} collective-permute-done((bf16[56,1024]{1,0:T(8,128)(2,1)S(1)}, bf16[56,1024]{1,0:T(8,128)(2,1)S(1)}, u32[]{:S(2)}, u32[]{:S(2)}) %collective-permute-start.17) | collective-permute-done | bytes 114720 | tf_op jit(solution)/shard_map/ppermute | solution.py:192
  61.2 1.6 %collective-permute-start.15 = (f32[56,64]{1,0:T(8,128)S(1)}, f32[56,64]{1,0:T(8,128)S(1)}, u32[]{:S(2)}, u32[]{:S(2)}) collective-permute-start(f32[56,64]{1,0:T(8,128)S(1)} %get-tuple-element.40), channel_id=1, source_target_pairs={{0,2},{2,0},{1,3},{3,1},{4,6},{6,4},{5,7},{7,5},{8,10},{10,8},{9,1... | collective-permute-start | bytes 43016 | tf_op jit(solution)/shard_map/ppermute | solution.py:192
  62.8 0.1 maximum_select_fusion.1
  63.0 6.4 %covariance.1 = f32[2048,2048]{1,0:T(8,128)} custom-call(bf16[224,2048]{1,0:T(8,128)(2,1)S(1)} %get-tuple-element.27.all_ref.row_ref, bf16[224,2048]{1,0:T(8,128)(2,1)S(1)} %pad_maximum_fusion.1.col_ref), custom_call_target="tpu_custom_call" | custom-call | flops 1879048192 | bytes 16777216 | tf_op jit(solution)/shard_map/covariance/pallas_call | solution.py:179
  69.4 0.6 multiply_bitcast_fusion
  (56 shorter events, 1.5 us)
Async XLA Ops:
  0.6 2.0 %copy-start.2 = (bf16[1792,1024]{1,0:T(8,128)(2,1)S(1)}, bf16[1792,1024]{1,0:T(8,128)(2,1)}, u32[]{:S(2)}) copy-start(bf16[1792,1024]{1,0:T(8,128)(2,1)} %x_ref.2) | copy-start | bytes 11010052
  2.7 0.9 %copy-start.3 = (bf16[1024,64]{0,1:T(8,128)(2,1)S(1)}, bf16[1024,64]{0,1:T(8,128)(2,1)}, u32[]{:S(2)}) copy-start(bf16[1024,64]{0,1:T(8,128)(2,1)} %param.8) | copy-start | bytes 393220
  3.6 1.8 %copy-start.4 = (s32[1,56]{1,0:T(1,128)S(1)}, s32[1,56]{1,0:T(1,128)}, u32[]{:S(2)}) copy-start(s32[1,56]{1,0:T(1,128)} %param.10) | copy-start | bytes 676
  4.8 5.0 %copy-start.1 = (bf16[1024,128]{1,0:T(8,128)(2,1)S(1)}, bf16[1024,128]{1,0:T(8,128)(2,1)}, u32[]{:S(2)}) copy-start(bf16[1024,128]{1,0:T(8,128)(2,1)} %weight_ref) | copy-start | bytes 786436
  4.9 1.6 %collective-permute-start = (f32[32,1792]{1,0:T(8,128)S(1)}, f32[32,1792]{1,0:T(8,128)S(1)}, u32[]{:S(2)}, u32[]{:S(2)}) collective-permute-start(f32[32,1792]{1,0:T(8,128)S(1)} %slice_select_fusion.2), channel_id=1, source_target_pairs={{0,1},{1,0},{2,3},{3,2},{4,5},{5,4},{6,7},{7,6},{8,9},{9,8},{10,11... | collective-permute-start | bytes 688136 | tf_op jit(solution)/shard_map/ppermute | solution.py:192
  6.9 6.5 %collective-permute-start.1 = (s16[32,1920]{1,0:T(8,128)(2,1)S(1)}, s16[32,1920]{1,0:T(8,128)(2,1)S(1)}, u32[]{:S(2)}, u32[]{:S(2)}) collective-permute-start(s16[32,1920]{1,0:T(8,128)(2,1)S(1)} %pad_add_fusion), channel_id=1, source_target_pairs={{0,2},{2,0},{1,3},{3,1},{4,6},{6,4},{5,7},{7,5},{8,10},{10,8},{9,1... | collective-permute-start | bytes 368648 | tf_op jit(solution)/shard_map/ppermute | solution.py:192
  9.8 2.0 %copy-start = (bf16[1792,1024]{1,0:T(8,128)(2,1)S(1)}, bf16[1792,1024]{1,0:T(8,128)(2,1)}, u32[]{:S(2)}) copy-start(bf16[1792,1024]{1,0:T(8,128)(2,1)} %x_ref.3) | copy-start | bytes 11010052
  13.7 1.6 %collective-permute-start.2 = (f32[32,1792]{1,0:T(8,128)S(1)}, f32[32,1792]{1,0:T(8,128)S(1)}, u32[]{:S(2)}, u32[]{:S(2)}) collective-permute-start(f32[32,1792]{1,0:T(8,128)S(1)} %fusion.1), channel_id=1, source_target_pairs={{0,1},{1,0},{2,3},{3,2},{4,5},{5,4},{6,7},{7,6},{8,9},{9,8},{10,11... | collective-permute-start | bytes 688136 | tf_op jit(solution)/shard_map/ppermute | solution.py:192
  13.8 2.1 %collective-permute-start.3 = (f32[2,32,1792]{2,1,0:T(8,128)S(1)}, f32[2,32,1792]{2,1,0:T(8,128)S(1)}, u32[]{:S(2)}, u32[]{:S(2)}) collective-permute-start(f32[2,32,1792]{2,1,0:T(8,128)S(1)} %select_bitcast_fusion), channel_id=1, source_target_pairs={{0,1},{1,0},{2,3},{3,2},{4,5},{5,4},{6,7},{7,6},{8,9},{9,8},{10,11... | collective-permute-start | bytes 1376264 | tf_op jit(solution)/shard_map/ppermute | solution.py:192
  16.3 5.6 %collective-permute-start.4 = (s16[32,1920]{1,0:T(8,128)(2,1)S(1)}, s16[32,1920]{1,0:T(8,128)(2,1)S(1)}, u32[]{:S(2)}, u32[]{:S(2)}) collective-permute-start(s16[32,1920]{1,0:T(8,128)(2,1)S(1)} %pad_add_fusion.1), channel_id=1, source_target_pairs={{0,2},{2,0},{1,3},{3,1},{4,6},{6,4},{5,7},{7,5},{8,10},{10,8},{9,1... | collective-permute-start | bytes 368648 | tf_op jit(solution)/shard_map/ppermute | solution.py:192
  25.8 22.7 %copy-start.5 = (s32[64]{0:T(128)S(1)}, s32[64]{0:T(128)}, u32[]{:S(2)}) copy-start(s32[64]{0:T(128)} %param.11) | copy-start | bytes 772
  25.8 8.4 %collective-permute-start.5 = (bf16[56,2048]{1,0:T(8,128)(2,1)S(1)}, bf16[56,2048]{1,0:T(8,128)(2,1)S(1)}, u32[]{:S(2)}, u32[]{:S(2)}) collective-permute-start(bf16[56,2048]{1,0:T(8,128)(2,1)S(1)} %features.1), channel_id=1, source_target_pairs={{0,4},{4,12},{12,8},{8,0},{1,5},{5,13},{13,9},{9,1},{2,6},{6,14},{... | collective-permute-start | bytes 688136 | tf_op jit(solution)/shard_map/ppermute | solution.py:240
  34.2 1.9 %collective-permute-start.7 = (bf16[112,2048]{1,0:T(8,128)(2,1)S(1)}, bf16[112,2048]{1,0:T(8,128)(2,1)S(1)}, u32[]{:S(2)}, u32[]{:S(2)}) collective-permute-start(bf16[112,2048]{1,0:T(8,128)(2,1)S(1)} %pad_maximum_fusion.3), channel_id=1, source_target_pairs={{0,1},{1,0},{2,3},{3,2},{4,5},{5,4},{6,7},{7,6},{8,9},{9,8},{10,11... | collective-permute-start | bytes 1376264 | tf_op jit(solution)/shard_map/ppermute | solution.py:192
  34.3 8.9 %collective-permute-start.6 = (bf16[56,2048]{1,0:T(8,128)(2,1)S(1)}, bf16[56,2048]{1,0:T(8,128)(2,1)S(1)}, u32[]{:S(2)}, u32[]{:S(2)}) collective-permute-start(bf16[56,2048]{1,0:T(8,128)(2,1)S(1)} %collective-permute-done.5), channel_id=1, source_target_pairs={{0,4},{4,12},{12,8},{8,0},{1,5},{5,13},{13,9},{9,1},{2,6},{6,14},{... | collective-permute-start | bytes 688136 | tf_op jit(solution)/shard_map/ppermute | solution.py:240
  36.3 7.7 %collective-permute-start.8 = (bf16[56,2048]{1,0:T(8,128)(2,1)S(1)}, bf16[56,2048]{1,0:T(8,128)(2,1)S(1)}, u32[]{:S(2)}, u32[]{:S(2)}) collective-permute-start(bf16[56,2048]{1,0:T(8,128)(2,1)S(1)} %slice_select_fusion), channel_id=1, source_target_pairs={{0,2},{2,0},{1,3},{3,1},{4,6},{6,4},{5,7},{7,5},{8,10},{10,8},{9,1... | collective-permute-start | bytes 688136 | tf_op jit(solution)/shard_map/ppermute | solution.py:192
  44.0 3.0 %collective-permute-start.10 = (bf16[56,2048]{1,0:T(8,128)(2,1)S(1)}, bf16[56,2048]{1,0:T(8,128)(2,1)S(1)}, u32[]{:S(2)}, u32[]{:S(2)}) collective-permute-start(bf16[56,2048]{1,0:T(8,128)(2,1)S(1)} %collective-permute-done.6), channel_id=1, source_target_pairs={{0,1},{1,0},{2,3},{3,2},{4,5},{5,4},{6,7},{7,6},{8,9},{9,8},{10,11... | collective-permute-start | bytes 688136 | tf_op jit(solution)/shard_map/ppermute | solution.py:192
  44.0 8.9 %collective-permute-start.9 = (bf16[56,2048]{1,0:T(8,128)(2,1)S(1)}, bf16[56,2048]{1,0:T(8,128)(2,1)S(1)}, u32[]{:S(2)}, u32[]{:S(2)}) collective-permute-start(bf16[56,2048]{1,0:T(8,128)(2,1)S(1)} %collective-permute-done.6), channel_id=1, source_target_pairs={{0,4},{4,12},{12,8},{8,0},{1,5},{5,13},{13,9},{9,1},{2,6},{6,14},{... | collective-permute-start | bytes 688136 | tf_op jit(solution)/shard_map/ppermute | solution.py:240
  46.7 1.9 %collective-permute-start.12 = (bf16[56,2048]{1,0:T(8,128)(2,1)S(1)}, bf16[56,2048]{1,0:T(8,128)(2,1)S(1)}, u32[]{:S(2)}, u32[]{:S(2)}) collective-permute-start(bf16[56,2048]{1,0:T(8,128)(2,1)S(1)} %collective-permute-done.8), channel_id=1, source_target_pairs={{0,1},{1,0},{2,3},{3,2},{4,5},{5,4},{6,7},{7,6},{8,9},{9,8},{10,11... | collective-permute-start | bytes 688136 | tf_op jit(solution)/shard_map/ppermute | solution.py:192
  47.0 5.9 %collective-permute-start.11 = (bf16[56,1024]{1,0:T(8,128)(2,1)S(1)}, bf16[56,1024]{1,0:T(8,128)(2,1)S(1)}, u32[]{:S(2)}, u32[]{:S(2)}) collective-permute-start(bf16[56,1024]{1,0:T(8,128)(2,1)S(1)} %slice_select_fusion.3), channel_id=1, source_target_pairs={{0,2},{2,0},{1,3},{3,1},{4,6},{6,4},{5,7},{7,5},{8,10},{10,8},{9,1... | collective-permute-start | bytes 344072 | tf_op jit(solution)/shard_map/ppermute | solution.py:192
  52.9 1.7 %collective-permute-start.13 = (bf16[56,2048]{1,0:T(8,128)(2,1)S(1)}, bf16[56,2048]{1,0:T(8,128)(2,1)S(1)}, u32[]{:S(2)}, u32[]{:S(2)}) collective-permute-start(bf16[56,2048]{1,0:T(8,128)(2,1)S(1)} %collective-permute-done.9), channel_id=1, source_target_pairs={{0,1},{1,0},{2,3},{3,2},{4,5},{5,4},{6,7},{7,6},{8,9},{9,8},{10,11... | collective-permute-start | bytes 688136 | tf_op jit(solution)/shard_map/ppermute | solution.py:192
  53.0 1.6 %collective-permute-start.16 = (bf16[56,1024]{1,0:T(8,128)(2,1)S(1)}, bf16[56,1024]{1,0:T(8,128)(2,1)S(1)}, u32[]{:S(2)}, u32[]{:S(2)}) collective-permute-start(bf16[56,1024]{1,0:T(8,128)(2,1)S(1)} %collective-permute-done.11), channel_id=1, source_target_pairs={{0,1},{1,0},{2,3},{3,2},{4,5},{5,4},{6,7},{7,6},{8,9},{9,8},{10,11... | collective-permute-start | bytes 344072 | tf_op jit(solution)/shard_map/ppermute | solution.py:192
  55.5 1.8 %collective-permute-start.14 = (f32[2,56,64]{2,1,0:T(8,128)S(1)}, f32[2,56,64]{2,1,0:T(8,128)S(1)}, u32[]{:S(2)}, u32[]{:S(2)}) collective-permute-start(f32[2,56,64]{2,1,0:T(8,128)S(1)} %pad_maximum_fusion.4), channel_id=1, source_target_pairs={{0,1},{1,0},{2,3},{3,2},{4,5},{5,4},{6,7},{7,6},{8,9},{9,8},{10,11... | collective-permute-start | bytes 86024 | tf_op jit(solution)/shard_map/ppermute | solution.py:192
  55.8 5.4 %collective-permute-start.17 = (bf16[56,1024]{1,0:T(8,128)(2,1)S(1)}, bf16[56,1024]{1,0:T(8,128)(2,1)S(1)}, u32[]{:S(2)}, u32[]{:S(2)}) collective-permute-start(bf16[56,1024]{1,0:T(8,128)(2,1)S(1)} %slice_select_fusion.4), channel_id=1, source_target_pairs={{0,2},{2,0},{1,3},{3,1},{4,6},{6,4},{5,7},{7,5},{8,10},{10,8},{9,1... | collective-permute-start | bytes 344072 | tf_op jit(solution)/shard_map/ppermute | solution.py:192
  61.2 1.6 %collective-permute-start.18 = (bf16[56,1024]{1,0:T(8,128)(2,1)S(1)}, bf16[56,1024]{1,0:T(8,128)(2,1)S(1)}, u32[]{:S(2)}, u32[]{:S(2)}) collective-permute-start(bf16[56,1024]{1,0:T(8,128)(2,1)S(1)} %collective-permute-done.17), channel_id=1, source_target_pairs={{0,1},{1,0},{2,3},{3,2},{4,5},{5,4},{6,7},{7,6},{8,9},{9,8},{10,11... | collective-permute-start | bytes 344072 | tf_op jit(solution)/shard_map/ppermute | solution.py:192
  61.2 8.2 %collective-permute-start.15 = (f32[56,64]{1,0:T(8,128)S(1)}, f32[56,64]{1,0:T(8,128)S(1)}, u32[]{:S(2)}, u32[]{:S(2)}) collective-permute-start(f32[56,64]{1,0:T(8,128)S(1)} %get-tuple-element.40), channel_id=1, source_target_pairs={{0,2},{2,0},{1,3},{3,1},{4,6},{6,4},{5,7},{7,5},{8,10},{10,8},{9,1... | collective-permute-start | bytes 43016 | tf_op jit(solution)/shard_map/ppermute | solution.py:192

commit v4 on v3

--- a/solution.py
+++ b/solution.py
@@ -154,11 +154,13 @@
     )(ids[:, None], gathered, squares)
 
 
-def covariance_kernel(row_ref, col_ref, tile_hbm, tile_ref, sem):
+def covariance_kernel(row_ref, col_ref, one_ref, two_ref, tile_hbm, score_hbm, tile_ref, score_ref, sem):
     seqs = row_ref.shape[0]
-    steps = sem.shape[0]
+    steps = sem.shape[0] - 1
     tile = tile_ref.shape[0] // steps
-    copies = []
+    score_ref[...] = one_ref[...] + two_ref[...]
+    copies = [pltpu.make_async_copy(score_ref, score_hbm, sem.at[steps])]
+    copies[0].start()
     for i in range(steps):
         at = slice(i * tile, (i + 1) * tile)
         product = lax.dot_general(
@@ -172,20 +174,24 @@
         copy.wait()
 
 
-def covariance_of(gathered, other_cols):
+def covariance_of(gathered, other_cols, one, two):
     seqs, rows = gathered.shape
     cols = other_cols.shape[1]
     steps = rows // 256
     return pl.pallas_call(
         covariance_kernel,
-        in_specs=[VMEM, VMEM],
-        out_specs=pl.BlockSpec(memory_space=pltpu.HBM),
-        out_shape=jax.ShapeDtypeStruct((rows, cols), F32),
-        scratch_shapes=[pltpu.VMEM((rows, cols), F32), pltpu.SemaphoreType.DMA((steps,))],
+        in_specs=[VMEM] * 4,
+        out_specs=[pl.BlockSpec(memory_space=pltpu.HBM)] * 2,
+        out_shape=[jax.ShapeDtypeStruct((rows, cols), F32), jax.ShapeDtypeStruct(one.shape, F32)],
+        scratch_shapes=[
+            pltpu.VMEM((rows, cols), F32),
+            pltpu.VMEM(one.shape, F32),
+            pltpu.SemaphoreType.DMA((steps + 1,)),
+        ],
         compiler_params=params(32),
         cost_estimate=pl.CostEstimate(flops=2 * seqs * rows * cols, bytes_accessed=4 * rows * cols, transcendentals=0),
         name="covariance",
-    )(gathered, other_cols)
+    )(gathered, other_cols, one, two)
 
 
 def both_ways(x, axis):
@@ -199,13 +205,17 @@
 STEPS = 32000.0
 
 
-def exchanged(keep, give):
+def coded(give):
     top = jnp.max(jnp.abs(give), axis=1, keepdims=True)
     power = jnp.ceil(jnp.log2(jnp.maximum(top, 1e-30)))
-    coded = jnp.round(give * (jnp.exp2(-power) * STEPS))
-    sent = jnp.concatenate([coded, jnp.broadcast_to(power, (give.shape[0], 128))], axis=1)
-    got = both_ways(sent.astype(jnp.int16), "feat").astype(F32)
-    return keep + got[:, :-128] * (jnp.exp2(got[:, -128:-127]) * (1.0 / STEPS))
+    steps = jnp.round(give * (jnp.exp2(-power) * STEPS))
+    both = jnp.concatenate([steps, jnp.broadcast_to(power, (give.shape[0], 128))], axis=1)
+    return both.astype(jnp.int16)
+
+
+def decoded(got):
+    got = got.astype(F32)
+    return got[:, :-128] * (jnp.exp2(got[:, -128:-127]) * (1.0 / STEPS))
 
 
 def u_of_chip(u):
@@ -216,13 +226,16 @@
 
 def reduced(u_chip, v, share):
     feat, sub = lax.axis_index("feat"), lax.axis_index("sub")
-    u_mine = exchanged(u_chip, u_chip)
+    u_got = both_ways(coded(u_chip), "feat")
+    v = v.reshape(2, 2, share, -1)
+    v_chip = picked(sub, v[:, 0], v[:, 1]) + both_ways(picked(sub, v[:, 1], v[:, 0]), "sub")
+    v_given = coded(picked(feat, v_chip[1], v_chip[0]))
+    u_got = lax.optimization_barrier((u_got, v_given))[0]
+    v_got = both_ways(v_given, "feat")
+    u_mine = u_chip + decoded(u_got)
     u_other = both_ways(u_mine, "sub")
     u = jnp.concatenate([picked(sub, u_mine, u_other), picked(sub, u_other, u_mine)])
-    v = v.reshape(2, 2, share, -1)
-    v_chip = picked(sub, v[:, 0], v[:, 1]) + both_ways(picked(sub, v[:, 1], v[:, 0]), "sub")
-    v_mine = exchanged(picked(feat, v_chip[0], v_chip[1]), picked(feat, v_chip[1], v_chip[0]))
-    return u, v_mine
+    return u, picked(feat, v_chip[0], v_chip[1]) + decoded(v_got)
 
 
 def is_square():
@@ -248,17 +261,15 @@
     return jnp.where(lax.axis_index(WIDE) == lax.axis_index("dp"), part, other)
 
 
-def sent_across(part, axis):
-    size = part.shape[axis] // 2
-    low = lax.slice_in_dim(part, 0, size, axis=axis)
-    high = lax.slice_in_dim(part, size, 2 * size, axis=axis)
-    half = picked(lax.axis_index("sub"), low, high)
+def sent_across(part):
+    size = part.shape[1] // 2
+    half = picked(lax.axis_index("sub"), part[:, :size], part[:, size:])
     return both_ways(half, "feat")
 
 
-def spread(part, mine, other, axis):
+def spread(part, mine, other):
     sub = lax.axis_index("sub")
-    both = jnp.concatenate([picked(sub, mine, other), picked(sub, other, mine)], axis=axis)
+    both = jnp.concatenate([picked(sub, mine, other), picked(sub, other, mine)], axis=1)
     return jnp.where(on_owner_chip(), part, both)
 
 
@@ -281,7 +292,7 @@
     share = proj_out.shape[1] // group
     u = project(layer_inputs, jnp.transpose(proj_in), True)
     if is_square():
-        u_chip, proj_out = lax.optimization_barrier((u_of_chip(u), proj_out))
+        u_chip = u_of_chip(u)
         v = project(output_grads, proj_out, False)
         u, v_mine = reduced(u_chip, v, share)
     else:
@@ -296,20 +307,15 @@
     me = lax.axis_index(WIDE)
     at = lax.axis_index("dp")
     if is_square():
-        chunks = [local_feat]
-        chunks.append(around(chunks[0]))
-        chunks.append(around(chunks[1]))
-        pair = jnp.concatenate(chunks[:2])
-        pair = owned(pair, both_ways(pair, "sub"))
-        pair_over = sent_across(pair, 0)
-        chunks[2], pair_over = lax.optimization_barrier((chunks[2], pair_over))
-        chunks.append(around(chunks[2]))
-        third = owned(chunks[2], both_ways(chunks[2], "sub"))
-        third_over = sent_across(third, 1)
-        pair_other = both_ways(pair_over, "sub")
-        chunks[3], third_over, pair_other = lax.optimization_barrier((chunks[3], third_over, pair_other))
+        chunks, owns, overs = [local_feat], [], []
+        for k in range(3):
+            chunks.append(around(chunks[k]))
+            owns.append(owned(chunks[k], both_ways(chunks[k], "sub")))
+            overs.append(sent_across(owns[k]))
+            chunks[k + 1], overs[k] = lax.optimization_barrier((chunks[k + 1], overs[k]))
         last = owned(chunks[3], both_ways(chunks[3], "sub"))
-        third_other = both_ways(third_over, "sub")
+        early_over = jnp.concatenate(overs)
+        early_other = both_ways(early_over, "sub")
         gathered = jnp.concatenate(chunks)
         squares = summed_squares(gathered)
         seqs = local_feat.shape[0]
@@ -319,10 +325,10 @@
         other_cols = column_block(gathered, gathered.shape[1] * group // lax.axis_size("dp"))
         ids = target_ids
         squares = summed_squares(gathered)
+    part = partial_scores_of(ids, gathered, squares) / jnp.sqrt(jnp.float32(gathered.shape[1] * group))
     if is_square():
-        last, ids = lax.optimization_barrier((last, ids))
-        last_over = sent_across(last, 1)
-    part = partial_scores_of(ids, gathered, squares)
+        last, part = lax.optimization_barrier((last, part))
+        last_over = sent_across(last)
     own = part.shape[0] // group
     if is_square():
         places = [(ring_place(at) - ring_place(me ^ k)) & 3 for k in range(4)]
@@ -330,22 +336,13 @@
         pieces = [lax.dynamic_index_in_dim(pieces, place, 0, keepdims=False) for place in places]
         summed = jnp.stack([pieces[0], pieces[2]]) + both_ways(jnp.stack([pieces[1], pieces[3]]), "sub")
         last_other = both_ways(last_over, "sub")
-        other_cols = jnp.concatenate(
-            [
-                spread(pair, pair_over, pair_other, 0),
-                spread(third, third_over, third_other, 1),
-                spread(last, last_over, last_other, 1),
-            ]
-        )
-        given = both_ways(summed[1], "feat")
-        tile = covariance_of(gathered, other_cols)
-        mine, given, tile = lax.optimization_barrier((summed[0], given, tile))
-        total = mine + given
+        early = spread(jnp.concatenate(owns), early_over, early_other)
+        other_cols = jnp.concatenate([early, spread(last, last_over, last_other)])
+        mine, given = summed[0], both_ways(summed[1], "feat")
     else:
-        total = lax.psum_scatter(part, WIDE, scatter_dimension=0, tiled=True)
-        tile = covariance_of(gathered, other_cols)
-    scores = jnp.transpose(total) / jnp.sqrt(jnp.float32(gathered.shape[1] * group))
-    return (tile, scores)
+        mine, given = lax.psum_scatter(part, WIDE, scatter_dimension=0, tiled=True), jnp.zeros((own, ids.shape[0]), F32)
+    tile, total = covariance_of(gathered, other_cols, mine, given)
+    return (tile, jnp.transpose(total))
 
 
 def solution(mesh):

time: 70.3 us -> 64.7 us (0.920)
  waiting for transfers between devices: 28.3 us -> 26.3 us
  local copies, waits for them, and re-layouts: 5.42 us -> 3.66 us
  starting transfers between devices: 19.4 us -> 17.7 us
    ppermute x16 -> x17, waiting for transfers between devices: 12.6 us -> 9.59 us  [both_ways(): return lax.ppermute(x, axis, [(0, 1), (1, 0)])]
    ppermute x3, starting transfers between devices: 6.16 us -> 4.01 us  [around(): lax.ppermute(part, 'dp', [(RING[i], RING[(i + 1) % 4]) for i in range(4)])]
    unnamed x12 -> x14, local copies, waits for them, and re-layouts: 4.99 us -> 3.21 us
    ppermute x3, waiting for transfers between devices: 15.8 us -> 16.7 us  [around(): lax.ppermute(part, 'dp', [(RING[i], RING[(i + 1) % 4]) for i in range(4)])]
    ppermute x16 -> x17, starting transfers between devices: 13.2 us -> 13.7 us  [both_ways(): return lax.ppermute(x, axis, [(0, 1), (1, 0)])]
  transfers between devices with their start and end apart: 19 -> 20, of which waited for: 12 -> 10; matrix products, arithmetic and copies ran while one was open for 2% -> 4% of each run, Pallas kernels for 11% -> 3%
where the time goes in v4:
time: 64.7 us; the launch traced here: 64.3 us
  waiting for transfers between devices  26.3 us (41%)
  starting transfers between devices  17.7 us (27%)
  Pallas kernels  13.2 us (20%)
  local copies, waits for them, and re-layouts  3.66 us (6%)
  other arithmetic  2.36 us (4%)
  between operations  0.97 us (1%)
    ppermute x3, waiting for transfers between devices, around(): lax.ppermute(part, 'dp', [(RING[i], RING[(i + 1) % 4]) for i in range(4)])  16.7 us
    ppermute x17, starting transfers between devices, both_ways(): return lax.ppermute(x, axis, [(0, 1), (1, 0)])  13.7 us
    ppermute x17, waiting for transfers between devices, both_ways(): return lax.ppermute(x, axis, [(0, 1), (1, 0)])  9.59 us
    pallas_call x1, Pallas kernels, covariance_of(): pl.pallas_call(covariance_kernel, in_specs=[VMEM] * 4, out_specs=[pl.Bloc...  6.4 us
    ppermute x3, starting transfers between devices, around(): lax.ppermute(part, 'dp', [(RING[i], RING[(i + 1) % 4]) for i in range(4)])  4.01 us
    pallas_call x1, Pallas kernels, features_of(): pl.pallas_call(feature_kernel, in_specs=[SMEM, SMEM, VMEM, VMEM, VMEM], o...  3.76 us
    unnamed x14, local copies, waits for them, and re-layouts  3.21 us
    pallas_call x2, Pallas kernels, project(): pl.pallas_call(project_flipped_kernel if flipped else project_kernel, in_...  2.41 us
  transfers between devices with their start and end apart: 20, of which 10 were waited for; matrix products, arithmetic and copies ran while one was open for 4% of the time, Pallas kernels for 3%

profile of v4, /device:TPU:0, one launch (start us, length us, event | category | flops | bytes accessed | tf_op | source)
XLA Modules:
  0.0 64.3 jit_solution(8546958717983997277)
XLA Ops:
  0.6 2.0 %copy-done.2 = bf16[1792,1024]{1,0:T(8,128)(2,1)S(1)} copy-done((bf16[1792,1024]{1,0:T(8,128)(2,1)S(1)}, bf16[1792,1024]{1,0:T(8,128)(2,1)}, u32[]{:S(2)}) %copy-start.2) | copy-done | bytes 3670040
  2.7 0.9 %copy-done.3 = bf16[1024,64]{0,1:T(8,128)(2,1)S(1)} copy-done((bf16[1024,64]{0,1:T(8,128)(2,1)S(1)}, bf16[1024,64]{0,1:T(8,128)(2,1)}, u32[]{:S(2)}) %copy-start.3) | copy-done | bytes 131096
  3.6 1.2 %project.2 = f32[64,1792]{1,0:T(8,128)S(1)} custom-call(bf16[1792,1024]{1,0:T(8,128)(2,1)S(1)} %copy-done.2, bf16[64,1024]{1,0:T(8,128)(2,1)S(1)} %bitcast.47), custom_call_target="tpu_custom_call" | custom-call | flops 4697620480 | bytes 3670016 | tf_op jit(solution)/shard_map/project/pallas_call | solution.py:35
  4.9 0.5 collective-permute-start
  5.4 0.2 copy-done
  5.6 1.2 %project.3 = f32[128,1792]{1,0:T(8,128)S(1)} custom-call(bf16[1792,1024]{1,0:T(8,128)(2,1)S(1)} %copy-done, bf16[1024,128]{1,0:T(8,128)(2,1)S(1)} %copy-done.1), custom_call_target="tpu_custom_call" | custom-call | flops 469762048 | bytes 3670016 | tf_op jit(solution)/shard_map/project/pallas_call | solution.py:35
  6.9 0.5 collective-permute-start.2
  7.4 0.1 copy.10
  7.5 0.1 reduce-window.9
  7.6 0.1 reduce.end_ref
  7.7 0.1 abs_reduce_fusion
  7.9 0.1 round-nearest-even_convert_fusion
  8.0 0.1 broadcast_in_dim.10
  8.1 2.6 %collective-permute-start.1 = (s16[32,1920]{1,0:T(8,128)(2,1)S(1)}, s16[32,1920]{1,0:T(8,128)(2,1)S(1)}, u32[]{:S(2)}, u32[]{:S(2)}) collective-permute-start(s16[32,1920]{1,0:T(8,128)(2,1)S(1)} %pad_add_fusion), channel_id=1, source_target_pairs={{0,2},{2,0},{1,3},{3,1},{4,6},{6,4},{5,7},{7,5},{8,10},{10,8},{9,1... | collective-permute-start | bytes 368648 | tf_op jit(solution)/shard_map/ppermute | solution.py:198
  10.7 0.1 bitcast_add_fusion
  10.7 0.1 fusion.2
  10.9 0.1 fusion.4
  11.1 1.1 %collective-permute-start.4 = (s16[32,1920]{1,0:T(8,128)(2,1)S(1)}, s16[32,1920]{1,0:T(8,128)(2,1)S(1)}, u32[]{:S(2)}, u32[]{:S(2)}) collective-permute-start(s16[32,1920]{1,0:T(8,128)(2,1)S(1)} %pad_add_fusion.1), channel_id=1, source_target_pairs={{0,2},{2,0},{1,3},{3,1},{4,6},{6,4},{5,7},{7,5},{8,10},{10,8},{9,1... | collective-permute-start | bytes 368648 | tf_op jit(solution)/shard_map/ppermute | solution.py:198
  12.2 2.6 %collective-permute-done.1 = s16[32,1920]{1,0:T(8,128)(2,1)S(1)} collective-permute-done((s16[32,1920]{1,0:T(8,128)(2,1)S(1)}, s16[32,1920]{1,0:T(8,128)(2,1)S(1)}, u32[]{:S(2)}, u32[]{:S(2)}) %collective-permute-start.1) | collective-permute-done | bytes 122912 | tf_op jit(solution)/shard_map/ppermute | solution.py:198
  14.9 0.1 fusion.10
  15.0 0.1 fusion.1
  15.2 2.1 %collective-permute-done.4 = s16[32,1920]{1,0:T(8,128)(2,1)S(1)} collective-permute-done((s16[32,1920]{1,0:T(8,128)(2,1)S(1)}, s16[32,1920]{1,0:T(8,128)(2,1)S(1)}, u32[]{:S(2)}, u32[]{:S(2)}) %collective-permute-start.4) | collective-permute-done | bytes 122912 | tf_op jit(solution)/shard_map/ppermute | solution.py:198
  17.3 0.1 fusion.7
  17.4 0.1 fusion.v_ref
  17.7 3.8 %features.1 = bf16[56,2048]{1,0:T(8,128)(2,1)S(1)} custom-call(s32[56]{0:T(128)S(1)} %bitcast_subtract_fusion.start_ref, s32[56]{0:T(128)S(1)} %reduce.end_ref, f32[64,1792]{1,0:T(8,128)S(1)} %pad_maximum_fusion.2.u_ref, f32[32,1792]{1,0:T(8,128)S(1)} %fusion.v_ref, f32[56,128]{1,0:T(8,128)S(1)} %broadcast_in_dim.12.scale_ref), custom_call_target="tpu_custom_call" | custom-call | tf_op jit(solution)/shard_map/features/pallas_call | solution.py:114
  21.6 1.9 %collective-permute-start.5 = (bf16[56,2048]{1,0:T(8,128)(2,1)S(1)}, bf16[56,2048]{1,0:T(8,128)(2,1)S(1)}, u32[]{:S(2)}, u32[]{:S(2)}) collective-permute-start(bf16[56,2048]{1,0:T(8,128)(2,1)S(1)} %features.1), channel_id=1, source_target_pairs={{0,4},{4,12},{12,8},{8,0},{1,5},{5,13},{13,9},{9,1},{2,6},{6,14},{... | collective-permute-start | bytes 688136 | tf_op jit(solution)/shard_map/ppermute | solution.py:253
  23.5 1.6 %collective-permute-start.7 = (bf16[56,1024]{1,0:T(8,128)(2,1)S(1)}, bf16[56,1024]{1,0:T(8,128)(2,1)S(1)}, u32[]{:S(2)}, u32[]{:S(2)}) collective-permute-start(bf16[56,1024]{1,0:T(8,128)(2,1)S(1)} %slice_select_fusion.4), channel_id=1, source_target_pairs={{0,2},{2,0},{1,3},{3,1},{4,6},{6,4},{5,7},{7,5},{8,10},{10,8},{9,1... | collective-permute-start | bytes 344072 | tf_op jit(solution)/shard_map/ppermute | solution.py:198
  25.0 5.4 %collective-permute-done.5 = bf16[56,2048]{1,0:T(8,128)(2,1)S(1)} collective-permute-done((bf16[56,2048]{1,0:T(8,128)(2,1)S(1)}, bf16[56,2048]{1,0:T(8,128)(2,1)S(1)}, u32[]{:S(2)}, u32[]{:S(2)}) %collective-permute-start.5) | collective-permute-done | bytes 229408 | tf_op jit(solution)/shard_map/ppermute | solution.py:253
  30.5 1.0 %collective-permute-start.8 = (bf16[56,2048]{1,0:T(8,128)(2,1)S(1)}, bf16[56,2048]{1,0:T(8,128)(2,1)S(1)}, u32[]{:S(2)}, u32[]{:S(2)}) collective-permute-start(bf16[56,2048]{1,0:T(8,128)(2,1)S(1)} %collective-permute-done.5), channel_id=1, source_target_pairs={{0,4},{4,12},{12,8},{8,0},{1,5},{5,13},{13,9},{9,1},{2,6},{6,14},{... | collective-permute-start | bytes 688136 | tf_op jit(solution)/shard_map/ppermute | solution.py:253
  31.5 0.4 collective-permute-done.9
  32.0 1.8 %collective-permute-start.10 = (bf16[56,1024]{1,0:T(8,128)(2,1)S(1)}, bf16[56,1024]{1,0:T(8,128)(2,1)S(1)}, u32[]{:S(2)}, u32[]{:S(2)}) collective-permute-start(bf16[56,1024]{1,0:T(8,128)(2,1)S(1)} %slice_select_fusion.3), channel_id=1, source_target_pairs={{0,2},{2,0},{1,3},{3,1},{4,6},{6,4},{5,7},{7,5},{8,10},{10,8},{9,1... | collective-permute-start | bytes 344072 | tf_op jit(solution)/shard_map/ppermute | solution.py:198
  33.8 5.6 %collective-permute-done.8 = bf16[56,2048]{1,0:T(8,128)(2,1)S(1)} collective-permute-done((bf16[56,2048]{1,0:T(8,128)(2,1)S(1)}, bf16[56,2048]{1,0:T(8,128)(2,1)S(1)}, u32[]{:S(2)}, u32[]{:S(2)}) %collective-permute-start.8) | collective-permute-done | bytes 229408 | tf_op jit(solution)/shard_map/ppermute | solution.py:253
  39.4 0.1 copy.13.ids_ref
  39.5 1.1 %collective-permute-start.11 = (bf16[56,2048]{1,0:T(8,128)(2,1)S(1)}, bf16[56,2048]{1,0:T(8,128)(2,1)S(1)}, u32[]{:S(2)}, u32[]{:S(2)}) collective-permute-start(bf16[56,2048]{1,0:T(8,128)(2,1)S(1)} %collective-permute-done.8), channel_id=1, source_target_pairs={{0,4},{4,12},{12,8},{8,0},{1,5},{5,13},{13,9},{9,1},{2,6},{6,14},{... | collective-permute-start | bytes 688136 | tf_op jit(solution)/shard_map/ppermute | solution.py:253
  40.6 0.3 collective-permute-done.12
  40.9 1.8 %collective-permute-start.13 = (bf16[56,1024]{1,0:T(8,128)(2,1)S(1)}, bf16[56,1024]{1,0:T(8,128)(2,1)S(1)}, u32[]{:S(2)}, u32[]{:S(2)}) collective-permute-start(bf16[56,1024]{1,0:T(8,128)(2,1)S(1)} %slice_select_fusion.2), channel_id=1, source_target_pairs={{0,2},{2,0},{1,3},{3,1},{4,6},{6,4},{5,7},{7,5},{8,10},{10,8},{9,1... | collective-permute-start | bytes 344072 | tf_op jit(solution)/shard_map/ppermute | solution.py:198
  42.7 5.7 %collective-permute-done.11 = bf16[56,2048]{1,0:T(8,128)(2,1)S(1)} collective-permute-done((bf16[56,2048]{1,0:T(8,128)(2,1)S(1)}, bf16[56,2048]{1,0:T(8,128)(2,1)S(1)}, u32[]{:S(2)}, u32[]{:S(2)}) %collective-permute-start.11) | collective-permute-done | bytes 229408 | tf_op jit(solution)/shard_map/ppermute | solution.py:253
  48.5 0.2 multiply_reduce_fusion
  48.8 0.6 collective-permute-start.14
  49.4 0.6 %partial_scores.1 = f32[224,64]{1,0:T(8,128)S(1)} custom-call(s32[64,1]{1,0:T(8,128)S(1)} %copy.13.ids_ref, bf16[224,2048]{1,0:T(8,128)(2,1)S(1)} %get-tuple-element.25.all_ref.row_ref, f32[1,2048]{1,0:T(1,128)S(1)} %bitcast.46), custom_call_target="tpu_custom_call" | custom-call | flops 234881024 | bytes 917504 | tf_op jit(solution)/shard_map/partial_scores/pallas_call | solution.py:146
  50.0 0.2 collective-permute-done.15
  50.4 0.2 collective-permute-start.18
  50.6 1.8 %collective-permute-start.16 = (bf16[56,1024]{1,0:T(8,128)(2,1)S(1)}, bf16[56,1024]{1,0:T(8,128)(2,1)S(1)}, u32[]{:S(2)}, u32[]{:S(2)}) collective-permute-start(bf16[56,1024]{1,0:T(8,128)(2,1)S(1)} %slice_select_fusion.5), channel_id=1, source_target_pairs={{0,2},{2,0},{1,3},{3,1},{4,6},{6,4},{5,7},{7,5},{8,10},{10,8},{9,1... | collective-permute-start | bytes 344072 | tf_op jit(solution)/shard_map/ppermute | solution.py:198
  52.4 1.1 %collective-permute-start.19 = (f32[56,64]{1,0:T(8,128)S(1)}, f32[56,64]{1,0:T(8,128)S(1)}, u32[]{:S(2)}, u32[]{:S(2)}) collective-permute-start(f32[56,64]{1,0:T(8,128)S(1)} %get-tuple-element.38), channel_id=1, source_target_pairs={{0,2},{2,0},{1,3},{3,1},{4,6},{6,4},{5,7},{7,5},{8,10},{10,8},{9,1... | collective-permute-start | bytes 43016 | tf_op jit(solution)/shard_map/ppermute | solution.py:198
  53.5 2.9 %collective-permute-done.16 = bf16[56,1024]{1,0:T(8,128)(2,1)S(1)} collective-permute-done((bf16[56,1024]{1,0:T(8,128)(2,1)S(1)}, bf16[56,1024]{1,0:T(8,128)(2,1)S(1)}, u32[]{:S(2)}, u32[]{:S(2)}) %collective-permute-start.16) | collective-permute-done | bytes 114720 | tf_op jit(solution)/shard_map/ppermute | solution.py:198
  56.4 0.2 maximum_select_fusion
  56.7 1.0 %collective-permute-done.17 = bf16[56,1024]{1,0:T(8,128)(2,1)S(1)} collective-permute-done((bf16[56,1024]{1,0:T(8,128)(2,1)S(1)}, bf16[56,1024]{1,0:T(8,128)(2,1)S(1)}, u32[]{:S(2)}, u32[]{:S(2)}) %collective-permute-start.17) | collective-permute-done | bytes 114720 | tf_op jit(solution)/shard_map/ppermute | solution.py:198
  57.9 6.4 %covariance.1 = (f32[2048,2048]{1,0:T(8,128)}, f32[56,64]{1,0:T(8,128)}) custom-call(bf16[224,2048]{1,0:T(8,128)(2,1)S(1)} %get-tuple-element.25.all_ref.row_ref, bf16[224,2048]{1,0:T(8,128)(2,1)S(1)} %pad_maximum_fusion.1.col_ref, f32[56,64]{1,0:T(8,128)S(1)} %get-tuple-element.39.one_ref, f32[56,64]{1,0:T(8,128)S(1)} %collective-permute-done.19.two_ref), custom_call_target="tpu_custom_call" | custom-call | flops 1879048192 | bytes 16777216 | tf_op jit(solution)/shard_map/covariance/pallas_call | solution.py:181
  (60 shorter events, 1.2 us)
Async XLA Ops:
  0.6 2.0 %copy-start.2 = (bf16[1792,1024]{1,0:T(8,128)(2,1)S(1)}, bf16[1792,1024]{1,0:T(8,128)(2,1)}, u32[]{:S(2)}) copy-start(bf16[1792,1024]{1,0:T(8,128)(2,1)} %x_ref.2) | copy-start | bytes 11010052
  2.7 0.9 %copy-start.3 = (bf16[1024,64]{0,1:T(8,128)(2,1)S(1)}, bf16[1024,64]{0,1:T(8,128)(2,1)}, u32[]{:S(2)}) copy-start(bf16[1024,64]{0,1:T(8,128)(2,1)} %param.8) | copy-start | bytes 393220
  3.6 2.0 %copy-start = (bf16[1792,1024]{1,0:T(8,128)(2,1)S(1)}, bf16[1792,1024]{1,0:T(8,128)(2,1)}, u32[]{:S(2)}) copy-start(bf16[1792,1024]{1,0:T(8,128)(2,1)} %x_ref.3) | copy-start | bytes 11010052
  3.6 2.1 %copy-start.1 = (bf16[1024,128]{1,0:T(8,128)(2,1)S(1)}, bf16[1024,128]{1,0:T(8,128)(2,1)}, u32[]{:S(2)}) copy-start(bf16[1024,128]{1,0:T(8,128)(2,1)} %weight_ref.1) | copy-start | bytes 786436
  4.9 2.5 %copy-start.4 = (s32[1,56]{1,0:T(1,128)S(1)}, s32[1,56]{1,0:T(1,128)}, u32[]{:S(2)}) copy-start(s32[1,56]{1,0:T(1,128)} %param.10) | copy-start | bytes 676
  4.9 2.8 %collective-permute-start = (f32[32,1792]{1,0:T(8,128)S(1)}, f32[32,1792]{1,0:T(8,128)S(1)}, u32[]{:S(2)}, u32[]{:S(2)}) collective-permute-start(f32[32,1792]{1,0:T(8,128)S(1)} %slice_select_fusion.1), channel_id=1, source_target_pairs={{0,1},{1,0},{2,3},{3,2},{4,5},{5,4},{6,7},{7,6},{8,9},{9,8},{10,11... | collective-permute-start | bytes 688136 | tf_op jit(solution)/shard_map/ppermute | solution.py:198
  6.9 3.8 %collective-permute-start.2 = (f32[2,32,1792]{2,1,0:T(8,128)S(1)}, f32[2,32,1792]{2,1,0:T(8,128)S(1)}, u32[]{:S(2)}, u32[]{:S(2)}) collective-permute-start(f32[2,32,1792]{2,1,0:T(8,128)S(1)} %select_bitcast_fusion), channel_id=1, source_target_pairs={{0,1},{1,0},{2,3},{3,2},{4,5},{5,4},{6,7},{7,6},{8,9},{9,8},{10,11... | collective-permute-start | bytes 1376264 | tf_op jit(solution)/shard_map/ppermute | solution.py:198
  8.1 6.8 %collective-permute-start.1 = (s16[32,1920]{1,0:T(8,128)(2,1)S(1)}, s16[32,1920]{1,0:T(8,128)(2,1)S(1)}, u32[]{:S(2)}, u32[]{:S(2)}) collective-permute-start(s16[32,1920]{1,0:T(8,128)(2,1)S(1)} %pad_add_fusion), channel_id=1, source_target_pairs={{0,2},{2,0},{1,3},{3,1},{4,6},{6,4},{5,7},{7,5},{8,10},{10,8},{9,1... | collective-permute-start | bytes 368648 | tf_op jit(solution)/shard_map/ppermute | solution.py:198
  11.1 6.2 %collective-permute-start.4 = (s16[32,1920]{1,0:T(8,128)(2,1)S(1)}, s16[32,1920]{1,0:T(8,128)(2,1)S(1)}, u32[]{:S(2)}, u32[]{:S(2)}) collective-permute-start(s16[32,1920]{1,0:T(8,128)(2,1)S(1)} %pad_add_fusion.1), channel_id=1, source_target_pairs={{0,2},{2,0},{1,3},{3,1},{4,6},{6,4},{5,7},{7,5},{8,10},{10,8},{9,1... | collective-permute-start | bytes 368648 | tf_op jit(solution)/shard_map/ppermute | solution.py:198
  15.1 2.4 %collective-permute-start.3 = (f32[32,1792]{1,0:T(8,128)S(1)}, f32[32,1792]{1,0:T(8,128)S(1)}, u32[]{:S(2)}, u32[]{:S(2)}) collective-permute-start(f32[32,1792]{1,0:T(8,128)S(1)} %fusion.1), channel_id=1, source_target_pairs={{0,1},{1,0},{2,3},{3,2},{4,5},{5,4},{6,7},{7,6},{8,9},{9,8},{10,11... | collective-permute-start | bytes 688136 | tf_op jit(solution)/shard_map/ppermute | solution.py:198
  17.6 21.8 %copy-start.5 = (s32[64]{0:T(128)S(1)}, s32[64]{0:T(128)}, u32[]{:S(2)}) copy-start(s32[64]{0:T(128)} %param.11) | copy-start | bytes 772
  21.5 2.0 %collective-permute-start.6 = (bf16[56,2048]{1,0:T(8,128)(2,1)S(1)}, bf16[56,2048]{1,0:T(8,128)(2,1)S(1)}, u32[]{:S(2)}, u32[]{:S(2)}) collective-permute-start(bf16[56,2048]{1,0:T(8,128)(2,1)S(1)} %features.1), channel_id=1, source_target_pairs={{0,1},{1,0},{2,3},{3,2},{4,5},{5,4},{6,7},{7,6},{8,9},{9,8},{10,11... | collective-permute-start | bytes 688136 | tf_op jit(solution)/shard_map/ppermute | solution.py:198
  21.6 8.9 %collective-permute-start.5 = (bf16[56,2048]{1,0:T(8,128)(2,1)S(1)}, bf16[56,2048]{1,0:T(8,128)(2,1)S(1)}, u32[]{:S(2)}, u32[]{:S(2)}) collective-permute-start(bf16[56,2048]{1,0:T(8,128)(2,1)S(1)} %features.1), channel_id=1, source_target_pairs={{0,4},{4,12},{12,8},{8,0},{1,5},{5,13},{13,9},{9,1},{2,6},{6,14},{... | collective-permute-start | bytes 688136 | tf_op jit(solution)/shard_map/ppermute | solution.py:253
  23.5 7.0 %collective-permute-start.7 = (bf16[56,1024]{1,0:T(8,128)(2,1)S(1)}, bf16[56,1024]{1,0:T(8,128)(2,1)S(1)}, u32[]{:S(2)}, u32[]{:S(2)}) collective-permute-start(bf16[56,1024]{1,0:T(8,128)(2,1)S(1)} %slice_select_fusion.4), channel_id=1, source_target_pairs={{0,2},{2,0},{1,3},{3,1},{4,6},{6,4},{5,7},{7,5},{8,10},{10,8},{9,1... | collective-permute-start | bytes 344072 | tf_op jit(solution)/shard_map/ppermute | solution.py:198
  30.5 1.5 %collective-permute-start.9 = (bf16[56,2048]{1,0:T(8,128)(2,1)S(1)}, bf16[56,2048]{1,0:T(8,128)(2,1)S(1)}, u32[]{:S(2)}, u32[]{:S(2)}) collective-permute-start(bf16[56,2048]{1,0:T(8,128)(2,1)S(1)} %collective-permute-done.5), channel_id=1, source_target_pairs={{0,1},{1,0},{2,3},{3,2},{4,5},{5,4},{6,7},{7,6},{8,9},{9,8},{10,11... | collective-permute-start | bytes 688136 | tf_op jit(solution)/shard_map/ppermute | solution.py:198
  30.5 8.9 %collective-permute-start.8 = (bf16[56,2048]{1,0:T(8,128)(2,1)S(1)}, bf16[56,2048]{1,0:T(8,128)(2,1)S(1)}, u32[]{:S(2)}, u32[]{:S(2)}) collective-permute-start(bf16[56,2048]{1,0:T(8,128)(2,1)S(1)} %collective-permute-done.5), channel_id=1, source_target_pairs={{0,4},{4,12},{12,8},{8,0},{1,5},{5,13},{13,9},{9,1},{2,6},{6,14},{... | collective-permute-start | bytes 688136 | tf_op jit(solution)/shard_map/ppermute | solution.py:253
  32.0 7.4 %collective-permute-start.10 = (bf16[56,1024]{1,0:T(8,128)(2,1)S(1)}, bf16[56,1024]{1,0:T(8,128)(2,1)S(1)}, u32[]{:S(2)}, u32[]{:S(2)}) collective-permute-start(bf16[56,1024]{1,0:T(8,128)(2,1)S(1)} %slice_select_fusion.3), channel_id=1, source_target_pairs={{0,2},{2,0},{1,3},{3,1},{4,6},{6,4},{5,7},{7,5},{8,10},{10,8},{9,1... | collective-permute-start | bytes 344072 | tf_op jit(solution)/shard_map/ppermute | solution.py:198
  39.4 1.5 %collective-permute-start.12 = (bf16[56,2048]{1,0:T(8,128)(2,1)S(1)}, bf16[56,2048]{1,0:T(8,128)(2,1)S(1)}, u32[]{:S(2)}, u32[]{:S(2)}) collective-permute-start(bf16[56,2048]{1,0:T(8,128)(2,1)S(1)} %collective-permute-done.8), channel_id=1, source_target_pairs={{0,1},{1,0},{2,3},{3,2},{4,5},{5,4},{6,7},{7,6},{8,9},{9,8},{10,11... | collective-permute-start | bytes 688136 | tf_op jit(solution)/shard_map/ppermute | solution.py:198
  39.5 9.0 %collective-permute-start.11 = (bf16[56,2048]{1,0:T(8,128)(2,1)S(1)}, bf16[56,2048]{1,0:T(8,128)(2,1)S(1)}, u32[]{:S(2)}, u32[]{:S(2)}) collective-permute-start(bf16[56,2048]{1,0:T(8,128)(2,1)S(1)} %collective-permute-done.8), channel_id=1, source_target_pairs={{0,4},{4,12},{12,8},{8,0},{1,5},{5,13},{13,9},{9,1},{2,6},{6,14},{... | collective-permute-start | bytes 688136 | tf_op jit(solution)/shard_map/ppermute | solution.py:253
  40.9 7.6 %collective-permute-start.13 = (bf16[56,1024]{1,0:T(8,128)(2,1)S(1)}, bf16[56,1024]{1,0:T(8,128)(2,1)S(1)}, u32[]{:S(2)}, u32[]{:S(2)}) collective-permute-start(bf16[56,1024]{1,0:T(8,128)(2,1)S(1)} %slice_select_fusion.2), channel_id=1, source_target_pairs={{0,2},{2,0},{1,3},{3,1},{4,6},{6,4},{5,7},{7,5},{8,10},{10,8},{9,1... | collective-permute-start | bytes 344072 | tf_op jit(solution)/shard_map/ppermute | solution.py:198
  48.7 1.6 %collective-permute-start.15 = (bf16[56,2048]{1,0:T(8,128)(2,1)S(1)}, bf16[56,2048]{1,0:T(8,128)(2,1)S(1)}, u32[]{:S(2)}, u32[]{:S(2)}) collective-permute-start(bf16[56,2048]{1,0:T(8,128)(2,1)S(1)} %collective-permute-done.11), channel_id=1, source_target_pairs={{0,1},{1,0},{2,3},{3,2},{4,5},{5,4},{6,7},{7,6},{8,9},{9,8},{10,11... | collective-permute-start | bytes 688136 | tf_op jit(solution)/shard_map/ppermute | solution.py:198
  48.8 7.6 %collective-permute-start.14 = (bf16[168,1024]{1,0:T(8,128)(2,1)S(1)}, bf16[168,1024]{1,0:T(8,128)(2,1)S(1)}, u32[]{:S(2)}, u32[]{:S(2)}) collective-permute-start(bf16[168,1024]{1,0:T(8,128)(2,1)S(1)} %constant_dynamic-update-slice_fusion), channel_id=1, source_target_pairs={{0,1},{1,0},{2,3},{3,2},{4,5},{5,4},{6,7},{7,6},{8,9},{9,8},{10,11... | collective-permute-start | bytes 1032200 | tf_op jit(solution)/shard_map/ppermute | solution.py:198
  50.4 2.0 %collective-permute-start.18 = (f32[2,56,64]{2,1,0:T(8,128)S(1)}, f32[2,56,64]{2,1,0:T(8,128)S(1)}, u32[]{:S(2)}, u32[]{:S(2)}) collective-permute-start(f32[2,56,64]{2,1,0:T(8,128)S(1)} %pad_maximum_fusion.3), channel_id=1, source_target_pairs={{0,1},{1,0},{2,3},{3,2},{4,5},{5,4},{6,7},{7,6},{8,9},{9,8},{10,11... | collective-permute-start | bytes 86024 | tf_op jit(solution)/shard_map/ppermute | solution.py:198
  50.6 5.8 %collective-permute-start.16 = (bf16[56,1024]{1,0:T(8,128)(2,1)S(1)}, bf16[56,1024]{1,0:T(8,128)(2,1)S(1)}, u32[]{:S(2)}, u32[]{:S(2)}) collective-permute-start(bf16[56,1024]{1,0:T(8,128)(2,1)S(1)} %slice_select_fusion.5), channel_id=1, source_target_pairs={{0,2},{2,0},{1,3},{3,1},{4,6},{6,4},{5,7},{7,5},{8,10},{10,8},{9,1... | collective-permute-start | bytes 344072 | tf_op jit(solution)/shard_map/ppermute | solution.py:198
  52.4 5.4 %collective-permute-start.19 = (f32[56,64]{1,0:T(8,128)S(1)}, f32[56,64]{1,0:T(8,128)S(1)}, u32[]{:S(2)}, u32[]{:S(2)}) collective-permute-start(f32[56,64]{1,0:T(8,128)S(1)} %get-tuple-element.38), channel_id=1, source_target_pairs={{0,2},{2,0},{1,3},{3,1},{4,6},{6,4},{5,7},{7,5},{8,10},{10,8},{9,1... | collective-permute-start | bytes 43016 | tf_op jit(solution)/shard_map/ppermute | solution.py:198
  56.4 1.3 %collective-permute-start.17 = (bf16[56,1024]{1,0:T(8,128)(2,1)S(1)}, bf16[56,1024]{1,0:T(8,128)(2,1)S(1)}, u32[]{:S(2)}, u32[]{:S(2)}) collective-permute-start(bf16[56,1024]{1,0:T(8,128)(2,1)S(1)} %collective-permute-done.16), channel_id=1, source_target_pairs={{0,1},{1,0},{2,3},{3,2},{4,5},{5,4},{6,7},{7,6},{8,9},{9,8},{10,11... | collective-permute-start | bytes 344072 | tf_op jit(solution)/shard_map/ppermute | solution.py:198

commit v5 on v4

--- a/solution.py
+++ b/solution.py
@@ -1,3 +1,5 @@
+import functools
+
 import jax
 import jax.numpy as jnp
 from jax import lax
@@ -67,39 +69,38 @@
         ref[:, tokens:] = jnp.zeros((ref.shape[0], ref.shape[1] - tokens), BF16)
     lane = lax.broadcasted_iota(I32, (8, tile), 1)
     left = lax.broadcasted_iota(I32, (8, 2 * rank_in), 1) < rank_in
+    sets = range(0, seqs, 4)
+    bases = [(start_ref[s] // 128) * 128 for s in sets]
+    needs = [(end_ref[s + 3] - base + tile - 1) // tile for s, base in zip(sets, bases)]
+
+    def add(k, begun):
+        for i, first in enumerate(sets):
+            at = pl.multiple_of(bases[i] + k * tile, 128)
+            tops, lows = [], []
+            v_high = vh[:, pl.ds(at, tile)]
+            v_low = vl[:, pl.ds(at, tile)]
+            for s in range(first, first + 4):
+                begin = start_ref[s] - at
+                stop = end_ref[s] - at
+                inside = jnp.where((lane >= begin) & (lane < stop), 1.0, 0.0).astype(F32)
+                inside = jnp.concatenate([inside] * (share // 8), axis=0).astype(BF16)
+                tops.append(v_high * inside)
+                lows.append(v_low * inside)
+            total = jnp.dot(
+                jnp.concatenate(tops + lows, 0), uu[pl.ds(at, tile), :], preferred_element_type=F32
+            )
+            total = total[: 4 * share] + total[4 * share :]
+            rows = slice(4 * share * i, 4 * share * (i + 1))
+            acc[rows, :] = acc[rows, :] + total if begun else total
+
+    add(0, False)
+    lax.fori_loop(1, functools.reduce(jnp.maximum, needs), lambda k, carry: add(k, True) or carry, 0)
     for group in range(seqs // 8):
-        sets = (8 * group, 8 * group + 4)
-        bases = [(start_ref[s] // 128) * 128 for s in sets]
-        needs = [(end_ref[s + 3] - base + tile - 1) // tile for s, base in zip(sets, bases)]
-        acc[...] = jnp.zeros_like(acc)
-
-        def step(k, carry):
-            for i in range(2):
-                at = pl.multiple_of(bases[i] + k * tile, 128)
-                tops, lows = [], []
-                v_high = vh[:, pl.ds(at, tile)]
-                v_low = vl[:, pl.ds(at, tile)]
-                for s in range(sets[i], sets[i] + 4):
-                    begin = start_ref[s] - at
-                    stop = end_ref[s] - at
-                    inside = jnp.where((lane >= begin) & (lane < stop), 1.0, 0.0).astype(F32)
-                    inside = jnp.concatenate([inside] * (share // 8), axis=0).astype(BF16)
-                    tops.append(v_high * inside)
-                    lows.append(v_low * inside)
-                total = jnp.dot(
-                    jnp.concatenate(tops + lows, 0),
-                    uu[pl.ds(at, tile), :],
-                    preferred_element_type=F32,
-                )
-                rows = slice(4 * share * i, 4 * share * (i + 1))
-                acc[rows, :] += total[: 4 * share] + total[4 * share :]
-            return carry
-
-        lax.fori_loop(0, jnp.maximum(needs[0], needs[1]), step, 0)
         factor = scale_ref[8 * group : 8 * group + 8, :]
         for pair in range(share // 2):
-            even = acc[pl.ds(2 * pair, 8, stride=share), :]
-            odd = acc[pl.ds(2 * pair + 1, 8, stride=share), :]
+            row = 8 * share * group + 2 * pair
+            even = acc[pl.ds(row, 8, stride=share), :]
+            odd = acc[pl.ds(row + 1, 8, stride=share), :]
             even = even + pltpu.roll(even, rank_in, 1)
             odd = odd + pltpu.roll(odd, rank_in, 1)
             both = jnp.where(left, even, odd) * factor
@@ -120,7 +121,7 @@
             pltpu.VMEM((tokens + 768, 2 * rank_in), BF16),
             pltpu.VMEM((share, tokens + 768), BF16),
             pltpu.VMEM((share, tokens + 768), BF16),
-            pltpu.VMEM((8 * share, 2 * rank_in), F32),
+            pltpu.VMEM((seqs * share, 2 * rank_in), F32),
             pltpu.VMEM((seqs, share * rank_in), F32),
         ],
         compiler_params=params(16),

time: 64.7 us -> 63.6 us (0.983)
  waiting for transfers between devices: 26.3 us -> 27.4 us
  Pallas kernels: 13.2 us -> 12.2 us
  starting transfers between devices: 17.7 us -> 16.8 us
    pallas_call x1, Pallas kernels: 3.76 us -> 2.7 us  [features_of(): pl.pallas_call(feature_kernel, in_specs=[SMEM, SMEM, VMEM, VMEM, VMEM], o...]
where the time goes in v5:
time: 63.6 us; the launch traced here: 63.4 us
  waiting for transfers between devices  27.4 us (43%)
  starting transfers between devices  16.8 us (26%)
  Pallas kernels  12.2 us (19%)
  local copies, waits for them, and re-layouts  3.66 us (6%)
  other arithmetic  2.36 us (4%)
  between operations  0.97 us (2%)
    ppermute x3, waiting for transfers between devices, around(): lax.ppermute(part, 'dp', [(RING[i], RING[(i + 1) % 4]) for i in range(4)])  17.3 us
    ppermute x17, starting transfers between devices, both_ways(): return lax.ppermute(x, axis, [(0, 1), (1, 0)])  13.2 us
    ppermute x17, waiting for transfers between devices, both_ways(): return lax.ppermute(x, axis, [(0, 1), (1, 0)])  10.1 us
    pallas_call x1, Pallas kernels, covariance_of(): pl.pallas_call(covariance_kernel, in_specs=[VMEM] * 4, out_specs=[pl.Bloc...  6.4 us
    ppermute x3, starting transfers between devices, around(): lax.ppermute(part, 'dp', [(RING[i], RING[(i + 1) % 4]) for i in range(4)])  3.64 us
    unnamed x14, local copies, waits for them, and re-layouts  3.21 us
    pallas_call x1, Pallas kernels, features_of(): pl.pallas_call(feature_kernel, in_specs=[SMEM, SMEM, VMEM, VMEM, VMEM], o...  2.7 us
    pallas_call x2, Pallas kernels, project(): pl.pallas_call(project_flipped_kernel if flipped else project_kernel, in_...  2.41 us
  transfers between devices with their start and end apart: 20, of which 10 were waited for; matrix products, arithmetic and copies ran while one was open for 4% of the time, Pallas kernels for 3%

profile of v5, /device:TPU:0, one launch (start us, length us, event | category | flops | bytes accessed | tf_op | source)
XLA Modules:
  0.0 63.4 jit_solution(10952879516900864124)
XLA Ops:
  0.6 2.0 %copy-done.2 = bf16[1792,1024]{1,0:T(8,128)(2,1)S(1)} copy-done((bf16[1792,1024]{1,0:T(8,128)(2,1)S(1)}, bf16[1792,1024]{1,0:T(8,128)(2,1)}, u32[]{:S(2)}) %copy-start.2) | copy-done | bytes 3670040
  2.7 0.9 %copy-done.3 = bf16[1024,64]{0,1:T(8,128)(2,1)S(1)} copy-done((bf16[1024,64]{0,1:T(8,128)(2,1)S(1)}, bf16[1024,64]{0,1:T(8,128)(2,1)}, u32[]{:S(2)}) %copy-start.3) | copy-done | bytes 131096
  3.6 1.2 %project.2 = f32[64,1792]{1,0:T(8,128)S(1)} custom-call(bf16[1792,1024]{1,0:T(8,128)(2,1)S(1)} %copy-done.2, bf16[64,1024]{1,0:T(8,128)(2,1)S(1)} %bitcast.47), custom_call_target="tpu_custom_call" | custom-call | flops 4697620480 | bytes 3670016 | tf_op jit(solution)/shard_map/project/pallas_call | solution.py:37
  4.9 0.5 collective-permute-start
  5.4 0.2 copy-done
  5.6 1.2 %project.3 = f32[128,1792]{1,0:T(8,128)S(1)} custom-call(bf16[1792,1024]{1,0:T(8,128)(2,1)S(1)} %copy-done, bf16[1024,128]{1,0:T(8,128)(2,1)S(1)} %copy-done.1), custom_call_target="tpu_custom_call" | custom-call | flops 469762048 | bytes 3670016 | tf_op jit(solution)/shard_map/project/pallas_call | solution.py:37
  6.9 0.5 collective-permute-start.2
  7.4 0.1 copy.10
  7.5 0.1 reduce-window.9
  7.6 0.1 reduce.end_ref
  7.7 0.1 abs_reduce_fusion
  7.9 0.1 round-nearest-even_convert_fusion
  8.0 0.1 broadcast_in_dim.10
  8.1 2.6 %collective-permute-start.1 = (s16[32,1920]{1,0:T(8,128)(2,1)S(1)}, s16[32,1920]{1,0:T(8,128)(2,1)S(1)}, u32[]{:S(2)}, u32[]{:S(2)}) collective-permute-start(s16[32,1920]{1,0:T(8,128)(2,1)S(1)} %pad_add_fusion), channel_id=1, source_target_pairs={{0,2},{2,0},{1,3},{3,1},{4,6},{6,4},{5,7},{7,5},{8,10},{10,8},{9,1... | collective-permute-start | bytes 368648 | tf_op jit(solution)/shard_map/ppermute | solution.py:199
  10.7 0.1 bitcast_add_fusion
  10.7 0.1 fusion.2
  10.9 0.1 fusion.4
  11.1 1.1 %collective-permute-start.4 = (s16[32,1920]{1,0:T(8,128)(2,1)S(1)}, s16[32,1920]{1,0:T(8,128)(2,1)S(1)}, u32[]{:S(2)}, u32[]{:S(2)}) collective-permute-start(s16[32,1920]{1,0:T(8,128)(2,1)S(1)} %pad_add_fusion.1), channel_id=1, source_target_pairs={{0,2},{2,0},{1,3},{3,1},{4,6},{6,4},{5,7},{7,5},{8,10},{10,8},{9,1... | collective-permute-start | bytes 368648 | tf_op jit(solution)/shard_map/ppermute | solution.py:199
  12.2 2.6 %collective-permute-done.1 = s16[32,1920]{1,0:T(8,128)(2,1)S(1)} collective-permute-done((s16[32,1920]{1,0:T(8,128)(2,1)S(1)}, s16[32,1920]{1,0:T(8,128)(2,1)S(1)}, u32[]{:S(2)}, u32[]{:S(2)}) %collective-permute-start.1) | collective-permute-done | bytes 122912 | tf_op jit(solution)/shard_map/ppermute | solution.py:199
  14.9 0.1 fusion.10
  15.0 0.1 fusion.1
  15.2 2.1 %collective-permute-done.4 = s16[32,1920]{1,0:T(8,128)(2,1)S(1)} collective-permute-done((s16[32,1920]{1,0:T(8,128)(2,1)S(1)}, s16[32,1920]{1,0:T(8,128)(2,1)S(1)}, u32[]{:S(2)}, u32[]{:S(2)}) %collective-permute-start.4) | collective-permute-done | bytes 122912 | tf_op jit(solution)/shard_map/ppermute | solution.py:199
  17.3 0.1 fusion.7
  17.4 0.1 fusion.v_ref
  17.7 2.7 %features.1 = bf16[56,2048]{1,0:T(8,128)(2,1)S(1)} custom-call(s32[56]{0:T(128)S(1)} %bitcast_subtract_fusion.start_ref, s32[56]{0:T(128)S(1)} %reduce.end_ref, f32[64,1792]{1,0:T(8,128)S(1)} %pad_maximum_fusion.2.u_ref, f32[32,1792]{1,0:T(8,128)S(1)} %fusion.v_ref, f32[56,128]{1,0:T(8,128)S(1)} %broadcast_in_dim.12.scale_ref), custom_call_target="tpu_custom_call" | custom-call | tf_op jit(solution)/shard_map/features/pallas_call | solution.py:115
  20.5 1.9 %collective-permute-start.5 = (bf16[56,2048]{1,0:T(8,128)(2,1)S(1)}, bf16[56,2048]{1,0:T(8,128)(2,1)S(1)}, u32[]{:S(2)}, u32[]{:S(2)}) collective-permute-start(bf16[56,2048]{1,0:T(8,128)(2,1)S(1)} %features.1), channel_id=1, source_target_pairs={{0,4},{4,12},{12,8},{8,0},{1,5},{5,13},{13,9},{9,1},{2,6},{6,14},{... | collective-permute-start | bytes 688136 | tf_op jit(solution)/shard_map/ppermute | solution.py:254
  22.4 1.6 %collective-permute-start.7 = (bf16[56,1024]{1,0:T(8,128)(2,1)S(1)}, bf16[56,1024]{1,0:T(8,128)(2,1)S(1)}, u32[]{:S(2)}, u32[]{:S(2)}) collective-permute-start(bf16[56,1024]{1,0:T(8,128)(2,1)S(1)} %slice_select_fusion.4), channel_id=1, source_target_pairs={{0,2},{2,0},{1,3},{3,1},{4,6},{6,4},{5,7},{7,5},{8,10},{10,8},{9,1... | collective-permute-start | bytes 344072 | tf_op jit(solution)/shard_map/ppermute | solution.py:199
  24.0 5.6 %collective-permute-done.5 = bf16[56,2048]{1,0:T(8,128)(2,1)S(1)} collective-permute-done((bf16[56,2048]{1,0:T(8,128)(2,1)S(1)}, bf16[56,2048]{1,0:T(8,128)(2,1)S(1)}, u32[]{:S(2)}, u32[]{:S(2)}) %collective-permute-start.5) | collective-permute-done | bytes 229408 | tf_op jit(solution)/shard_map/ppermute | solution.py:254
  29.6 0.9 %collective-permute-start.8 = (bf16[56,2048]{1,0:T(8,128)(2,1)S(1)}, bf16[56,2048]{1,0:T(8,128)(2,1)S(1)}, u32[]{:S(2)}, u32[]{:S(2)}) collective-permute-start(bf16[56,2048]{1,0:T(8,128)(2,1)S(1)} %collective-permute-done.5), channel_id=1, source_target_pairs={{0,4},{4,12},{12,8},{8,0},{1,5},{5,13},{13,9},{9,1},{2,6},{6,14},{... | collective-permute-start | bytes 688136 | tf_op jit(solution)/shard_map/ppermute | solution.py:254
  30.4 0.6 collective-permute-done.9
  31.1 1.6 %collective-permute-start.10 = (bf16[56,1024]{1,0:T(8,128)(2,1)S(1)}, bf16[56,1024]{1,0:T(8,128)(2,1)S(1)}, u32[]{:S(2)}, u32[]{:S(2)}) collective-permute-start(bf16[56,1024]{1,0:T(8,128)(2,1)S(1)} %slice_select_fusion.3), channel_id=1, source_target_pairs={{0,2},{2,0},{1,3},{3,1},{4,6},{6,4},{5,7},{7,5},{8,10},{10,8},{9,1... | collective-permute-start | bytes 344072 | tf_op jit(solution)/shard_map/ppermute | solution.py:199
  32.8 5.7 %collective-permute-done.8 = bf16[56,2048]{1,0:T(8,128)(2,1)S(1)} collective-permute-done((bf16[56,2048]{1,0:T(8,128)(2,1)S(1)}, bf16[56,2048]{1,0:T(8,128)(2,1)S(1)}, u32[]{:S(2)}, u32[]{:S(2)}) %collective-permute-start.8) | collective-permute-done | bytes 229408 | tf_op jit(solution)/shard_map/ppermute | solution.py:254
  38.5 0.1 copy.13.ids_ref
  38.7 0.9 %collective-permute-start.11 = (bf16[56,2048]{1,0:T(8,128)(2,1)S(1)}, bf16[56,2048]{1,0:T(8,128)(2,1)S(1)}, u32[]{:S(2)}, u32[]{:S(2)}) collective-permute-start(bf16[56,2048]{1,0:T(8,128)(2,1)S(1)} %collective-permute-done.8), channel_id=1, source_target_pairs={{0,4},{4,12},{12,8},{8,0},{1,5},{5,13},{13,9},{9,1},{2,6},{6,14},{... | collective-permute-start | bytes 688136 | tf_op jit(solution)/shard_map/ppermute | solution.py:254
  39.6 0.4 collective-permute-done.12
  40.1 1.6 %collective-permute-start.13 = (bf16[56,1024]{1,0:T(8,128)(2,1)S(1)}, bf16[56,1024]{1,0:T(8,128)(2,1)S(1)}, u32[]{:S(2)}, u32[]{:S(2)}) collective-permute-start(bf16[56,1024]{1,0:T(8,128)(2,1)S(1)} %slice_select_fusion.2), channel_id=1, source_target_pairs={{0,2},{2,0},{1,3},{3,1},{4,6},{6,4},{5,7},{7,5},{8,10},{10,8},{9,1... | collective-permute-start | bytes 344072 | tf_op jit(solution)/shard_map/ppermute | solution.py:199
  41.7 5.9 %collective-permute-done.11 = bf16[56,2048]{1,0:T(8,128)(2,1)S(1)} collective-permute-done((bf16[56,2048]{1,0:T(8,128)(2,1)S(1)}, bf16[56,2048]{1,0:T(8,128)(2,1)S(1)}, u32[]{:S(2)}, u32[]{:S(2)}) %collective-permute-start.11) | collective-permute-done | bytes 229408 | tf_op jit(solution)/shard_map/ppermute | solution.py:254
  47.6 0.2 multiply_reduce_fusion
  47.9 0.6 collective-permute-start.14
  48.5 0.6 %partial_scores.1 = f32[224,64]{1,0:T(8,128)S(1)} custom-call(s32[64,1]{1,0:T(8,128)S(1)} %copy.13.ids_ref, bf16[224,2048]{1,0:T(8,128)(2,1)S(1)} %get-tuple-element.25.all_ref.row_ref, f32[1,2048]{1,0:T(1,128)S(1)} %bitcast.46), custom_call_target="tpu_custom_call" | custom-call | flops 234881024 | bytes 917504 | tf_op jit(solution)/shard_map/partial_scores/pallas_call | solution.py:147
  49.2 0.2 collective-permute-done.15
  49.5 0.2 collective-permute-start.18
  49.7 1.6 %collective-permute-start.16 = (bf16[56,1024]{1,0:T(8,128)(2,1)S(1)}, bf16[56,1024]{1,0:T(8,128)(2,1)S(1)}, u32[]{:S(2)}, u32[]{:S(2)}) collective-permute-start(bf16[56,1024]{1,0:T(8,128)(2,1)S(1)} %slice_select_fusion.5), channel_id=1, source_target_pairs={{0,2},{2,0},{1,3},{3,1},{4,6},{6,4},{5,7},{7,5},{8,10},{10,8},{9,1... | collective-permute-start | bytes 344072 | tf_op jit(solution)/shard_map/ppermute | solution.py:199
  51.4 1.1 %collective-permute-start.19 = (f32[56,64]{1,0:T(8,128)S(1)}, f32[56,64]{1,0:T(8,128)S(1)}, u32[]{:S(2)}, u32[]{:S(2)}) collective-permute-start(f32[56,64]{1,0:T(8,128)S(1)} %get-tuple-element.38), channel_id=1, source_target_pairs={{0,2},{2,0},{1,3},{3,1},{4,6},{6,4},{5,7},{7,5},{8,10},{10,8},{9,1... | collective-permute-start | bytes 43016 | tf_op jit(solution)/shard_map/ppermute | solution.py:199
  52.4 3.1 %collective-permute-done.16 = bf16[56,1024]{1,0:T(8,128)(2,1)S(1)} collective-permute-done((bf16[56,1024]{1,0:T(8,128)(2,1)S(1)}, bf16[56,1024]{1,0:T(8,128)(2,1)S(1)}, u32[]{:S(2)}, u32[]{:S(2)}) %collective-permute-start.16) | collective-permute-done | bytes 114720 | tf_op jit(solution)/shard_map/ppermute | solution.py:199
  55.6 0.2 maximum_select_fusion
  55.8 1.0 %collective-permute-done.17 = bf16[56,1024]{1,0:T(8,128)(2,1)S(1)} collective-permute-done((bf16[56,1024]{1,0:T(8,128)(2,1)S(1)}, bf16[56,1024]{1,0:T(8,128)(2,1)S(1)}, u32[]{:S(2)}, u32[]{:S(2)}) %collective-permute-start.17) | collective-permute-done | bytes 114720 | tf_op jit(solution)/shard_map/ppermute | solution.py:199
  57.0 6.4 %covariance.1 = (f32[2048,2048]{1,0:T(8,128)}, f32[56,64]{1,0:T(8,128)}) custom-call(bf16[224,2048]{1,0:T(8,128)(2,1)S(1)} %get-tuple-element.25.all_ref.row_ref, bf16[224,2048]{1,0:T(8,128)(2,1)S(1)} %pad_maximum_fusion.1.col_ref, f32[56,64]{1,0:T(8,128)S(1)} %get-tuple-element.39.one_ref, f32[56,64]{1,0:T(8,128)S(1)} %collective-permute-done.19.two_ref), custom_call_target="tpu_custom_call" | custom-call | flops 1879048192 | bytes 16777216 | tf_op jit(solution)/shard_map/covariance/pallas_call | solution.py:182
  (60 shorter events, 1.2 us)
Async XLA Ops:
  0.6 2.0 %copy-start.2 = (bf16[1792,1024]{1,0:T(8,128)(2,1)S(1)}, bf16[1792,1024]{1,0:T(8,128)(2,1)}, u32[]{:S(2)}) copy-start(bf16[1792,1024]{1,0:T(8,128)(2,1)} %x_ref.2) | copy-start | bytes 11010052
  2.7 0.9 %copy-start.3 = (bf16[1024,64]{0,1:T(8,128)(2,1)S(1)}, bf16[1024,64]{0,1:T(8,128)(2,1)}, u32[]{:S(2)}) copy-start(bf16[1024,64]{0,1:T(8,128)(2,1)} %param.8) | copy-start | bytes 393220
  3.6 2.0 %copy-start = (bf16[1792,1024]{1,0:T(8,128)(2,1)S(1)}, bf16[1792,1024]{1,0:T(8,128)(2,1)}, u32[]{:S(2)}) copy-start(bf16[1792,1024]{1,0:T(8,128)(2,1)} %x_ref.3) | copy-start | bytes 11010052
  3.6 2.1 %copy-start.1 = (bf16[1024,128]{1,0:T(8,128)(2,1)S(1)}, bf16[1024,128]{1,0:T(8,128)(2,1)}, u32[]{:S(2)}) copy-start(bf16[1024,128]{1,0:T(8,128)(2,1)} %weight_ref.1) | copy-start | bytes 786436
  4.9 2.5 %copy-start.4 = (s32[1,56]{1,0:T(1,128)S(1)}, s32[1,56]{1,0:T(1,128)}, u32[]{:S(2)}) copy-start(s32[1,56]{1,0:T(1,128)} %param.10) | copy-start | bytes 676
  4.9 2.8 %collective-permute-start = (f32[32,1792]{1,0:T(8,128)S(1)}, f32[32,1792]{1,0:T(8,128)S(1)}, u32[]{:S(2)}, u32[]{:S(2)}) collective-permute-start(f32[32,1792]{1,0:T(8,128)S(1)} %slice_select_fusion.1), channel_id=1, source_target_pairs={{0,1},{1,0},{2,3},{3,2},{4,5},{5,4},{6,7},{7,6},{8,9},{9,8},{10,11... | collective-permute-start | bytes 688136 | tf_op jit(solution)/shard_map/ppermute | solution.py:199
  6.9 3.8 %collective-permute-start.2 = (f32[2,32,1792]{2,1,0:T(8,128)S(1)}, f32[2,32,1792]{2,1,0:T(8,128)S(1)}, u32[]{:S(2)}, u32[]{:S(2)}) collective-permute-start(f32[2,32,1792]{2,1,0:T(8,128)S(1)} %select_bitcast_fusion), channel_id=1, source_target_pairs={{0,1},{1,0},{2,3},{3,2},{4,5},{5,4},{6,7},{7,6},{8,9},{9,8},{10,11... | collective-permute-start | bytes 1376264 | tf_op jit(solution)/shard_map/ppermute | solution.py:199
  8.1 6.8 %collective-permute-start.1 = (s16[32,1920]{1,0:T(8,128)(2,1)S(1)}, s16[32,1920]{1,0:T(8,128)(2,1)S(1)}, u32[]{:S(2)}, u32[]{:S(2)}) collective-permute-start(s16[32,1920]{1,0:T(8,128)(2,1)S(1)} %pad_add_fusion), channel_id=1, source_target_pairs={{0,2},{2,0},{1,3},{3,1},{4,6},{6,4},{5,7},{7,5},{8,10},{10,8},{9,1... | collective-permute-start | bytes 368648 | tf_op jit(solution)/shard_map/ppermute | solution.py:199
  11.1 6.2 %collective-permute-start.4 = (s16[32,1920]{1,0:T(8,128)(2,1)S(1)}, s16[32,1920]{1,0:T(8,128)(2,1)S(1)}, u32[]{:S(2)}, u32[]{:S(2)}) collective-permute-start(s16[32,1920]{1,0:T(8,128)(2,1)S(1)} %pad_add_fusion.1), channel_id=1, source_target_pairs={{0,2},{2,0},{1,3},{3,1},{4,6},{6,4},{5,7},{7,5},{8,10},{10,8},{9,1... | collective-permute-start | bytes 368648 | tf_op jit(solution)/shard_map/ppermute | solution.py:199
  15.1 2.4 %collective-permute-start.3 = (f32[32,1792]{1,0:T(8,128)S(1)}, f32[32,1792]{1,0:T(8,128)S(1)}, u32[]{:S(2)}, u32[]{:S(2)}) collective-permute-start(f32[32,1792]{1,0:T(8,128)S(1)} %fusion.1), channel_id=1, source_target_pairs={{0,1},{1,0},{2,3},{3,2},{4,5},{5,4},{6,7},{7,6},{8,9},{9,8},{10,11... | collective-permute-start | bytes 688136 | tf_op jit(solution)/shard_map/ppermute | solution.py:199
  17.6 20.9 %copy-start.5 = (s32[64]{0:T(128)S(1)}, s32[64]{0:T(128)}, u32[]{:S(2)}) copy-start(s32[64]{0:T(128)} %param.11) | copy-start | bytes 772
  20.4 2.0 %collective-permute-start.6 = (bf16[56,2048]{1,0:T(8,128)(2,1)S(1)}, bf16[56,2048]{1,0:T(8,128)(2,1)S(1)}, u32[]{:S(2)}, u32[]{:S(2)}) collective-permute-start(bf16[56,2048]{1,0:T(8,128)(2,1)S(1)} %features.1), channel_id=1, source_target_pairs={{0,1},{1,0},{2,3},{3,2},{4,5},{5,4},{6,7},{7,6},{8,9},{9,8},{10,11... | collective-permute-start | bytes 688136 | tf_op jit(solution)/shard_map/ppermute | solution.py:199
  20.5 9.1 %collective-permute-start.5 = (bf16[56,2048]{1,0:T(8,128)(2,1)S(1)}, bf16[56,2048]{1,0:T(8,128)(2,1)S(1)}, u32[]{:S(2)}, u32[]{:S(2)}) collective-permute-start(bf16[56,2048]{1,0:T(8,128)(2,1)S(1)} %features.1), channel_id=1, source_target_pairs={{0,4},{4,12},{12,8},{8,0},{1,5},{5,13},{13,9},{9,1},{2,6},{6,14},{... | collective-permute-start | bytes 688136 | tf_op jit(solution)/shard_map/ppermute | solution.py:254
  22.4 7.2 %collective-permute-start.7 = (bf16[56,1024]{1,0:T(8,128)(2,1)S(1)}, bf16[56,1024]{1,0:T(8,128)(2,1)S(1)}, u32[]{:S(2)}, u32[]{:S(2)}) collective-permute-start(bf16[56,1024]{1,0:T(8,128)(2,1)S(1)} %slice_select_fusion.4), channel_id=1, source_target_pairs={{0,2},{2,0},{1,3},{3,1},{4,6},{6,4},{5,7},{7,5},{8,10},{10,8},{9,1... | collective-permute-start | bytes 344072 | tf_op jit(solution)/shard_map/ppermute | solution.py:199
  29.6 1.5 %collective-permute-start.9 = (bf16[56,2048]{1,0:T(8,128)(2,1)S(1)}, bf16[56,2048]{1,0:T(8,128)(2,1)S(1)}, u32[]{:S(2)}, u32[]{:S(2)}) collective-permute-start(bf16[56,2048]{1,0:T(8,128)(2,1)S(1)} %collective-permute-done.5), channel_id=1, source_target_pairs={{0,1},{1,0},{2,3},{3,2},{4,5},{5,4},{6,7},{7,6},{8,9},{9,8},{10,11... | collective-permute-start | bytes 688136 | tf_op jit(solution)/shard_map/ppermute | solution.py:199
  29.6 8.9 %collective-permute-start.8 = (bf16[56,2048]{1,0:T(8,128)(2,1)S(1)}, bf16[56,2048]{1,0:T(8,128)(2,1)S(1)}, u32[]{:S(2)}, u32[]{:S(2)}) collective-permute-start(bf16[56,2048]{1,0:T(8,128)(2,1)S(1)} %collective-permute-done.5), channel_id=1, source_target_pairs={{0,4},{4,12},{12,8},{8,0},{1,5},{5,13},{13,9},{9,1},{2,6},{6,14},{... | collective-permute-start | bytes 688136 | tf_op jit(solution)/shard_map/ppermute | solution.py:254
  31.1 7.4 %collective-permute-start.10 = (bf16[56,1024]{1,0:T(8,128)(2,1)S(1)}, bf16[56,1024]{1,0:T(8,128)(2,1)S(1)}, u32[]{:S(2)}, u32[]{:S(2)}) collective-permute-start(bf16[56,1024]{1,0:T(8,128)(2,1)S(1)} %slice_select_fusion.3), channel_id=1, source_target_pairs={{0,2},{2,0},{1,3},{3,1},{4,6},{6,4},{5,7},{7,5},{8,10},{10,8},{9,1... | collective-permute-start | bytes 344072 | tf_op jit(solution)/shard_map/ppermute | solution.py:199
  38.5 1.5 %collective-permute-start.12 = (bf16[56,2048]{1,0:T(8,128)(2,1)S(1)}, bf16[56,2048]{1,0:T(8,128)(2,1)S(1)}, u32[]{:S(2)}, u32[]{:S(2)}) collective-permute-start(bf16[56,2048]{1,0:T(8,128)(2,1)S(1)} %collective-permute-done.8), channel_id=1, source_target_pairs={{0,1},{1,0},{2,3},{3,2},{4,5},{5,4},{6,7},{7,6},{8,9},{9,8},{10,11... | collective-permute-start | bytes 688136 | tf_op jit(solution)/shard_map/ppermute | solution.py:199
  38.7 9.0 %collective-permute-start.11 = (bf16[56,2048]{1,0:T(8,128)(2,1)S(1)}, bf16[56,2048]{1,0:T(8,128)(2,1)S(1)}, u32[]{:S(2)}, u32[]{:S(2)}) collective-permute-start(bf16[56,2048]{1,0:T(8,128)(2,1)S(1)} %collective-permute-done.8), channel_id=1, source_target_pairs={{0,4},{4,12},{12,8},{8,0},{1,5},{5,13},{13,9},{9,1},{2,6},{6,14},{... | collective-permute-start | bytes 688136 | tf_op jit(solution)/shard_map/ppermute | solution.py:254
  40.1 7.6 %collective-permute-start.13 = (bf16[56,1024]{1,0:T(8,128)(2,1)S(1)}, bf16[56,1024]{1,0:T(8,128)(2,1)S(1)}, u32[]{:S(2)}, u32[]{:S(2)}) collective-permute-start(bf16[56,1024]{1,0:T(8,128)(2,1)S(1)} %slice_select_fusion.2), channel_id=1, source_target_pairs={{0,2},{2,0},{1,3},{3,1},{4,6},{6,4},{5,7},{7,5},{8,10},{10,8},{9,1... | collective-permute-start | bytes 344072 | tf_op jit(solution)/shard_map/ppermute | solution.py:199
  47.8 1.6 %collective-permute-start.15 = (bf16[56,2048]{1,0:T(8,128)(2,1)S(1)}, bf16[56,2048]{1,0:T(8,128)(2,1)S(1)}, u32[]{:S(2)}, u32[]{:S(2)}) collective-permute-start(bf16[56,2048]{1,0:T(8,128)(2,1)S(1)} %collective-permute-done.11), channel_id=1, source_target_pairs={{0,1},{1,0},{2,3},{3,2},{4,5},{5,4},{6,7},{7,6},{8,9},{9,8},{10,11... | collective-permute-start | bytes 688136 | tf_op jit(solution)/shard_map/ppermute | solution.py:199
  47.9 7.6 %collective-permute-start.14 = (bf16[168,1024]{1,0:T(8,128)(2,1)S(1)}, bf16[168,1024]{1,0:T(8,128)(2,1)S(1)}, u32[]{:S(2)}, u32[]{:S(2)}) collective-permute-start(bf16[168,1024]{1,0:T(8,128)(2,1)S(1)} %constant_dynamic-update-slice_fusion), channel_id=1, source_target_pairs={{0,1},{1,0},{2,3},{3,2},{4,5},{5,4},{6,7},{7,6},{8,9},{9,8},{10,11... | collective-permute-start | bytes 1032200 | tf_op jit(solution)/shard_map/ppermute | solution.py:199
  49.5 1.9 %collective-permute-start.18 = (f32[2,56,64]{2,1,0:T(8,128)S(1)}, f32[2,56,64]{2,1,0:T(8,128)S(1)}, u32[]{:S(2)}, u32[]{:S(2)}) collective-permute-start(f32[2,56,64]{2,1,0:T(8,128)S(1)} %pad_maximum_fusion.3), channel_id=1, source_target_pairs={{0,1},{1,0},{2,3},{3,2},{4,5},{5,4},{6,7},{7,6},{8,9},{9,8},{10,11... | collective-permute-start | bytes 86024 | tf_op jit(solution)/shard_map/ppermute | solution.py:199
  49.7 5.8 %collective-permute-start.16 = (bf16[56,1024]{1,0:T(8,128)(2,1)S(1)}, bf16[56,1024]{1,0:T(8,128)(2,1)S(1)}, u32[]{:S(2)}, u32[]{:S(2)}) collective-permute-start(bf16[56,1024]{1,0:T(8,128)(2,1)S(1)} %slice_select_fusion.5), channel_id=1, source_target_pairs={{0,2},{2,0},{1,3},{3,1},{4,6},{6,4},{5,7},{7,5},{8,10},{10,8},{9,1... | collective-permute-start | bytes 344072 | tf_op jit(solution)/shard_map/ppermute | solution.py:199
  51.4 5.6 %collective-permute-start.19 = (f32[56,64]{1,0:T(8,128)S(1)}, f32[56,64]{1,0:T(8,128)S(1)}, u32[]{:S(2)}, u32[]{:S(2)}) collective-permute-start(f32[56,64]{1,0:T(8,128)S(1)} %get-tuple-element.38), channel_id=1, source_target_pairs={{0,2},{2,0},{1,3},{3,1},{4,6},{6,4},{5,7},{7,5},{8,10},{10,8},{9,1... | collective-permute-start | bytes 43016 | tf_op jit(solution)/shard_map/ppermute | solution.py:199
  55.5 1.3 %collective-permute-start.17 = (bf16[56,1024]{1,0:T(8,128)(2,1)S(1)}, bf16[56,1024]{1,0:T(8,128)(2,1)S(1)}, u32[]{:S(2)}, u32[]{:S(2)}) collective-permute-start(bf16[56,1024]{1,0:T(8,128)(2,1)S(1)} %collective-permute-done.16), channel_id=1, source_target_pairs={{0,1},{1,0},{2,3},{3,2},{4,5},{5,4},{6,7},{7,6},{8,9},{9,8},{10,11... | collective-permute-start | bytes 344072 | tf_op jit(solution)/shard_map/ppermute | solution.py:199

commit v6 on v5

--- a/solution.py
+++ b/solution.py
@@ -155,13 +155,11 @@
     )(ids[:, None], gathered, squares)
 
 
-def covariance_kernel(row_ref, col_ref, one_ref, two_ref, tile_hbm, score_hbm, tile_ref, score_ref, sem):
+def covariance_kernel(row_ref, col_ref, tile_hbm, tile_ref, sem):
     seqs = row_ref.shape[0]
-    steps = sem.shape[0] - 1
+    steps = sem.shape[0]
     tile = tile_ref.shape[0] // steps
-    score_ref[...] = one_ref[...] + two_ref[...]
-    copies = [pltpu.make_async_copy(score_ref, score_hbm, sem.at[steps])]
-    copies[0].start()
+    copies = []
     for i in range(steps):
         at = slice(i * tile, (i + 1) * tile)
         product = lax.dot_general(
@@ -175,24 +173,20 @@
         copy.wait()
 
 
-def covariance_of(gathered, other_cols, one, two):
+def covariance_of(gathered, other_cols):
     seqs, rows = gathered.shape
     cols = other_cols.shape[1]
     steps = rows // 256
     return pl.pallas_call(
         covariance_kernel,
-        in_specs=[VMEM] * 4,
-        out_specs=[pl.BlockSpec(memory_space=pltpu.HBM)] * 2,
-        out_shape=[jax.ShapeDtypeStruct((rows, cols), F32), jax.ShapeDtypeStruct(one.shape, F32)],
-        scratch_shapes=[
-            pltpu.VMEM((rows, cols), F32),
-            pltpu.VMEM(one.shape, F32),
-            pltpu.SemaphoreType.DMA((steps + 1,)),
-        ],
+        in_specs=[VMEM, VMEM],
+        out_specs=pl.BlockSpec(memory_space=pltpu.HBM),
+        out_shape=jax.ShapeDtypeStruct((rows, cols), F32),
+        scratch_shapes=[pltpu.VMEM((rows, cols), F32), pltpu.SemaphoreType.DMA((steps,))],
         compiler_params=params(32),
         cost_estimate=pl.CostEstimate(flops=2 * seqs * rows * cols, bytes_accessed=4 * rows * cols, transcendentals=0),
         name="covariance",
-    )(gathered, other_cols, one, two)
+    )(gathered, other_cols)
 
 
 def both_ways(x, axis):
@@ -254,6 +248,10 @@
     return lax.ppermute(part, "dp", [(RING[i], RING[(i + 1) % 4]) for i in range(4)])
 
 
+def against(part):
+    return lax.ppermute(part, "dp", [(RING[(i + 1) % 4], RING[i]) for i in range(4)])
+
+
 def on_owner_chip():
     return (lax.axis_index(WIDE) ^ lax.axis_index("dp")) < 2
 
@@ -262,10 +260,9 @@
     return jnp.where(lax.axis_index(WIDE) == lax.axis_index("dp"), part, other)
 
 
-def sent_across(part):
+def half_of(part):
     size = part.shape[1] // 2
-    half = picked(lax.axis_index("sub"), part[:, :size], part[:, size:])
-    return both_ways(half, "feat")
+    return picked(lax.axis_index("sub"), part[:, :size], part[:, size:])
 
 
 def spread(part, mine, other):
@@ -308,15 +305,33 @@
     me = lax.axis_index(WIDE)
     at = lax.axis_index("dp")
     if is_square():
-        chunks, owns, overs = [local_feat], [], []
-        for k in range(3):
-            chunks.append(around(chunks[k]))
-            owns.append(owned(chunks[k], both_ways(chunks[k], "sub")))
-            overs.append(sent_across(owns[k]))
-            chunks[k + 1], overs[k] = lax.optimization_barrier((chunks[k + 1], overs[k]))
-        last = owned(chunks[3], both_ways(chunks[3], "sub"))
-        early_over = jnp.concatenate(overs)
-        early_other = both_ways(early_over, "sub")
+        before = ring_place((ring_place(at) - 1) & 3)
+        swapped = both_ways(local_feat, "sub")
+        owns = [owned(local_feat, swapped)]
+        overs = jnp.concatenate([half_of(owns[0]), half_of(jnp.where(me == before, local_feat, swapped))], axis=1)
+        chunks = [local_feat, around(local_feat)]
+        chunks[1], overs = lax.optimization_barrier((chunks[1], both_ways(overs, "feat")))
+        width = overs.shape[1] // 2
+        overs = [overs[:, :width], overs[:, width:]]
+        chunks.append(around(chunks[1]))
+        owns.append(owned(chunks[1], both_ways(chunks[1], "sub")))
+        over = both_ways(half_of(owns[1]), "feat")
+        back = against(overs[1])
+        chunks[2], over = lax.optimization_barrier((chunks[2], over))
+        early_over = jnp.concatenate([overs[0], over, back])
+        chunks.append(around(chunks[2]))
+        owns.append(owned(chunks[2], both_ways(chunks[2], "sub")))
+        over = both_ways(half_of(owns[2]), "feat")
+        chunks[3], over, early_other = lax.optimization_barrier((chunks[3], over, both_ways(early_over, "sub")))
+        owns.append(owned(chunks[3], both_ways(chunks[3], "sub")))
+        pair = 2 * local_feat.shape[0]
+        other_cols = jnp.concatenate(
+            [
+                spread(jnp.concatenate(owns[:2]), early_over[:pair], early_other[:pair]),
+                spread(owns[2], over, both_ways(over, "sub")),
+                spread(owns[3], early_over[pair:], early_other[pair:]),
+            ]
+        )
         gathered = jnp.concatenate(chunks)
         squares = summed_squares(gathered)
         seqs = local_feat.shape[0]
@@ -327,22 +342,19 @@
         ids = target_ids
         squares = summed_squares(gathered)
     part = partial_scores_of(ids, gathered, squares) / jnp.sqrt(jnp.float32(gathered.shape[1] * group))
-    if is_square():
-        last, part = lax.optimization_barrier((last, part))
-        last_over = sent_across(last)
     own = part.shape[0] // group
     if is_square():
         places = [(ring_place(at) - ring_place(me ^ k)) & 3 for k in range(4)]
         pieces = part.reshape(group, own, -1)
         pieces = [lax.dynamic_index_in_dim(pieces, place, 0, keepdims=False) for place in places]
         summed = jnp.stack([pieces[0], pieces[2]]) + both_ways(jnp.stack([pieces[1], pieces[3]]), "sub")
-        last_other = both_ways(last_over, "sub")
-        early = spread(jnp.concatenate(owns), early_over, early_other)
-        other_cols = jnp.concatenate([early, spread(last, last_over, last_other)])
-        mine, given = summed[0], both_ways(summed[1], "feat")
+        given = both_ways(summed[1], "feat")
+        tile = covariance_of(gathered, other_cols)
+        mine, given, tile = lax.optimization_barrier((summed[0], given, tile))
+        total = mine + given
     else:
-        mine, given = lax.psum_scatter(part, WIDE, scatter_dimension=0, tiled=True), jnp.zeros((own, ids.shape[0]), F32)
-    tile, total = covariance_of(gathered, other_cols, mine, given)
+        total = lax.psum_scatter(part, WIDE, scatter_dimension=0, tiled=True)
+        tile = covariance_of(gathered, other_cols)
     return (tile, jnp.transpose(total))
 
 

time: 63.6 us -> 61.1 us (0.961)
  waiting for transfers between devices: 27.4 us -> 22 us
  starting transfers between devices: 16.8 us -> 18.9 us
  other arithmetic: 2.36 us -> 3.09 us
    ppermute x3, waiting for transfers between devices: 17.3 us -> 13.7 us  [around(): lax.ppermute(part, 'dp', [(RING[i], RING[(i + 1) % 4]) for i in range(4)])]
    ppermute x3, starting transfers between devices: 3.64 us -> 6.44 us  [around(): lax.ppermute(part, 'dp', [(RING[i], RING[(i + 1) % 4]) for i in range(4)])]
    ppermute x17 -> x16, waiting for transfers between devices: 10.1 us -> 7.94 us  [both_ways(): return lax.ppermute(x, axis, [(0, 1), (1, 0)])]
    ppermute x17 -> x16, starting transfers between devices: 13.2 us -> 11.1 us  [both_ways(): return lax.ppermute(x, axis, [(0, 1), (1, 0)])]
    ppermute x0 -> x1, starting transfers between devices: none -> 1.33 us  [against(): lax.ppermute(part, 'dp', [(RING[(i + 1) % 4], RING[i]) for i in range(4)])]
    unnamed x14 -> x12, local copies, waits for them, and re-layouts: 3.21 us -> 3.29 us
  transfers between devices with their start and end apart: 20 -> 20, of which waited for: 10 -> 9; matrix products, arithmetic and copies ran while one was open for 4% -> 5% of each run, Pallas kernels for 3% -> 14%
where the time goes in v6:
time: 61.1 us; the launch traced here: 60.9 us
  waiting for transfers between devices  22 us (36%)
  starting transfers between devices  18.9 us (31%)
  Pallas kernels  12.2 us (20%)
  local copies, waits for them, and re-layouts  3.74 us (6%)
  other arithmetic  3.09 us (5%)
  between operations  0.99 us (2%)
    ppermute x3, waiting for transfers between devices, around(): lax.ppermute(part, 'dp', [(RING[i], RING[(i + 1) % 4]) for i in range(4)])  13.7 us
    ppermute x16, starting transfers between devices, both_ways(): return lax.ppermute(x, axis, [(0, 1), (1, 0)])  11.1 us
    ppermute x16, waiting for transfers between devices, both_ways(): return lax.ppermute(x, axis, [(0, 1), (1, 0)])  7.94 us
    ppermute x3, starting transfers between devices, around(): lax.ppermute(part, 'dp', [(RING[i], RING[(i + 1) % 4]) for i in range(4)])  6.44 us
    pallas_call x1, Pallas kernels, covariance_of(): pl.pallas_call(covariance_kernel, in_specs=[VMEM, VMEM], out_specs=pl.Blo...  6.39 us
    unnamed x12, local copies, waits for them, and re-layouts  3.29 us
    pallas_call x1, Pallas kernels, features_of(): pl.pallas_call(feature_kernel, in_specs=[SMEM, SMEM, VMEM, VMEM, VMEM], o...  2.71 us
    pallas_call x2, Pallas kernels, project(): pl.pallas_call(project_flipped_kernel if flipped else project_kernel, in_...  2.41 us
  transfers between devices with their start and end apart: 20, of which 9 were waited for; matrix products, arithmetic and copies ran while one was open for 5% of the time, Pallas kernels for 14%

profile of v6, /device:TPU:0, one launch (start us, length us, event | category | flops | bytes accessed | tf_op | source)
XLA Modules:
  0.0 60.9 jit_solution(3577089602113720)
XLA Ops:
  0.6 2.0 %copy-done = bf16[1792,1024]{1,0:T(8,128)(2,1)S(1)} copy-done((bf16[1792,1024]{1,0:T(8,128)(2,1)S(1)}, bf16[1792,1024]{1,0:T(8,128)(2,1)}, u32[]{:S(2)}) %copy-start) | copy-done | bytes 3670040
  2.7 0.9 %copy-done.1 = bf16[1024,128]{1,0:T(8,128)(2,1)S(1)} copy-done((bf16[1024,128]{1,0:T(8,128)(2,1)S(1)}, bf16[1024,128]{1,0:T(8,128)(2,1)}, u32[]{:S(2)}) %copy-start.1) | copy-done | bytes 262168
  3.6 1.2 %project.3 = f32[128,1792]{1,0:T(8,128)S(1)} custom-call(bf16[1792,1024]{1,0:T(8,128)(2,1)S(1)} %copy-done, bf16[1024,128]{1,0:T(8,128)(2,1)S(1)} %copy-done.1), custom_call_target="tpu_custom_call" | custom-call | flops 469762048 | bytes 3670016 | tf_op jit(solution)/shard_map/project/pallas_call | solution.py:37
  4.9 0.5 collective-permute-start.2
  5.4 0.3 copy-done.2
  5.7 1.2 %project.2 = f32[64,1792]{1,0:T(8,128)S(1)} custom-call(bf16[1792,1024]{1,0:T(8,128)(2,1)S(1)} %copy-done.2, bf16[64,1024]{1,0:T(8,128)(2,1)S(1)} %bitcast.48), custom_call_target="tpu_custom_call" | custom-call | flops 4697620480 | bytes 3670016 | tf_op jit(solution)/shard_map/project/pallas_call | solution.py:37
  6.9 0.5 collective-permute-start
  7.5 0.1 copy.10
  7.6 0.1 reduce-window.9
  7.7 0.1 reduce.end_ref
  7.8 0.8 %collective-permute-done = f32[32,1792]{1,0:T(8,128)S(1)} collective-permute-done((f32[32,1792]{1,0:T(8,128)S(1)}, f32[32,1792]{1,0:T(8,128)S(1)}, u32[]{:S(2)}, u32[]{:S(2)}) %collective-permute-start) | collective-permute-done | bytes 229408 | tf_op jit(solution)/shard_map/ppermute | solution.py:193
  8.6 0.1 abs_reduce_fusion
  8.7 0.1 round-nearest-even_convert_fusion
  9.0 2.9 %collective-permute-start.1 = (s16[32,1920]{1,0:T(8,128)(2,1)S(1)}, s16[32,1920]{1,0:T(8,128)(2,1)S(1)}, u32[]{:S(2)}, u32[]{:S(2)}) collective-permute-start(s16[32,1920]{1,0:T(8,128)(2,1)S(1)} %pad_add_fusion), channel_id=1, source_target_pairs={{0,2},{2,0},{1,3},{3,1},{4,6},{6,4},{5,7},{7,5},{8,10},{10,8},{9,1... | collective-permute-start | bytes 368648 | tf_op jit(solution)/shard_map/ppermute | solution.py:193
  12.0 0.1 fusion.2
  12.1 0.1 fusion.4
  12.3 0.1 collective-permute-start.4
  12.4 3.6 %collective-permute-done.1 = s16[32,1920]{1,0:T(8,128)(2,1)S(1)} collective-permute-done((s16[32,1920]{1,0:T(8,128)(2,1)S(1)}, s16[32,1920]{1,0:T(8,128)(2,1)S(1)}, u32[]{:S(2)}, u32[]{:S(2)}) %collective-permute-start.1) | collective-permute-done | bytes 122912 | tf_op jit(solution)/shard_map/ppermute | solution.py:193
  16.0 0.1 fusion.10
  16.1 0.1 fusion.1
  16.3 1.8 %collective-permute-done.4 = s16[32,1920]{1,0:T(8,128)(2,1)S(1)} collective-permute-done((s16[32,1920]{1,0:T(8,128)(2,1)S(1)}, s16[32,1920]{1,0:T(8,128)(2,1)S(1)}, u32[]{:S(2)}, u32[]{:S(2)}) %collective-permute-start.4) | collective-permute-done | bytes 122912 | tf_op jit(solution)/shard_map/ppermute | solution.py:193
  18.2 0.1 fusion.7
  18.3 0.1 fusion.v_ref
  18.6 2.7 %features.1 = bf16[56,2048]{1,0:T(8,128)(2,1)S(1)} custom-call(s32[56]{0:T(128)S(1)} %bitcast_subtract_fusion.start_ref, s32[56]{0:T(128)S(1)} %reduce.end_ref, f32[64,1792]{1,0:T(8,128)S(1)} %pad_maximum_fusion.2.u_ref, f32[32,1792]{1,0:T(8,128)S(1)} %fusion.v_ref, f32[56,128]{1,0:T(8,128)S(1)} %broadcast_in_dim.13.scale_ref), custom_call_target="tpu_custom_call" | custom-call | tf_op jit(solution)/shard_map/features/pallas_call | solution.py:115
  21.4 1.9 %collective-permute-start.5 = (bf16[56,2048]{1,0:T(8,128)(2,1)S(1)}, bf16[56,2048]{1,0:T(8,128)(2,1)S(1)}, u32[]{:S(2)}, u32[]{:S(2)}) collective-permute-start(bf16[56,2048]{1,0:T(8,128)(2,1)S(1)} %features.1), channel_id=1, source_target_pairs={{0,4},{4,12},{12,8},{8,0},{1,5},{5,13},{13,9},{9,1},{2,6},{6,14},{... | collective-permute-start | bytes 688136 | tf_op jit(solution)/shard_map/ppermute | solution.py:248
  23.4 1.6 %collective-permute-start.7 = (bf16[56,2048]{1,0:T(8,128)(2,1)S(1)}, bf16[56,2048]{1,0:T(8,128)(2,1)S(1)}, u32[]{:S(2)}, u32[]{:S(2)}) collective-permute-start(bf16[56,2048]{1,0:T(8,128)(2,1)S(1)} %pad_maximum_fusion.4), channel_id=1, source_target_pairs={{0,2},{2,0},{1,3},{3,1},{4,6},{6,4},{5,7},{7,5},{8,10},{10,8},{9,1... | collective-permute-start | bytes 688136 | tf_op jit(solution)/shard_map/ppermute | solution.py:193
  24.9 5.5 %collective-permute-done.5 = bf16[56,2048]{1,0:T(8,128)(2,1)S(1)} collective-permute-done((bf16[56,2048]{1,0:T(8,128)(2,1)S(1)}, bf16[56,2048]{1,0:T(8,128)(2,1)S(1)}, u32[]{:S(2)}, u32[]{:S(2)}) %collective-permute-start.5) | collective-permute-done | bytes 229408 | tf_op jit(solution)/shard_map/ppermute | solution.py:248
  30.4 0.6 %collective-permute-done.7 = bf16[56,2048]{1,0:T(8,128)(2,1)S(1)} collective-permute-done((bf16[56,2048]{1,0:T(8,128)(2,1)S(1)}, bf16[56,2048]{1,0:T(8,128)(2,1)S(1)}, u32[]{:S(2)}, u32[]{:S(2)}) %collective-permute-start.7) | collective-permute-done | bytes 229408 | tf_op jit(solution)/shard_map/ppermute | solution.py:193
  31.1 2.6 %collective-permute-start.8 = (bf16[56,2048]{1,0:T(8,128)(2,1)S(1)}, bf16[56,2048]{1,0:T(8,128)(2,1)S(1)}, u32[]{:S(2)}, u32[]{:S(2)}) collective-permute-start(bf16[56,2048]{1,0:T(8,128)(2,1)S(1)} %collective-permute-done.5), channel_id=1, source_target_pairs={{0,4},{4,12},{12,8},{8,0},{1,5},{5,13},{13,9},{9,1},{2,6},{6,14},{... | collective-permute-start | bytes 688136 | tf_op jit(solution)/shard_map/ppermute | solution.py:248
  33.7 1.6 %collective-permute-start.10 = (bf16[56,1024]{1,0:T(8,128)(2,1)S(1)}, bf16[56,1024]{1,0:T(8,128)(2,1)S(1)}, u32[]{:S(2)}, u32[]{:S(2)}) collective-permute-start(bf16[56,1024]{1,0:T(8,128)(2,1)S(1)} %slice_select_fusion.3), channel_id=1, source_target_pairs={{0,2},{2,0},{1,3},{3,1},{4,6},{6,4},{5,7},{7,5},{8,10},{10,8},{9,1... | collective-permute-start | bytes 344072 | tf_op jit(solution)/shard_map/ppermute | solution.py:193
  35.3 1.3 %collective-permute-start.14 = (bf16[56,1024]{1,0:T(8,128)(2,1)S(1)}, bf16[56,1024]{1,0:T(8,128)(2,1)S(1)}, u32[]{:S(2)}, u32[]{:S(2)}) collective-permute-start(bf16[56,1024]{1,0:T(8,128)(2,1)S(1)} %get-tuple-element.39), channel_id=1, source_target_pairs={{4,0},{12,4},{8,12},{0,8},{5,1},{13,5},{9,13},{1,9},{6,2},{14,6},{... | collective-permute-start | bytes 344072 | tf_op jit(solution)/shard_map/ppermute | solution.py:252
  36.7 3.5 %collective-permute-done.8 = bf16[56,2048]{1,0:T(8,128)(2,1)S(1)} collective-permute-done((bf16[56,2048]{1,0:T(8,128)(2,1)S(1)}, bf16[56,2048]{1,0:T(8,128)(2,1)S(1)}, u32[]{:S(2)}, u32[]{:S(2)}) %collective-permute-start.8) | collective-permute-done | bytes 229408 | tf_op jit(solution)/shard_map/ppermute | solution.py:248
  40.1 2.0 %collective-permute-start.11 = (bf16[56,2048]{1,0:T(8,128)(2,1)S(1)}, bf16[56,2048]{1,0:T(8,128)(2,1)S(1)}, u32[]{:S(2)}, u32[]{:S(2)}) collective-permute-start(bf16[56,2048]{1,0:T(8,128)(2,1)S(1)} %collective-permute-done.8), channel_id=1, source_target_pairs={{0,4},{4,12},{12,8},{8,0},{1,5},{5,13},{13,9},{9,1},{2,6},{6,14},{... | collective-permute-start | bytes 688136 | tf_op jit(solution)/shard_map/ppermute | solution.py:248
  42.1 0.4 collective-permute-done.14
  42.6 1.6 %collective-permute-start.13 = (bf16[56,1024]{1,0:T(8,128)(2,1)S(1)}, bf16[56,1024]{1,0:T(8,128)(2,1)S(1)}, u32[]{:S(2)}, u32[]{:S(2)}) collective-permute-start(bf16[56,1024]{1,0:T(8,128)(2,1)S(1)} %slice_select_fusion.2), channel_id=1, source_target_pairs={{0,2},{2,0},{1,3},{3,1},{4,6},{6,4},{5,7},{7,5},{8,10},{10,8},{9,1... | collective-permute-start | bytes 344072 | tf_op jit(solution)/shard_map/ppermute | solution.py:193
  44.2 0.1 copy.13.ids_ref
  44.3 4.7 %collective-permute-done.11 = bf16[56,2048]{1,0:T(8,128)(2,1)S(1)} collective-permute-done((bf16[56,2048]{1,0:T(8,128)(2,1)S(1)}, bf16[56,2048]{1,0:T(8,128)(2,1)S(1)}, u32[]{:S(2)}, u32[]{:S(2)}) %collective-permute-start.11) | collective-permute-done | bytes 229408 | tf_op jit(solution)/shard_map/ppermute | solution.py:248
  49.1 0.3 multiply_reduce_fusion
  49.3 0.1 broadcast_select_fusion.1
  49.4 0.6 collective-permute-start.18
  50.0 0.6 %partial_scores.1 = f32[224,64]{1,0:T(8,128)S(1)} custom-call(s32[64,1]{1,0:T(8,128)S(1)} %copy.13.ids_ref, bf16[224,2048]{1,0:T(8,128)(2,1)S(1)} %get-tuple-element.25.all_ref.row_ref, f32[1,2048]{1,0:T(1,128)S(1)} %bitcast.47), custom_call_target="tpu_custom_call" | custom-call | flops 234881024 | bytes 917504 | tf_op jit(solution)/shard_map/partial_scores/pallas_call | solution.py:147
  50.8 0.1 maximum_select_fusion
  50.9 1.1 %collective-permute-done.16 = f32[2,56,64]{2,1,0:T(8,128)S(1)} collective-permute-done((f32[2,56,64]{2,1,0:T(8,128)S(1)}, f32[2,56,64]{2,1,0:T(8,128)S(1)}, u32[]{:S(2)}, u32[]{:S(2)}) %collective-permute-start.16) | collective-permute-done | bytes 28704 | tf_op jit(solution)/shard_map/ppermute | solution.py:193
  52.0 1.6 %collective-permute-start.17 = (f32[56,64]{1,0:T(8,128)S(1)}, f32[56,64]{1,0:T(8,128)S(1)}, u32[]{:S(2)}, u32[]{:S(2)}) collective-permute-start(f32[56,64]{1,0:T(8,128)S(1)} %get-tuple-element.44), channel_id=1, source_target_pairs={{0,2},{2,0},{1,3},{3,1},{4,6},{6,4},{5,7},{7,5},{8,10},{10,8},{9,1... | collective-permute-start | bytes 43016 | tf_op jit(solution)/shard_map/ppermute | solution.py:193
  53.7 0.1 maximum_select_fusion.2
  53.8 0.1 pad_maximum_fusion.1.col_ref
  53.9 6.4 %covariance.1 = f32[2048,2048]{1,0:T(8,128)} custom-call(bf16[224,2048]{1,0:T(8,128)(2,1)S(1)} %get-tuple-element.25.all_ref.row_ref, bf16[224,2048]{1,0:T(8,128)(2,1)S(1)} %pad_maximum_fusion.1.col_ref), custom_call_target="tpu_custom_call" | custom-call | flops 1879048192 | bytes 16777216 | tf_op jit(solution)/shard_map/covariance/pallas_call | solution.py:180
  60.3 0.6 %add_bitcast_fusion = f32[64,56]{0,1:T(8,128)} fusion(f32[56,64]{1,0:T(8,128)S(1)} %get-tuple-element.22, f32[56,64]{1,0:T(8,128)S(1)} %collective-permute-done.17), kind=kLoop, calls=%fused_computation.51 | loop fusion | flops 3584 | bytes 43008 | tf_op jit(solution)/shard_map/transpose | solution.py:358
  (61 shorter events, 1.3 us)
Async XLA Ops:
  0.6 2.0 %copy-start = (bf16[1792,1024]{1,0:T(8,128)(2,1)S(1)}, bf16[1792,1024]{1,0:T(8,128)(2,1)}, u32[]{:S(2)}) copy-start(bf16[1792,1024]{1,0:T(8,128)(2,1)} %x_ref.3) | copy-start | bytes 11010052
  2.7 0.9 %copy-start.1 = (bf16[1024,128]{1,0:T(8,128)(2,1)S(1)}, bf16[1024,128]{1,0:T(8,128)(2,1)}, u32[]{:S(2)}) copy-start(bf16[1024,128]{1,0:T(8,128)(2,1)} %weight_ref.1) | copy-start | bytes 786436
  3.6 2.0 %copy-start.2 = (bf16[1792,1024]{1,0:T(8,128)(2,1)S(1)}, bf16[1792,1024]{1,0:T(8,128)(2,1)}, u32[]{:S(2)}) copy-start(bf16[1792,1024]{1,0:T(8,128)(2,1)} %x_ref.2) | copy-start | bytes 11010052
  3.6 2.0 %copy-start.3 = (bf16[1024,64]{0,1:T(8,128)(2,1)S(1)}, bf16[1024,64]{0,1:T(8,128)(2,1)}, u32[]{:S(2)}) copy-start(bf16[1024,64]{0,1:T(8,128)(2,1)} %param.8) | copy-start | bytes 393220
  4.9 7.0 %collective-permute-start.2 = (f32[2,32,1792]{2,1,0:T(8,128)S(1)}, f32[2,32,1792]{2,1,0:T(8,128)S(1)}, u32[]{:S(2)}, u32[]{:S(2)}) collective-permute-start(f32[2,32,1792]{2,1,0:T(8,128)S(1)} %select_bitcast_fusion), channel_id=1, source_target_pairs={{0,1},{1,0},{2,3},{3,2},{4,5},{5,4},{6,7},{7,6},{8,9},{9,8},{10,11... | collective-permute-start | bytes 1376264 | tf_op jit(solution)/shard_map/ppermute | solution.py:193
  5.7 1.8 %copy-start.4 = (s32[1,56]{1,0:T(1,128)S(1)}, s32[1,56]{1,0:T(1,128)}, u32[]{:S(2)}) copy-start(s32[1,56]{1,0:T(1,128)} %param.10) | copy-start | bytes 676
  6.9 1.6 %collective-permute-start = (f32[32,1792]{1,0:T(8,128)S(1)}, f32[32,1792]{1,0:T(8,128)S(1)}, u32[]{:S(2)}, u32[]{:S(2)}) collective-permute-start(f32[32,1792]{1,0:T(8,128)S(1)} %slice_select_fusion.1), channel_id=1, source_target_pairs={{0,1},{1,0},{2,3},{3,2},{4,5},{5,4},{6,7},{7,6},{8,9},{9,8},{10,11... | collective-permute-start | bytes 688136 | tf_op jit(solution)/shard_map/ppermute | solution.py:193
  9.0 7.0 %collective-permute-start.1 = (s16[32,1920]{1,0:T(8,128)(2,1)S(1)}, s16[32,1920]{1,0:T(8,128)(2,1)S(1)}, u32[]{:S(2)}, u32[]{:S(2)}) collective-permute-start(s16[32,1920]{1,0:T(8,128)(2,1)S(1)} %pad_add_fusion), channel_id=1, source_target_pairs={{0,2},{2,0},{1,3},{3,1},{4,6},{6,4},{5,7},{7,5},{8,10},{10,8},{9,1... | collective-permute-start | bytes 368648 | tf_op jit(solution)/shard_map/ppermute | solution.py:193
  12.3 5.8 %collective-permute-start.4 = (s16[32,1920]{1,0:T(8,128)(2,1)S(1)}, s16[32,1920]{1,0:T(8,128)(2,1)S(1)}, u32[]{:S(2)}, u32[]{:S(2)}) collective-permute-start(s16[32,1920]{1,0:T(8,128)(2,1)S(1)} %pad_add_fusion.1), channel_id=1, source_target_pairs={{0,2},{2,0},{1,3},{3,1},{4,6},{6,4},{5,7},{7,5},{8,10},{10,8},{9,1... | collective-permute-start | bytes 368648 | tf_op jit(solution)/shard_map/ppermute | solution.py:193
  16.2 2.2 %collective-permute-start.3 = (f32[32,1792]{1,0:T(8,128)S(1)}, f32[32,1792]{1,0:T(8,128)S(1)}, u32[]{:S(2)}, u32[]{:S(2)}) collective-permute-start(f32[32,1792]{1,0:T(8,128)S(1)} %fusion.1), channel_id=1, source_target_pairs={{0,1},{1,0},{2,3},{3,2},{4,5},{5,4},{6,7},{7,6},{8,9},{9,8},{10,11... | collective-permute-start | bytes 688136 | tf_op jit(solution)/shard_map/ppermute | solution.py:193
  21.3 2.0 %collective-permute-start.6 = (bf16[56,2048]{1,0:T(8,128)(2,1)S(1)}, bf16[56,2048]{1,0:T(8,128)(2,1)S(1)}, u32[]{:S(2)}, u32[]{:S(2)}) collective-permute-start(bf16[56,2048]{1,0:T(8,128)(2,1)S(1)} %features.1), channel_id=1, source_target_pairs={{0,1},{1,0},{2,3},{3,2},{4,5},{5,4},{6,7},{7,6},{8,9},{9,8},{10,11... | collective-permute-start | bytes 688136 | tf_op jit(solution)/shard_map/ppermute | solution.py:193
  21.4 9.1 %collective-permute-start.5 = (bf16[56,2048]{1,0:T(8,128)(2,1)S(1)}, bf16[56,2048]{1,0:T(8,128)(2,1)S(1)}, u32[]{:S(2)}, u32[]{:S(2)}) collective-permute-start(bf16[56,2048]{1,0:T(8,128)(2,1)S(1)} %features.1), channel_id=1, source_target_pairs={{0,4},{4,12},{12,8},{8,0},{1,5},{5,13},{13,9},{9,1},{2,6},{6,14},{... | collective-permute-start | bytes 688136 | tf_op jit(solution)/shard_map/ppermute | solution.py:248
  23.3 20.9 %copy-start.5 = (s32[64]{0:T(128)S(1)}, s32[64]{0:T(128)}, u32[]{:S(2)}) copy-start(s32[64]{0:T(128)} %param.11) | copy-start | bytes 772
  23.4 7.7 %collective-permute-start.7 = (bf16[56,2048]{1,0:T(8,128)(2,1)S(1)}, bf16[56,2048]{1,0:T(8,128)(2,1)S(1)}, u32[]{:S(2)}, u32[]{:S(2)}) collective-permute-start(bf16[56,2048]{1,0:T(8,128)(2,1)S(1)} %pad_maximum_fusion.4), channel_id=1, source_target_pairs={{0,2},{2,0},{1,3},{3,1},{4,6},{6,4},{5,7},{7,5},{8,10},{10,8},{9,1... | collective-permute-start | bytes 688136 | tf_op jit(solution)/shard_map/ppermute | solution.py:193
  31.1 2.6 %collective-permute-start.9 = (bf16[56,2048]{1,0:T(8,128)(2,1)S(1)}, bf16[56,2048]{1,0:T(8,128)(2,1)S(1)}, u32[]{:S(2)}, u32[]{:S(2)}) collective-permute-start(bf16[56,2048]{1,0:T(8,128)(2,1)S(1)} %collective-permute-done.5), channel_id=1, source_target_pairs={{0,1},{1,0},{2,3},{3,2},{4,5},{5,4},{6,7},{7,6},{8,9},{9,8},{10,11... | collective-permute-start | bytes 688136 | tf_op jit(solution)/shard_map/ppermute | solution.py:193
  31.1 9.0 %collective-permute-start.8 = (bf16[56,2048]{1,0:T(8,128)(2,1)S(1)}, bf16[56,2048]{1,0:T(8,128)(2,1)S(1)}, u32[]{:S(2)}, u32[]{:S(2)}) collective-permute-start(bf16[56,2048]{1,0:T(8,128)(2,1)S(1)} %collective-permute-done.5), channel_id=1, source_target_pairs={{0,4},{4,12},{12,8},{8,0},{1,5},{5,13},{13,9},{9,1},{2,6},{6,14},{... | collective-permute-start | bytes 688136 | tf_op jit(solution)/shard_map/ppermute | solution.py:248
  33.7 6.4 %collective-permute-start.10 = (bf16[56,1024]{1,0:T(8,128)(2,1)S(1)}, bf16[56,1024]{1,0:T(8,128)(2,1)S(1)}, u32[]{:S(2)}, u32[]{:S(2)}) collective-permute-start(bf16[56,1024]{1,0:T(8,128)(2,1)S(1)} %slice_select_fusion.3), channel_id=1, source_target_pairs={{0,2},{2,0},{1,3},{3,1},{4,6},{6,4},{5,7},{7,5},{8,10},{10,8},{9,1... | collective-permute-start | bytes 344072 | tf_op jit(solution)/shard_map/ppermute | solution.py:193
  35.3 7.1 %collective-permute-start.14 = (bf16[56,1024]{1,0:T(8,128)(2,1)S(1)}, bf16[56,1024]{1,0:T(8,128)(2,1)S(1)}, u32[]{:S(2)}, u32[]{:S(2)}) collective-permute-start(bf16[56,1024]{1,0:T(8,128)(2,1)S(1)} %get-tuple-element.39), channel_id=1, source_target_pairs={{4,0},{12,4},{8,12},{0,8},{5,1},{13,5},{9,13},{1,9},{6,2},{14,6},{... | collective-permute-start | bytes 344072 | tf_op jit(solution)/shard_map/ppermute | solution.py:252
  40.1 2.5 %collective-permute-start.12 = (bf16[56,2048]{1,0:T(8,128)(2,1)S(1)}, bf16[56,2048]{1,0:T(8,128)(2,1)S(1)}, u32[]{:S(2)}, u32[]{:S(2)}) collective-permute-start(bf16[56,2048]{1,0:T(8,128)(2,1)S(1)} %collective-permute-done.8), channel_id=1, source_target_pairs={{0,1},{1,0},{2,3},{3,2},{4,5},{5,4},{6,7},{7,6},{8,9},{9,8},{10,11... | collective-permute-start | bytes 688136 | tf_op jit(solution)/shard_map/ppermute | solution.py:193
  40.1 8.9 %collective-permute-start.11 = (bf16[56,2048]{1,0:T(8,128)(2,1)S(1)}, bf16[56,2048]{1,0:T(8,128)(2,1)S(1)}, u32[]{:S(2)}, u32[]{:S(2)}) collective-permute-start(bf16[56,2048]{1,0:T(8,128)(2,1)S(1)} %collective-permute-done.8), channel_id=1, source_target_pairs={{0,4},{4,12},{12,8},{8,0},{1,5},{5,13},{13,9},{9,1},{2,6},{6,14},{... | collective-permute-start | bytes 688136 | tf_op jit(solution)/shard_map/ppermute | solution.py:248
  42.5 6.5 %collective-permute-start.15 = (bf16[168,1024]{1,0:T(8,128)(2,1)S(1)}, bf16[168,1024]{1,0:T(8,128)(2,1)S(1)}, u32[]{:S(2)}, u32[]{:S(2)}) collective-permute-start(bf16[168,1024]{1,0:T(8,128)(2,1)S(1)} %pad_maximum_fusion.3), channel_id=1, source_target_pairs={{0,1},{1,0},{2,3},{3,2},{4,5},{5,4},{6,7},{7,6},{8,9},{9,8},{10,11... | collective-permute-start | bytes 1032200 | tf_op jit(solution)/shard_map/ppermute | solution.py:193
  42.6 6.4 %collective-permute-start.13 = (bf16[56,1024]{1,0:T(8,128)(2,1)S(1)}, bf16[56,1024]{1,0:T(8,128)(2,1)S(1)}, u32[]{:S(2)}, u32[]{:S(2)}) collective-permute-start(bf16[56,1024]{1,0:T(8,128)(2,1)S(1)} %slice_select_fusion.2), channel_id=1, source_target_pairs={{0,2},{2,0},{1,3},{3,1},{4,6},{6,4},{5,7},{7,5},{8,10},{10,8},{9,1... | collective-permute-start | bytes 344072 | tf_op jit(solution)/shard_map/ppermute | solution.py:193
  49.0 4.7 %collective-permute-start.19 = (bf16[56,2048]{1,0:T(8,128)(2,1)S(1)}, bf16[56,2048]{1,0:T(8,128)(2,1)S(1)}, u32[]{:S(2)}, u32[]{:S(2)}) collective-permute-start(bf16[56,2048]{1,0:T(8,128)(2,1)S(1)} %collective-permute-done.11), channel_id=1, source_target_pairs={{0,1},{1,0},{2,3},{3,2},{4,5},{5,4},{6,7},{7,6},{8,9},{9,8},{10,11... | collective-permute-start | bytes 688136 | tf_op jit(solution)/shard_map/ppermute | solution.py:193
  49.4 4.2 %collective-permute-start.18 = (bf16[56,1024]{1,0:T(8,128)(2,1)S(1)}, bf16[56,1024]{1,0:T(8,128)(2,1)S(1)}, u32[]{:S(2)}, u32[]{:S(2)}) collective-permute-start(bf16[56,1024]{1,0:T(8,128)(2,1)S(1)} %collective-permute-done.13), channel_id=1, source_target_pairs={{0,1},{1,0},{2,3},{3,2},{4,5},{5,4},{6,7},{7,6},{8,9},{9,8},{10,11... | collective-permute-start | bytes 344072 | tf_op jit(solution)/shard_map/ppermute | solution.py:193
  50.7 1.3 %collective-permute-start.16 = (f32[2,56,64]{2,1,0:T(8,128)S(1)}, f32[2,56,64]{2,1,0:T(8,128)S(1)}, u32[]{:S(2)}, u32[]{:S(2)}) collective-permute-start(f32[2,56,64]{2,1,0:T(8,128)S(1)} %pad_maximum_fusion.6), channel_id=1, source_target_pairs={{0,1},{1,0},{2,3},{3,2},{4,5},{5,4},{6,7},{7,6},{8,9},{9,8},{10,11... | collective-permute-start | bytes 86024 | tf_op jit(solution)/shard_map/ppermute | solution.py:193
  52.0 8.3 %collective-permute-start.17 = (f32[56,64]{1,0:T(8,128)S(1)}, f32[56,64]{1,0:T(8,128)S(1)}, u32[]{:S(2)}, u32[]{:S(2)}) collective-permute-start(f32[56,64]{1,0:T(8,128)S(1)} %get-tuple-element.44), channel_id=1, source_target_pairs={{0,2},{2,0},{1,3},{3,1},{4,6},{6,4},{5,7},{7,5},{8,10},{10,8},{9,1... | collective-permute-start | bytes 43016 | tf_op jit(solution)/shard_map/ppermute | solution.py:193

commit v7 on v6

--- a/solution.py
+++ b/solution.py
@@ -129,11 +129,12 @@
     )(starts, ends, u, v, scale)
 
 
-def score_kernel(ids_ref, all_ref, square_ref, part_ref):
+def score_kernel(ids_ref, all_ref, part_ref):
     every = all_ref[...]
     seqs = every.shape[0]
     picks = ids_ref.shape[0]
-    weights = 1.0 / (square_ref[...] / seqs + 1e-05)
+    wide = every.astype(F32)
+    weights = 1.0 / (jnp.sum(wide * wide, axis=0, keepdims=True) / seqs + 1e-05)
     column = lax.broadcasted_iota(I32, (picks, seqs), 1)
     chosen_of = jnp.where(column == ids_ref[...], 1.0, 0.0).astype(BF16)
     chosen = jnp.dot(chosen_of, every, preferred_element_type=F32)
@@ -143,16 +144,16 @@
     )
 
 
-def partial_scores_of(ids, gathered, squares):
+def partial_scores_of(ids, gathered):
     return pl.pallas_call(
         score_kernel,
-        in_specs=[VMEM, VMEM, VMEM],
+        in_specs=[VMEM, VMEM],
         out_specs=VMEM,
         out_shape=jax.ShapeDtypeStruct((gathered.shape[0], ids.shape[0]), F32),
         compiler_params=params(24),
         cost_estimate=pl.CostEstimate(flops=8 * gathered.size * ids.shape[0], bytes_accessed=2 * gathered.size, transcendentals=0),
         name="partial_scores",
-    )(ids[:, None], gathered, squares)
+    )(ids[:, None], gathered)
 
 
 def covariance_kernel(row_ref, col_ref, tile_hbm, tile_ref, sem):
@@ -176,7 +177,7 @@
 def covariance_of(gathered, other_cols):
     seqs, rows = gathered.shape
     cols = other_cols.shape[1]
-    steps = rows // 256
+    steps = rows // 128
     return pl.pallas_call(
         covariance_kernel,
         in_specs=[VMEM, VMEM],
@@ -269,10 +270,6 @@
     sub = lax.axis_index("sub")
     both = jnp.concatenate([picked(sub, mine, other), picked(sub, other, mine)], axis=1)
     return jnp.where(on_owner_chip(), part, both)
-
-
-def summed_squares(part):
-    return jnp.sum(jnp.square(part.astype(F32)), axis=0, keepdims=True)
 
 
 def column_block(gathered, col_width):
@@ -333,15 +330,13 @@
             ]
         )
         gathered = jnp.concatenate(chunks)
-        squares = summed_squares(gathered)
         seqs = local_feat.shape[0]
         ids = ((ring_place(at) - ring_place(target_ids // seqs)) & 3) * seqs + target_ids % seqs
     else:
         gathered = lax.all_gather(local_feat, "dp", axis=0, tiled=True)
         other_cols = column_block(gathered, gathered.shape[1] * group // lax.axis_size("dp"))
         ids = target_ids
-        squares = summed_squares(gathered)
-    part = partial_scores_of(ids, gathered, squares) / jnp.sqrt(jnp.float32(gathered.shape[1] * group))
+    part = partial_scores_of(ids, gathered) / jnp.sqrt(jnp.float32(gathered.shape[1] * group))
     own = part.shape[0] // group
     if is_square():
         places = [(ring_place(at) - ring_place(me ^ k)) & 3 for k in range(4)]

time: 61.1 us -> 60.8 us (level)
  transfers between devices with their start and end apart: 20 -> 20, of which waited for: 9 -> 9; matrix products, arithmetic and copies ran while one was open for 5% -> 4% of each run, Pallas kernels for 14% -> 13%
where the time goes in v7:
time: 60.8 us; the launch traced here: 60.7 us
  waiting for transfers between devices  22 us (36%)
  starting transfers between devices  18.9 us (31%)
  Pallas kernels  12.1 us (20%)
  local copies, waits for them, and re-layouts  3.74 us (6%)
  other arithmetic  2.91 us (5%)
  between operations  1 us (2%)
    ppermute x3, waiting for transfers between devices, around(): lax.ppermute(part, 'dp', [(RING[i], RING[(i + 1) % 4]) for i in range(4)])  13.7 us
    ppermute x16, starting transfers between devices, both_ways(): return lax.ppermute(x, axis, [(0, 1), (1, 0)])  11.1 us
    ppermute x16, waiting for transfers between devices, both_ways(): return lax.ppermute(x, axis, [(0, 1), (1, 0)])  7.94 us
    ppermute x3, starting transfers between devices, around(): lax.ppermute(part, 'dp', [(RING[i], RING[(i + 1) % 4]) for i in range(4)])  6.44 us
    pallas_call x1, Pallas kernels, covariance_of(): pl.pallas_call(covariance_kernel, in_specs=[VMEM, VMEM], out_specs=pl.Blo...  6.3 us
    unnamed x12, local copies, waits for them, and re-layouts  3.29 us
    pallas_call x1, Pallas kernels, features_of(): pl.pallas_call(feature_kernel, in_specs=[SMEM, SMEM, VMEM, VMEM, VMEM], o...  2.71 us
    pallas_call x2, Pallas kernels, project(): pl.pallas_call(project_flipped_kernel if flipped else project_kernel, in_...  2.41 us
  transfers between devices with their start and end apart: 20, of which 9 were waited for; matrix products, arithmetic and copies ran while one was open for 4% of the time, Pallas kernels for 13%

profile of v7, /device:TPU:0, one launch (start us, length us, event | category | flops | bytes accessed | tf_op | source)
XLA Modules:
  0.0 60.7 jit_solution(12081681781635224917)
XLA Ops:
  0.6 2.0 %copy-done = bf16[1792,1024]{1,0:T(8,128)(2,1)S(1)} copy-done((bf16[1792,1024]{1,0:T(8,128)(2,1)S(1)}, bf16[1792,1024]{1,0:T(8,128)(2,1)}, u32[]{:S(2)}) %copy-start) | copy-done | bytes 3670040
  2.7 0.9 %copy-done.1 = bf16[1024,128]{1,0:T(8,128)(2,1)S(1)} copy-done((bf16[1024,128]{1,0:T(8,128)(2,1)S(1)}, bf16[1024,128]{1,0:T(8,128)(2,1)}, u32[]{:S(2)}) %copy-start.1) | copy-done | bytes 262168
  3.6 1.2 %project.3 = f32[128,1792]{1,0:T(8,128)S(1)} custom-call(bf16[1792,1024]{1,0:T(8,128)(2,1)S(1)} %copy-done, bf16[1024,128]{1,0:T(8,128)(2,1)S(1)} %copy-done.1), custom_call_target="tpu_custom_call" | custom-call | flops 469762048 | bytes 3670016 | tf_op jit(solution)/shard_map/project/pallas_call | solution.py:37
  4.9 0.5 collective-permute-start.2
  5.4 0.3 copy-done.2
  5.7 1.2 %project.2 = f32[64,1792]{1,0:T(8,128)S(1)} custom-call(bf16[1792,1024]{1,0:T(8,128)(2,1)S(1)} %copy-done.2, bf16[64,1024]{1,0:T(8,128)(2,1)S(1)} %bitcast.46), custom_call_target="tpu_custom_call" | custom-call | flops 4697620480 | bytes 3670016 | tf_op jit(solution)/shard_map/project/pallas_call | solution.py:37
  6.9 0.5 collective-permute-start
  7.5 0.1 copy.10
  7.6 0.1 reduce-window.9
  7.7 0.1 reduce.end_ref
  7.8 0.8 %collective-permute-done = f32[32,1792]{1,0:T(8,128)S(1)} collective-permute-done((f32[32,1792]{1,0:T(8,128)S(1)}, f32[32,1792]{1,0:T(8,128)S(1)}, u32[]{:S(2)}, u32[]{:S(2)}) %collective-permute-start) | collective-permute-done | bytes 229408 | tf_op jit(solution)/shard_map/ppermute | solution.py:194
  8.6 0.1 abs_reduce_fusion
  8.7 0.1 round-nearest-even_convert_fusion
  9.0 2.9 %collective-permute-start.1 = (s16[32,1920]{1,0:T(8,128)(2,1)S(1)}, s16[32,1920]{1,0:T(8,128)(2,1)S(1)}, u32[]{:S(2)}, u32[]{:S(2)}) collective-permute-start(s16[32,1920]{1,0:T(8,128)(2,1)S(1)} %pad_add_fusion), channel_id=1, source_target_pairs={{0,2},{2,0},{1,3},{3,1},{4,6},{6,4},{5,7},{7,5},{8,10},{10,8},{9,1... | collective-permute-start | bytes 368648 | tf_op jit(solution)/shard_map/ppermute | solution.py:194
  12.0 0.1 fusion.2
  12.1 0.1 fusion.4
  12.3 0.1 collective-permute-start.4
  12.4 3.6 %collective-permute-done.1 = s16[32,1920]{1,0:T(8,128)(2,1)S(1)} collective-permute-done((s16[32,1920]{1,0:T(8,128)(2,1)S(1)}, s16[32,1920]{1,0:T(8,128)(2,1)S(1)}, u32[]{:S(2)}, u32[]{:S(2)}) %collective-permute-start.1) | collective-permute-done | bytes 122912 | tf_op jit(solution)/shard_map/ppermute | solution.py:194
  16.0 0.1 fusion.10
  16.1 0.1 fusion.1
  16.3 1.8 %collective-permute-done.4 = s16[32,1920]{1,0:T(8,128)(2,1)S(1)} collective-permute-done((s16[32,1920]{1,0:T(8,128)(2,1)S(1)}, s16[32,1920]{1,0:T(8,128)(2,1)S(1)}, u32[]{:S(2)}, u32[]{:S(2)}) %collective-permute-start.4) | collective-permute-done | bytes 122912 | tf_op jit(solution)/shard_map/ppermute | solution.py:194
  18.2 0.1 fusion.7
  18.3 0.1 fusion.v_ref
  18.6 2.7 %features.1 = bf16[56,2048]{1,0:T(8,128)(2,1)S(1)} custom-call(s32[56]{0:T(128)S(1)} %bitcast_subtract_fusion.start_ref, s32[56]{0:T(128)S(1)} %reduce.end_ref, f32[64,1792]{1,0:T(8,128)S(1)} %pad_maximum_fusion.2.u_ref, f32[32,1792]{1,0:T(8,128)S(1)} %fusion.v_ref, f32[56,128]{1,0:T(8,128)S(1)} %broadcast_in_dim.11.scale_ref), custom_call_target="tpu_custom_call" | custom-call | tf_op jit(solution)/shard_map/features/pallas_call | solution.py:115
  21.4 1.9 %collective-permute-start.5 = (bf16[56,2048]{1,0:T(8,128)(2,1)S(1)}, bf16[56,2048]{1,0:T(8,128)(2,1)S(1)}, u32[]{:S(2)}, u32[]{:S(2)}) collective-permute-start(bf16[56,2048]{1,0:T(8,128)(2,1)S(1)} %features.1), channel_id=1, source_target_pairs={{0,4},{4,12},{12,8},{8,0},{1,5},{5,13},{13,9},{9,1},{2,6},{6,14},{... | collective-permute-start | bytes 688136 | tf_op jit(solution)/shard_map/ppermute | solution.py:249
  23.4 1.6 %collective-permute-start.7 = (bf16[56,2048]{1,0:T(8,128)(2,1)S(1)}, bf16[56,2048]{1,0:T(8,128)(2,1)S(1)}, u32[]{:S(2)}, u32[]{:S(2)}) collective-permute-start(bf16[56,2048]{1,0:T(8,128)(2,1)S(1)} %pad_maximum_fusion.4), channel_id=1, source_target_pairs={{0,2},{2,0},{1,3},{3,1},{4,6},{6,4},{5,7},{7,5},{8,10},{10,8},{9,1... | collective-permute-start | bytes 688136 | tf_op jit(solution)/shard_map/ppermute | solution.py:194
  24.9 5.5 %collective-permute-done.5 = bf16[56,2048]{1,0:T(8,128)(2,1)S(1)} collective-permute-done((bf16[56,2048]{1,0:T(8,128)(2,1)S(1)}, bf16[56,2048]{1,0:T(8,128)(2,1)S(1)}, u32[]{:S(2)}, u32[]{:S(2)}) %collective-permute-start.5) | collective-permute-done | bytes 229408 | tf_op jit(solution)/shard_map/ppermute | solution.py:249
  30.4 0.6 %collective-permute-done.7 = bf16[56,2048]{1,0:T(8,128)(2,1)S(1)} collective-permute-done((bf16[56,2048]{1,0:T(8,128)(2,1)S(1)}, bf16[56,2048]{1,0:T(8,128)(2,1)S(1)}, u32[]{:S(2)}, u32[]{:S(2)}) %collective-permute-start.7) | collective-permute-done | bytes 229408 | tf_op jit(solution)/shard_map/ppermute | solution.py:194
  31.1 2.6 %collective-permute-start.8 = (bf16[56,2048]{1,0:T(8,128)(2,1)S(1)}, bf16[56,2048]{1,0:T(8,128)(2,1)S(1)}, u32[]{:S(2)}, u32[]{:S(2)}) collective-permute-start(bf16[56,2048]{1,0:T(8,128)(2,1)S(1)} %collective-permute-done.5), channel_id=1, source_target_pairs={{0,4},{4,12},{12,8},{8,0},{1,5},{5,13},{13,9},{9,1},{2,6},{6,14},{... | collective-permute-start | bytes 688136 | tf_op jit(solution)/shard_map/ppermute | solution.py:249
  33.7 1.6 %collective-permute-start.10 = (bf16[56,1024]{1,0:T(8,128)(2,1)S(1)}, bf16[56,1024]{1,0:T(8,128)(2,1)S(1)}, u32[]{:S(2)}, u32[]{:S(2)}) collective-permute-start(bf16[56,1024]{1,0:T(8,128)(2,1)S(1)} %slice_select_fusion.3), channel_id=1, source_target_pairs={{0,2},{2,0},{1,3},{3,1},{4,6},{6,4},{5,7},{7,5},{8,10},{10,8},{9,1... | collective-permute-start | bytes 344072 | tf_op jit(solution)/shard_map/ppermute | solution.py:194
  35.3 1.3 %collective-permute-start.14 = (bf16[56,1024]{1,0:T(8,128)(2,1)S(1)}, bf16[56,1024]{1,0:T(8,128)(2,1)S(1)}, u32[]{:S(2)}, u32[]{:S(2)}) collective-permute-start(bf16[56,1024]{1,0:T(8,128)(2,1)S(1)} %get-tuple-element.37), channel_id=1, source_target_pairs={{4,0},{12,4},{8,12},{0,8},{5,1},{13,5},{9,13},{1,9},{6,2},{14,6},{... | collective-permute-start | bytes 344072 | tf_op jit(solution)/shard_map/ppermute | solution.py:253
  36.7 3.5 %collective-permute-done.8 = bf16[56,2048]{1,0:T(8,128)(2,1)S(1)} collective-permute-done((bf16[56,2048]{1,0:T(8,128)(2,1)S(1)}, bf16[56,2048]{1,0:T(8,128)(2,1)S(1)}, u32[]{:S(2)}, u32[]{:S(2)}) %collective-permute-start.8) | collective-permute-done | bytes 229408 | tf_op jit(solution)/shard_map/ppermute | solution.py:249
  40.1 2.0 %collective-permute-start.11 = (bf16[56,2048]{1,0:T(8,128)(2,1)S(1)}, bf16[56,2048]{1,0:T(8,128)(2,1)S(1)}, u32[]{:S(2)}, u32[]{:S(2)}) collective-permute-start(bf16[56,2048]{1,0:T(8,128)(2,1)S(1)} %collective-permute-done.8), channel_id=1, source_target_pairs={{0,4},{4,12},{12,8},{8,0},{1,5},{5,13},{13,9},{9,1},{2,6},{6,14},{... | collective-permute-start | bytes 688136 | tf_op jit(solution)/shard_map/ppermute | solution.py:249
  42.1 0.4 collective-permute-done.14
  42.6 1.6 %collective-permute-start.13 = (bf16[56,1024]{1,0:T(8,128)(2,1)S(1)}, bf16[56,1024]{1,0:T(8,128)(2,1)S(1)}, u32[]{:S(2)}, u32[]{:S(2)}) collective-permute-start(bf16[56,1024]{1,0:T(8,128)(2,1)S(1)} %slice_select_fusion.2), channel_id=1, source_target_pairs={{0,2},{2,0},{1,3},{3,1},{4,6},{6,4},{5,7},{7,5},{8,10},{10,8},{9,1... | collective-permute-start | bytes 344072 | tf_op jit(solution)/shard_map/ppermute | solution.py:194
  44.2 0.1 copy.13.ids_ref
  44.3 4.7 %collective-permute-done.11 = bf16[56,2048]{1,0:T(8,128)(2,1)S(1)} collective-permute-done((bf16[56,2048]{1,0:T(8,128)(2,1)S(1)}, bf16[56,2048]{1,0:T(8,128)(2,1)S(1)}, u32[]{:S(2)}, u32[]{:S(2)}) %collective-permute-start.11) | collective-permute-done | bytes 229408 | tf_op jit(solution)/shard_map/ppermute | solution.py:249
  49.1 0.1 pad_maximum_fusion.all_ref.row_ref
  49.1 0.1 broadcast_select_fusion.1
  49.3 0.6 collective-permute-start.18
  49.8 0.7 %partial_scores.1 = f32[224,64]{1,0:T(8,128)S(1)} custom-call(s32[64,1]{1,0:T(8,128)S(1)} %copy.13.ids_ref, bf16[224,2048]{1,0:T(8,128)(2,1)S(1)} %pad_maximum_fusion.all_ref.row_ref), custom_call_target="tpu_custom_call" | custom-call | flops 234881024 | bytes 917504 | tf_op jit(solution)/shard_map/partial_scores/pallas_call | solution.py:148
  50.6 0.1 maximum_select_fusion
  50.8 1.1 %collective-permute-done.16 = f32[2,56,64]{2,1,0:T(8,128)S(1)} collective-permute-done((f32[2,56,64]{2,1,0:T(8,128)S(1)}, f32[2,56,64]{2,1,0:T(8,128)S(1)}, u32[]{:S(2)}, u32[]{:S(2)}) %collective-permute-start.16) | collective-permute-done | bytes 28704 | tf_op jit(solution)/shard_map/ppermute | solution.py:194
  51.9 1.6 %collective-permute-start.17 = (f32[56,64]{1,0:T(8,128)S(1)}, f32[56,64]{1,0:T(8,128)S(1)}, u32[]{:S(2)}, u32[]{:S(2)}) collective-permute-start(f32[56,64]{1,0:T(8,128)S(1)} %get-tuple-element.42), channel_id=1, source_target_pairs={{0,2},{2,0},{1,3},{3,1},{4,6},{6,4},{5,7},{7,5},{8,10},{10,8},{9,1... | collective-permute-start | bytes 43016 | tf_op jit(solution)/shard_map/ppermute | solution.py:194
  53.5 0.1 maximum_select_fusion.2
  53.6 0.1 pad_maximum_fusion.1.col_ref
  53.7 6.3 %covariance.1 = f32[2048,2048]{1,0:T(8,128)} custom-call(bf16[224,2048]{1,0:T(8,128)(2,1)S(1)} %pad_maximum_fusion.all_ref.row_ref, bf16[224,2048]{1,0:T(8,128)(2,1)S(1)} %pad_maximum_fusion.1.col_ref), custom_call_target="tpu_custom_call" | custom-call | flops 1879048192 | bytes 16777216 | tf_op jit(solution)/shard_map/covariance/pallas_call | solution.py:181
  60.0 0.6 %add_bitcast_fusion = f32[64,56]{0,1:T(8,128)} fusion(f32[56,64]{1,0:T(8,128)S(1)} %get-tuple-element.22, f32[56,64]{1,0:T(8,128)S(1)} %collective-permute-done.17), kind=kLoop, calls=%fused_computation.50 | loop fusion | flops 3584 | bytes 43008 | tf_op jit(solution)/shard_map/transpose | solution.py:353
  (61 shorter events, 1.3 us)
Async XLA Ops:
  0.6 2.0 %copy-start = (bf16[1792,1024]{1,0:T(8,128)(2,1)S(1)}, bf16[1792,1024]{1,0:T(8,128)(2,1)}, u32[]{:S(2)}) copy-start(bf16[1792,1024]{1,0:T(8,128)(2,1)} %x_ref.3) | copy-start | bytes 11010052
  2.7 0.9 %copy-start.1 = (bf16[1024,128]{1,0:T(8,128)(2,1)S(1)}, bf16[1024,128]{1,0:T(8,128)(2,1)}, u32[]{:S(2)}) copy-start(bf16[1024,128]{1,0:T(8,128)(2,1)} %weight_ref.1) | copy-start | bytes 786436
  3.6 2.0 %copy-start.2 = (bf16[1792,1024]{1,0:T(8,128)(2,1)S(1)}, bf16[1792,1024]{1,0:T(8,128)(2,1)}, u32[]{:S(2)}) copy-start(bf16[1792,1024]{1,0:T(8,128)(2,1)} %x_ref.2) | copy-start | bytes 11010052
  3.6 2.0 %copy-start.3 = (bf16[1024,64]{0,1:T(8,128)(2,1)S(1)}, bf16[1024,64]{0,1:T(8,128)(2,1)}, u32[]{:S(2)}) copy-start(bf16[1024,64]{0,1:T(8,128)(2,1)} %param.8) | copy-start | bytes 393220
  4.9 7.0 %collective-permute-start.2 = (f32[2,32,1792]{2,1,0:T(8,128)S(1)}, f32[2,32,1792]{2,1,0:T(8,128)S(1)}, u32[]{:S(2)}, u32[]{:S(2)}) collective-permute-start(f32[2,32,1792]{2,1,0:T(8,128)S(1)} %select_bitcast_fusion), channel_id=1, source_target_pairs={{0,1},{1,0},{2,3},{3,2},{4,5},{5,4},{6,7},{7,6},{8,9},{9,8},{10,11... | collective-permute-start | bytes 1376264 | tf_op jit(solution)/shard_map/ppermute | solution.py:194
  5.7 1.8 %copy-start.4 = (s32[1,56]{1,0:T(1,128)S(1)}, s32[1,56]{1,0:T(1,128)}, u32[]{:S(2)}) copy-start(s32[1,56]{1,0:T(1,128)} %param.10) | copy-start | bytes 676
  6.9 1.6 %collective-permute-start = (f32[32,1792]{1,0:T(8,128)S(1)}, f32[32,1792]{1,0:T(8,128)S(1)}, u32[]{:S(2)}, u32[]{:S(2)}) collective-permute-start(f32[32,1792]{1,0:T(8,128)S(1)} %slice_select_fusion.1), channel_id=1, source_target_pairs={{0,1},{1,0},{2,3},{3,2},{4,5},{5,4},{6,7},{7,6},{8,9},{9,8},{10,11... | collective-permute-start | bytes 688136 | tf_op jit(solution)/shard_map/ppermute | solution.py:194
  9.0 7.0 %collective-permute-start.1 = (s16[32,1920]{1,0:T(8,128)(2,1)S(1)}, s16[32,1920]{1,0:T(8,128)(2,1)S(1)}, u32[]{:S(2)}, u32[]{:S(2)}) collective-permute-start(s16[32,1920]{1,0:T(8,128)(2,1)S(1)} %pad_add_fusion), channel_id=1, source_target_pairs={{0,2},{2,0},{1,3},{3,1},{4,6},{6,4},{5,7},{7,5},{8,10},{10,8},{9,1... | collective-permute-start | bytes 368648 | tf_op jit(solution)/shard_map/ppermute | solution.py:194
  12.3 5.8 %collective-permute-start.4 = (s16[32,1920]{1,0:T(8,128)(2,1)S(1)}, s16[32,1920]{1,0:T(8,128)(2,1)S(1)}, u32[]{:S(2)}, u32[]{:S(2)}) collective-permute-start(s16[32,1920]{1,0:T(8,128)(2,1)S(1)} %pad_add_fusion.1), channel_id=1, source_target_pairs={{0,2},{2,0},{1,3},{3,1},{4,6},{6,4},{5,7},{7,5},{8,10},{10,8},{9,1... | collective-permute-start | bytes 368648 | tf_op jit(solution)/shard_map/ppermute | solution.py:194
  16.2 2.2 %collective-permute-start.3 = (f32[32,1792]{1,0:T(8,128)S(1)}, f32[32,1792]{1,0:T(8,128)S(1)}, u32[]{:S(2)}, u32[]{:S(2)}) collective-permute-start(f32[32,1792]{1,0:T(8,128)S(1)} %fusion.1), channel_id=1, source_target_pairs={{0,1},{1,0},{2,3},{3,2},{4,5},{5,4},{6,7},{7,6},{8,9},{9,8},{10,11... | collective-permute-start | bytes 688136 | tf_op jit(solution)/shard_map/ppermute | solution.py:194
  21.3 2.0 %collective-permute-start.6 = (bf16[56,2048]{1,0:T(8,128)(2,1)S(1)}, bf16[56,2048]{1,0:T(8,128)(2,1)S(1)}, u32[]{:S(2)}, u32[]{:S(2)}) collective-permute-start(bf16[56,2048]{1,0:T(8,128)(2,1)S(1)} %features.1), channel_id=1, source_target_pairs={{0,1},{1,0},{2,3},{3,2},{4,5},{5,4},{6,7},{7,6},{8,9},{9,8},{10,11... | collective-permute-start | bytes 688136 | tf_op jit(solution)/shard_map/ppermute | solution.py:194
  21.4 9.1 %collective-permute-start.5 = (bf16[56,2048]{1,0:T(8,128)(2,1)S(1)}, bf16[56,2048]{1,0:T(8,128)(2,1)S(1)}, u32[]{:S(2)}, u32[]{:S(2)}) collective-permute-start(bf16[56,2048]{1,0:T(8,128)(2,1)S(1)} %features.1), channel_id=1, source_target_pairs={{0,4},{4,12},{12,8},{8,0},{1,5},{5,13},{13,9},{9,1},{2,6},{6,14},{... | collective-permute-start | bytes 688136 | tf_op jit(solution)/shard_map/ppermute | solution.py:249
  23.3 20.9 %copy-start.5 = (s32[64]{0:T(128)S(1)}, s32[64]{0:T(128)}, u32[]{:S(2)}) copy-start(s32[64]{0:T(128)} %param.11) | copy-start | bytes 772
  23.4 7.7 %collective-permute-start.7 = (bf16[56,2048]{1,0:T(8,128)(2,1)S(1)}, bf16[56,2048]{1,0:T(8,128)(2,1)S(1)}, u32[]{:S(2)}, u32[]{:S(2)}) collective-permute-start(bf16[56,2048]{1,0:T(8,128)(2,1)S(1)} %pad_maximum_fusion.4), channel_id=1, source_target_pairs={{0,2},{2,0},{1,3},{3,1},{4,6},{6,4},{5,7},{7,5},{8,10},{10,8},{9,1... | collective-permute-start | bytes 688136 | tf_op jit(solution)/shard_map/ppermute | solution.py:194
  31.1 2.6 %collective-permute-start.9 = (bf16[56,2048]{1,0:T(8,128)(2,1)S(1)}, bf16[56,2048]{1,0:T(8,128)(2,1)S(1)}, u32[]{:S(2)}, u32[]{:S(2)}) collective-permute-start(bf16[56,2048]{1,0:T(8,128)(2,1)S(1)} %collective-permute-done.5), channel_id=1, source_target_pairs={{0,1},{1,0},{2,3},{3,2},{4,5},{5,4},{6,7},{7,6},{8,9},{9,8},{10,11... | collective-permute-start | bytes 688136 | tf_op jit(solution)/shard_map/ppermute | solution.py:194
  31.1 9.0 %collective-permute-start.8 = (bf16[56,2048]{1,0:T(8,128)(2,1)S(1)}, bf16[56,2048]{1,0:T(8,128)(2,1)S(1)}, u32[]{:S(2)}, u32[]{:S(2)}) collective-permute-start(bf16[56,2048]{1,0:T(8,128)(2,1)S(1)} %collective-permute-done.5), channel_id=1, source_target_pairs={{0,4},{4,12},{12,8},{8,0},{1,5},{5,13},{13,9},{9,1},{2,6},{6,14},{... | collective-permute-start | bytes 688136 | tf_op jit(solution)/shard_map/ppermute | solution.py:249
  33.7 6.4 %collective-permute-start.10 = (bf16[56,1024]{1,0:T(8,128)(2,1)S(1)}, bf16[56,1024]{1,0:T(8,128)(2,1)S(1)}, u32[]{:S(2)}, u32[]{:S(2)}) collective-permute-start(bf16[56,1024]{1,0:T(8,128)(2,1)S(1)} %slice_select_fusion.3), channel_id=1, source_target_pairs={{0,2},{2,0},{1,3},{3,1},{4,6},{6,4},{5,7},{7,5},{8,10},{10,8},{9,1... | collective-permute-start | bytes 344072 | tf_op jit(solution)/shard_map/ppermute | solution.py:194
  35.3 7.1 %collective-permute-start.14 = (bf16[56,1024]{1,0:T(8,128)(2,1)S(1)}, bf16[56,1024]{1,0:T(8,128)(2,1)S(1)}, u32[]{:S(2)}, u32[]{:S(2)}) collective-permute-start(bf16[56,1024]{1,0:T(8,128)(2,1)S(1)} %get-tuple-element.37), channel_id=1, source_target_pairs={{4,0},{12,4},{8,12},{0,8},{5,1},{13,5},{9,13},{1,9},{6,2},{14,6},{... | collective-permute-start | bytes 344072 | tf_op jit(solution)/shard_map/ppermute | solution.py:253
  40.1 2.5 %collective-permute-start.12 = (bf16[56,2048]{1,0:T(8,128)(2,1)S(1)}, bf16[56,2048]{1,0:T(8,128)(2,1)S(1)}, u32[]{:S(2)}, u32[]{:S(2)}) collective-permute-start(bf16[56,2048]{1,0:T(8,128)(2,1)S(1)} %collective-permute-done.8), channel_id=1, source_target_pairs={{0,1},{1,0},{2,3},{3,2},{4,5},{5,4},{6,7},{7,6},{8,9},{9,8},{10,11... | collective-permute-start | bytes 688136 | tf_op jit(solution)/shard_map/ppermute | solution.py:194
  40.1 8.9 %collective-permute-start.11 = (bf16[56,2048]{1,0:T(8,128)(2,1)S(1)}, bf16[56,2048]{1,0:T(8,128)(2,1)S(1)}, u32[]{:S(2)}, u32[]{:S(2)}) collective-permute-start(bf16[56,2048]{1,0:T(8,128)(2,1)S(1)} %collective-permute-done.8), channel_id=1, source_target_pairs={{0,4},{4,12},{12,8},{8,0},{1,5},{5,13},{13,9},{9,1},{2,6},{6,14},{... | collective-permute-start | bytes 688136 | tf_op jit(solution)/shard_map/ppermute | solution.py:249
  42.5 6.5 %collective-permute-start.15 = (bf16[168,1024]{1,0:T(8,128)(2,1)S(1)}, bf16[168,1024]{1,0:T(8,128)(2,1)S(1)}, u32[]{:S(2)}, u32[]{:S(2)}) collective-permute-start(bf16[168,1024]{1,0:T(8,128)(2,1)S(1)} %pad_maximum_fusion.3), channel_id=1, source_target_pairs={{0,1},{1,0},{2,3},{3,2},{4,5},{5,4},{6,7},{7,6},{8,9},{9,8},{10,11... | collective-permute-start | bytes 1032200 | tf_op jit(solution)/shard_map/ppermute | solution.py:194
  42.6 6.4 %collective-permute-start.13 = (bf16[56,1024]{1,0:T(8,128)(2,1)S(1)}, bf16[56,1024]{1,0:T(8,128)(2,1)S(1)}, u32[]{:S(2)}, u32[]{:S(2)}) collective-permute-start(bf16[56,1024]{1,0:T(8,128)(2,1)S(1)} %slice_select_fusion.2), channel_id=1, source_target_pairs={{0,2},{2,0},{1,3},{3,1},{4,6},{6,4},{5,7},{7,5},{8,10},{10,8},{9,1... | collective-permute-start | bytes 344072 | tf_op jit(solution)/shard_map/ppermute | solution.py:194
  49.0 4.5 %collective-permute-start.19 = (bf16[56,2048]{1,0:T(8,128)(2,1)S(1)}, bf16[56,2048]{1,0:T(8,128)(2,1)S(1)}, u32[]{:S(2)}, u32[]{:S(2)}) collective-permute-start(bf16[56,2048]{1,0:T(8,128)(2,1)S(1)} %collective-permute-done.11), channel_id=1, source_target_pairs={{0,1},{1,0},{2,3},{3,2},{4,5},{5,4},{6,7},{7,6},{8,9},{9,8},{10,11... | collective-permute-start | bytes 688136 | tf_op jit(solution)/shard_map/ppermute | solution.py:194
  49.3 4.2 %collective-permute-start.18 = (bf16[56,1024]{1,0:T(8,128)(2,1)S(1)}, bf16[56,1024]{1,0:T(8,128)(2,1)S(1)}, u32[]{:S(2)}, u32[]{:S(2)}) collective-permute-start(bf16[56,1024]{1,0:T(8,128)(2,1)S(1)} %collective-permute-done.13), channel_id=1, source_target_pairs={{0,1},{1,0},{2,3},{3,2},{4,5},{5,4},{6,7},{7,6},{8,9},{9,8},{10,11... | collective-permute-start | bytes 344072 | tf_op jit(solution)/shard_map/ppermute | solution.py:194
  50.5 1.3 %collective-permute-start.16 = (f32[2,56,64]{2,1,0:T(8,128)S(1)}, f32[2,56,64]{2,1,0:T(8,128)S(1)}, u32[]{:S(2)}, u32[]{:S(2)}) collective-permute-start(f32[2,56,64]{2,1,0:T(8,128)S(1)} %pad_maximum_fusion.6), channel_id=1, source_target_pairs={{0,1},{1,0},{2,3},{3,2},{4,5},{5,4},{6,7},{7,6},{8,9},{9,8},{10,11... | collective-permute-start | bytes 86024 | tf_op jit(solution)/shard_map/ppermute | solution.py:194
  51.9 8.2 %collective-permute-start.17 = (f32[56,64]{1,0:T(8,128)S(1)}, f32[56,64]{1,0:T(8,128)S(1)}, u32[]{:S(2)}, u32[]{:S(2)}) collective-permute-start(f32[56,64]{1,0:T(8,128)S(1)} %get-tuple-element.42), channel_id=1, source_target_pairs={{0,2},{2,0},{1,3},{3,1},{4,6},{6,4},{5,7},{7,5},{8,10},{10,8},{9,1... | collective-permute-start | bytes 43016 | tf_op jit(solution)/shard_map/ppermute | solution.py:194

commit v8 on v7

--- a/solution.py
+++ b/solution.py
@@ -342,11 +342,10 @@
         places = [(ring_place(at) - ring_place(me ^ k)) & 3 for k in range(4)]
         pieces = part.reshape(group, own, -1)
         pieces = [lax.dynamic_index_in_dim(pieces, place, 0, keepdims=False) for place in places]
-        summed = jnp.stack([pieces[0], pieces[2]]) + both_ways(jnp.stack([pieces[1], pieces[3]]), "sub")
-        given = both_ways(summed[1], "feat")
+        given = [lax.ppermute(pieces[k], WIDE, [(i, i ^ k) for i in range(4)]) for k in (1, 2, 3)]
         tile = covariance_of(gathered, other_cols)
-        mine, given, tile = lax.optimization_barrier((summed[0], given, tile))
-        total = mine + given
+        mine, given, tile = lax.optimization_barrier((pieces[0], given, tile))
+        total = mine + given[0] + given[1] + given[2]
     else:
         total = lax.psum_scatter(part, WIDE, scatter_dimension=0, tiled=True)
         tile = covariance_of(gathered, other_cols)

time: 60.8 us -> 60.1 us (0.988)
  waiting for transfers between devices: 22 us -> 20.9 us
    ppermute x0 -> x3, starting transfers between devices: none -> 1.94 us  [shards(): lax.ppermute(pieces[k], WIDE, [(i, i ^ k) for i in range(4)])]
    ppermute x16 -> x14, starting transfers between devices: 11.1 us -> 9.51 us  [both_ways(): return lax.ppermute(x, axis, [(0, 1), (1, 0)])]
    ppermute x16 -> x14, waiting for transfers between devices: 7.94 us -> 6.86 us  [both_ways(): return lax.ppermute(x, axis, [(0, 1), (1, 0)])]
  transfers between devices with their start and end apart: 20 -> 21, of which waited for: 9 -> 8; matrix products, arithmetic and copies ran while one was open for 4% -> 4% of each run, Pallas kernels for 13% -> 14%
where the time goes in v8:
time: 60.1 us; the launch traced here: 59.9 us
  waiting for transfers between devices  20.9 us (35%)
  starting transfers between devices  19.2 us (32%)
  Pallas kernels  12.1 us (20%)
  local copies, waits for them, and re-layouts  3.74 us (6%)
  other arithmetic  2.9 us (5%)
  between operations  1.01 us (2%)
    ppermute x3, waiting for transfers between devices, around(): lax.ppermute(part, 'dp', [(RING[i], RING[(i + 1) % 4]) for i in range(4)])  13.7 us
    ppermute x14, starting transfers between devices, both_ways(): return lax.ppermute(x, axis, [(0, 1), (1, 0)])  9.51 us
    ppermute x14, waiting for transfers between devices, both_ways(): return lax.ppermute(x, axis, [(0, 1), (1, 0)])  6.86 us
    ppermute x3, starting transfers between devices, around(): lax.ppermute(part, 'dp', [(RING[i], RING[(i + 1) % 4]) for i in range(4)])  6.44 us
    pallas_call x1, Pallas kernels, covariance_of(): pl.pallas_call(covariance_kernel, in_specs=[VMEM, VMEM], out_specs=pl.Blo...  6.3 us
    unnamed x12, local copies, waits for them, and re-layouts  3.29 us
    pallas_call x1, Pallas kernels, features_of(): pl.pallas_call(feature_kernel, in_specs=[SMEM, SMEM, VMEM, VMEM, VMEM], o...  2.71 us
    pallas_call x2, Pallas kernels, project(): pl.pallas_call(project_flipped_kernel if flipped else project_kernel, in_...  2.41 us
  transfers between devices with their start and end apart: 21, of which 8 were waited for; matrix products, arithmetic and copies ran while one was open for 4% of the time, Pallas kernels for 14%

profile of v8, /device:TPU:0, one launch (start us, length us, event | category | flops | bytes accessed | tf_op | source)
XLA Modules:
  0.0 59.9 jit_solution(9322071927579378295)
XLA Ops:
  0.6 2.0 %copy-done = bf16[1792,1024]{1,0:T(8,128)(2,1)S(1)} copy-done((bf16[1792,1024]{1,0:T(8,128)(2,1)S(1)}, bf16[1792,1024]{1,0:T(8,128)(2,1)}, u32[]{:S(2)}) %copy-start) | copy-done | bytes 3670040
  2.7 0.9 %copy-done.1 = bf16[1024,128]{1,0:T(8,128)(2,1)S(1)} copy-done((bf16[1024,128]{1,0:T(8,128)(2,1)S(1)}, bf16[1024,128]{1,0:T(8,128)(2,1)}, u32[]{:S(2)}) %copy-start.1) | copy-done | bytes 262168
  3.6 1.2 %project.3 = f32[128,1792]{1,0:T(8,128)S(1)} custom-call(bf16[1792,1024]{1,0:T(8,128)(2,1)S(1)} %copy-done, bf16[1024,128]{1,0:T(8,128)(2,1)S(1)} %copy-done.1), custom_call_target="tpu_custom_call" | custom-call | flops 469762048 | bytes 3670016 | tf_op jit(solution)/shard_map/project/pallas_call | solution.py:37
  4.9 0.5 collective-permute-start.2
  5.4 0.3 copy-done.2
  5.7 1.2 %project.2 = f32[64,1792]{1,0:T(8,128)S(1)} custom-call(bf16[1792,1024]{1,0:T(8,128)(2,1)S(1)} %copy-done.2, bf16[64,1024]{1,0:T(8,128)(2,1)S(1)} %bitcast.50), custom_call_target="tpu_custom_call" | custom-call | flops 4697620480 | bytes 3670016 | tf_op jit(solution)/shard_map/project/pallas_call | solution.py:37
  6.9 0.5 collective-permute-start
  7.5 0.1 copy.10
  7.6 0.1 reduce-window.9
  7.7 0.1 reduce.end_ref
  7.8 0.8 %collective-permute-done = f32[32,1792]{1,0:T(8,128)S(1)} collective-permute-done((f32[32,1792]{1,0:T(8,128)S(1)}, f32[32,1792]{1,0:T(8,128)S(1)}, u32[]{:S(2)}, u32[]{:S(2)}) %collective-permute-start) | collective-permute-done | bytes 229408 | tf_op jit(solution)/shard_map/ppermute | solution.py:194
  8.6 0.1 abs_reduce_fusion
  8.7 0.1 round-nearest-even_convert_fusion
  9.0 2.9 %collective-permute-start.1 = (s16[32,1920]{1,0:T(8,128)(2,1)S(1)}, s16[32,1920]{1,0:T(8,128)(2,1)S(1)}, u32[]{:S(2)}, u32[]{:S(2)}) collective-permute-start(s16[32,1920]{1,0:T(8,128)(2,1)S(1)} %pad_add_fusion), channel_id=1, source_target_pairs={{0,2},{2,0},{1,3},{3,1},{4,6},{6,4},{5,7},{7,5},{8,10},{10,8},{9,1... | collective-permute-start | bytes 368648 | tf_op jit(solution)/shard_map/ppermute | solution.py:194
  12.0 0.1 fusion.2
  12.1 0.1 fusion.4
  12.3 0.1 collective-permute-start.4
  12.4 3.6 %collective-permute-done.1 = s16[32,1920]{1,0:T(8,128)(2,1)S(1)} collective-permute-done((s16[32,1920]{1,0:T(8,128)(2,1)S(1)}, s16[32,1920]{1,0:T(8,128)(2,1)S(1)}, u32[]{:S(2)}, u32[]{:S(2)}) %collective-permute-start.1) | collective-permute-done | bytes 122912 | tf_op jit(solution)/shard_map/ppermute | solution.py:194
  16.0 0.1 fusion.10
  16.1 0.1 fusion.1
  16.3 1.8 %collective-permute-done.4 = s16[32,1920]{1,0:T(8,128)(2,1)S(1)} collective-permute-done((s16[32,1920]{1,0:T(8,128)(2,1)S(1)}, s16[32,1920]{1,0:T(8,128)(2,1)S(1)}, u32[]{:S(2)}, u32[]{:S(2)}) %collective-permute-start.4) | collective-permute-done | bytes 122912 | tf_op jit(solution)/shard_map/ppermute | solution.py:194
  18.2 0.1 fusion.7
  18.3 0.1 fusion.v_ref
  18.6 2.7 %features.1 = bf16[56,2048]{1,0:T(8,128)(2,1)S(1)} custom-call(s32[56]{0:T(128)S(1)} %bitcast_subtract_fusion.start_ref, s32[56]{0:T(128)S(1)} %reduce.end_ref, f32[64,1792]{1,0:T(8,128)S(1)} %pad_maximum_fusion.2.u_ref, f32[32,1792]{1,0:T(8,128)S(1)} %fusion.v_ref, f32[56,128]{1,0:T(8,128)S(1)} %broadcast_in_dim.11.scale_ref), custom_call_target="tpu_custom_call" | custom-call | tf_op jit(solution)/shard_map/features/pallas_call | solution.py:115
  21.4 1.9 %collective-permute-start.5 = (bf16[56,2048]{1,0:T(8,128)(2,1)S(1)}, bf16[56,2048]{1,0:T(8,128)(2,1)S(1)}, u32[]{:S(2)}, u32[]{:S(2)}) collective-permute-start(bf16[56,2048]{1,0:T(8,128)(2,1)S(1)} %features.1), channel_id=1, source_target_pairs={{0,4},{4,12},{12,8},{8,0},{1,5},{5,13},{13,9},{9,1},{2,6},{6,14},{... | collective-permute-start | bytes 688136 | tf_op jit(solution)/shard_map/ppermute | solution.py:249
  23.4 1.6 %collective-permute-start.7 = (bf16[56,2048]{1,0:T(8,128)(2,1)S(1)}, bf16[56,2048]{1,0:T(8,128)(2,1)S(1)}, u32[]{:S(2)}, u32[]{:S(2)}) collective-permute-start(bf16[56,2048]{1,0:T(8,128)(2,1)S(1)} %pad_maximum_fusion.4), channel_id=1, source_target_pairs={{0,2},{2,0},{1,3},{3,1},{4,6},{6,4},{5,7},{7,5},{8,10},{10,8},{9,1... | collective-permute-start | bytes 688136 | tf_op jit(solution)/shard_map/ppermute | solution.py:194
  24.9 5.5 %collective-permute-done.5 = bf16[56,2048]{1,0:T(8,128)(2,1)S(1)} collective-permute-done((bf16[56,2048]{1,0:T(8,128)(2,1)S(1)}, bf16[56,2048]{1,0:T(8,128)(2,1)S(1)}, u32[]{:S(2)}, u32[]{:S(2)}) %collective-permute-start.5) | collective-permute-done | bytes 229408 | tf_op jit(solution)/shard_map/ppermute | solution.py:249
  30.4 0.6 %collective-permute-done.7 = bf16[56,2048]{1,0:T(8,128)(2,1)S(1)} collective-permute-done((bf16[56,2048]{1,0:T(8,128)(2,1)S(1)}, bf16[56,2048]{1,0:T(8,128)(2,1)S(1)}, u32[]{:S(2)}, u32[]{:S(2)}) %collective-permute-start.7) | collective-permute-done | bytes 229408 | tf_op jit(solution)/shard_map/ppermute | solution.py:194
  31.1 2.6 %collective-permute-start.8 = (bf16[56,2048]{1,0:T(8,128)(2,1)S(1)}, bf16[56,2048]{1,0:T(8,128)(2,1)S(1)}, u32[]{:S(2)}, u32[]{:S(2)}) collective-permute-start(bf16[56,2048]{1,0:T(8,128)(2,1)S(1)} %collective-permute-done.5), channel_id=1, source_target_pairs={{0,4},{4,12},{12,8},{8,0},{1,5},{5,13},{13,9},{9,1},{2,6},{6,14},{... | collective-permute-start | bytes 688136 | tf_op jit(solution)/shard_map/ppermute | solution.py:249
  33.7 1.6 %collective-permute-start.10 = (bf16[56,1024]{1,0:T(8,128)(2,1)S(1)}, bf16[56,1024]{1,0:T(8,128)(2,1)S(1)}, u32[]{:S(2)}, u32[]{:S(2)}) collective-permute-start(bf16[56,1024]{1,0:T(8,128)(2,1)S(1)} %slice_select_fusion.3), channel_id=1, source_target_pairs={{0,2},{2,0},{1,3},{3,1},{4,6},{6,4},{5,7},{7,5},{8,10},{10,8},{9,1... | collective-permute-start | bytes 344072 | tf_op jit(solution)/shard_map/ppermute | solution.py:194
  35.3 1.3 %collective-permute-start.14 = (bf16[56,1024]{1,0:T(8,128)(2,1)S(1)}, bf16[56,1024]{1,0:T(8,128)(2,1)S(1)}, u32[]{:S(2)}, u32[]{:S(2)}) collective-permute-start(bf16[56,1024]{1,0:T(8,128)(2,1)S(1)} %get-tuple-element.41), channel_id=1, source_target_pairs={{4,0},{12,4},{8,12},{0,8},{5,1},{13,5},{9,13},{1,9},{6,2},{14,6},{... | collective-permute-start | bytes 344072 | tf_op jit(solution)/shard_map/ppermute | solution.py:253
  36.7 3.5 %collective-permute-done.8 = bf16[56,2048]{1,0:T(8,128)(2,1)S(1)} collective-permute-done((bf16[56,2048]{1,0:T(8,128)(2,1)S(1)}, bf16[56,2048]{1,0:T(8,128)(2,1)S(1)}, u32[]{:S(2)}, u32[]{:S(2)}) %collective-permute-start.8) | collective-permute-done | bytes 229408 | tf_op jit(solution)/shard_map/ppermute | solution.py:249
  40.1 2.0 %collective-permute-start.11 = (bf16[56,2048]{1,0:T(8,128)(2,1)S(1)}, bf16[56,2048]{1,0:T(8,128)(2,1)S(1)}, u32[]{:S(2)}, u32[]{:S(2)}) collective-permute-start(bf16[56,2048]{1,0:T(8,128)(2,1)S(1)} %collective-permute-done.8), channel_id=1, source_target_pairs={{0,4},{4,12},{12,8},{8,0},{1,5},{5,13},{13,9},{9,1},{2,6},{6,14},{... | collective-permute-start | bytes 688136 | tf_op jit(solution)/shard_map/ppermute | solution.py:249
  42.1 0.4 collective-permute-done.14
  42.6 1.6 %collective-permute-start.13 = (bf16[56,1024]{1,0:T(8,128)(2,1)S(1)}, bf16[56,1024]{1,0:T(8,128)(2,1)S(1)}, u32[]{:S(2)}, u32[]{:S(2)}) collective-permute-start(bf16[56,1024]{1,0:T(8,128)(2,1)S(1)} %slice_select_fusion.2), channel_id=1, source_target_pairs={{0,2},{2,0},{1,3},{3,1},{4,6},{6,4},{5,7},{7,5},{8,10},{10,8},{9,1... | collective-permute-start | bytes 344072 | tf_op jit(solution)/shard_map/ppermute | solution.py:194
  44.2 0.1 copy.13.ids_ref
  44.3 4.7 %collective-permute-done.11 = bf16[56,2048]{1,0:T(8,128)(2,1)S(1)} collective-permute-done((bf16[56,2048]{1,0:T(8,128)(2,1)S(1)}, bf16[56,2048]{1,0:T(8,128)(2,1)S(1)}, u32[]{:S(2)}, u32[]{:S(2)}) %collective-permute-start.11) | collective-permute-done | bytes 229408 | tf_op jit(solution)/shard_map/ppermute | solution.py:249
  49.1 0.1 pad_maximum_fusion.all_ref.row_ref
  49.1 0.1 broadcast_select_fusion.1
  49.2 0.6 collective-permute-start.19
  49.8 0.7 %partial_scores.1 = f32[224,64]{1,0:T(8,128)S(1)} custom-call(s32[64,1]{1,0:T(8,128)S(1)} %copy.13.ids_ref, bf16[224,2048]{1,0:T(8,128)(2,1)S(1)} %pad_maximum_fusion.all_ref.row_ref), custom_call_target="tpu_custom_call" | custom-call | flops 234881024 | bytes 917504 | tf_op jit(solution)/shard_map/partial_scores/pallas_call | solution.py:148
  50.6 1.6 %collective-permute-start.17 = (f32[56,64]{1,0:T(8,128)S(1)}, f32[56,64]{1,0:T(8,128)S(1)}, u32[]{:S(2)}, u32[]{:S(2)}) collective-permute-start(f32[56,64]{1,0:T(8,128)S(1)} %get-tuple-element.43), channel_id=1, source_target_pairs={{0,2},{1,3},{2,0},{3,1},{4,6},{5,7},{6,4},{7,5},{8,10},{9,11},{10,... | collective-permute-start | bytes 43016 | tf_op jit(solution)/shard_map/ppermute | solution.py:345
  52.2 0.3 collective-permute-start.18
  52.5 0.1 maximum_select_fusion
  52.7 0.1 maximum_select_fusion.2
  52.8 0.1 pad_maximum_fusion.1.col_ref
  52.9 6.3 %covariance.1 = f32[2048,2048]{1,0:T(8,128)} custom-call(bf16[224,2048]{1,0:T(8,128)(2,1)S(1)} %pad_maximum_fusion.all_ref.row_ref, bf16[224,2048]{1,0:T(8,128)(2,1)S(1)} %pad_maximum_fusion.1.col_ref), custom_call_target="tpu_custom_call" | custom-call | flops 1879048192 | bytes 16777216 | tf_op jit(solution)/shard_map/covariance/pallas_call | solution.py:181
  59.3 0.6 %add_bitcast_fusion = f32[64,56]{0,1:T(8,128)} fusion(f32[56,64]{1,0:T(8,128)S(1)} %collective-permute-done.18, f32[56,64]{1,0:T(8,128)S(1)} %collective-permute-done.17, f32[56,64]{1,0:T(8,128)S(1)} %get-tuple-element.24, f32[56,64]{1,0:T(8,128)S(1)} %collective-permute-done.16), kind=kLoop, calls=%fused_computation.46 | loop fusion | flops 10752 | bytes 71680 | tf_op jit(solution)/shard_map/transpose | solution.py:352
  (60 shorter events, 1.3 us)
Async XLA Ops:
  0.6 2.0 %copy-start = (bf16[1792,1024]{1,0:T(8,128)(2,1)S(1)}, bf16[1792,1024]{1,0:T(8,128)(2,1)}, u32[]{:S(2)}) copy-start(bf16[1792,1024]{1,0:T(8,128)(2,1)} %x_ref.3) | copy-start | bytes 11010052
  2.7 0.9 %copy-start.1 = (bf16[1024,128]{1,0:T(8,128)(2,1)S(1)}, bf16[1024,128]{1,0:T(8,128)(2,1)}, u32[]{:S(2)}) copy-start(bf16[1024,128]{1,0:T(8,128)(2,1)} %weight_ref.1) | copy-start | bytes 786436
  3.6 2.0 %copy-start.2 = (bf16[1792,1024]{1,0:T(8,128)(2,1)S(1)}, bf16[1792,1024]{1,0:T(8,128)(2,1)}, u32[]{:S(2)}) copy-start(bf16[1792,1024]{1,0:T(8,128)(2,1)} %x_ref.2) | copy-start | bytes 11010052
  3.6 2.0 %copy-start.3 = (bf16[1024,64]{0,1:T(8,128)(2,1)S(1)}, bf16[1024,64]{0,1:T(8,128)(2,1)}, u32[]{:S(2)}) copy-start(bf16[1024,64]{0,1:T(8,128)(2,1)} %param.8) | copy-start | bytes 393220
  4.9 7.0 %collective-permute-start.2 = (f32[2,32,1792]{2,1,0:T(8,128)S(1)}, f32[2,32,1792]{2,1,0:T(8,128)S(1)}, u32[]{:S(2)}, u32[]{:S(2)}) collective-permute-start(f32[2,32,1792]{2,1,0:T(8,128)S(1)} %select_bitcast_fusion), channel_id=1, source_target_pairs={{0,1},{1,0},{2,3},{3,2},{4,5},{5,4},{6,7},{7,6},{8,9},{9,8},{10,11... | collective-permute-start | bytes 1376264 | tf_op jit(solution)/shard_map/ppermute | solution.py:194
  5.7 1.8 %copy-start.4 = (s32[1,56]{1,0:T(1,128)S(1)}, s32[1,56]{1,0:T(1,128)}, u32[]{:S(2)}) copy-start(s32[1,56]{1,0:T(1,128)} %param.10) | copy-start | bytes 676
  6.9 1.6 %collective-permute-start = (f32[32,1792]{1,0:T(8,128)S(1)}, f32[32,1792]{1,0:T(8,128)S(1)}, u32[]{:S(2)}, u32[]{:S(2)}) collective-permute-start(f32[32,1792]{1,0:T(8,128)S(1)} %slice_select_fusion.1), channel_id=1, source_target_pairs={{0,1},{1,0},{2,3},{3,2},{4,5},{5,4},{6,7},{7,6},{8,9},{9,8},{10,11... | collective-permute-start | bytes 688136 | tf_op jit(solution)/shard_map/ppermute | solution.py:194
  9.0 7.0 %collective-permute-start.1 = (s16[32,1920]{1,0:T(8,128)(2,1)S(1)}, s16[32,1920]{1,0:T(8,128)(2,1)S(1)}, u32[]{:S(2)}, u32[]{:S(2)}) collective-permute-start(s16[32,1920]{1,0:T(8,128)(2,1)S(1)} %pad_add_fusion), channel_id=1, source_target_pairs={{0,2},{2,0},{1,3},{3,1},{4,6},{6,4},{5,7},{7,5},{8,10},{10,8},{9,1... | collective-permute-start | bytes 368648 | tf_op jit(solution)/shard_map/ppermute | solution.py:194
  12.3 5.8 %collective-permute-start.4 = (s16[32,1920]{1,0:T(8,128)(2,1)S(1)}, s16[32,1920]{1,0:T(8,128)(2,1)S(1)}, u32[]{:S(2)}, u32[]{:S(2)}) collective-permute-start(s16[32,1920]{1,0:T(8,128)(2,1)S(1)} %pad_add_fusion.1), channel_id=1, source_target_pairs={{0,2},{2,0},{1,3},{3,1},{4,6},{6,4},{5,7},{7,5},{8,10},{10,8},{9,1... | collective-permute-start | bytes 368648 | tf_op jit(solution)/shard_map/ppermute | solution.py:194
  16.2 2.2 %collective-permute-start.3 = (f32[32,1792]{1,0:T(8,128)S(1)}, f32[32,1792]{1,0:T(8,128)S(1)}, u32[]{:S(2)}, u32[]{:S(2)}) collective-permute-start(f32[32,1792]{1,0:T(8,128)S(1)} %fusion.1), channel_id=1, source_target_pairs={{0,1},{1,0},{2,3},{3,2},{4,5},{5,4},{6,7},{7,6},{8,9},{9,8},{10,11... | collective-permute-start | bytes 688136 | tf_op jit(solution)/shard_map/ppermute | solution.py:194
  21.3 2.0 %collective-permute-start.6 = (bf16[56,2048]{1,0:T(8,128)(2,1)S(1)}, bf16[56,2048]{1,0:T(8,128)(2,1)S(1)}, u32[]{:S(2)}, u32[]{:S(2)}) collective-permute-start(bf16[56,2048]{1,0:T(8,128)(2,1)S(1)} %features.1), channel_id=1, source_target_pairs={{0,1},{1,0},{2,3},{3,2},{4,5},{5,4},{6,7},{7,6},{8,9},{9,8},{10,11... | collective-permute-start | bytes 688136 | tf_op jit(solution)/shard_map/ppermute | solution.py:194
  21.4 9.1 %collective-permute-start.5 = (bf16[56,2048]{1,0:T(8,128)(2,1)S(1)}, bf16[56,2048]{1,0:T(8,128)(2,1)S(1)}, u32[]{:S(2)}, u32[]{:S(2)}) collective-permute-start(bf16[56,2048]{1,0:T(8,128)(2,1)S(1)} %features.1), channel_id=1, source_target_pairs={{0,4},{4,12},{12,8},{8,0},{1,5},{5,13},{13,9},{9,1},{2,6},{6,14},{... | collective-permute-start | bytes 688136 | tf_op jit(solution)/shard_map/ppermute | solution.py:249
  23.3 20.9 %copy-start.5 = (s32[64]{0:T(128)S(1)}, s32[64]{0:T(128)}, u32[]{:S(2)}) copy-start(s32[64]{0:T(128)} %param.11) | copy-start | bytes 772
  23.4 7.7 %collective-permute-start.7 = (bf16[56,2048]{1,0:T(8,128)(2,1)S(1)}, bf16[56,2048]{1,0:T(8,128)(2,1)S(1)}, u32[]{:S(2)}, u32[]{:S(2)}) collective-permute-start(bf16[56,2048]{1,0:T(8,128)(2,1)S(1)} %pad_maximum_fusion.4), channel_id=1, source_target_pairs={{0,2},{2,0},{1,3},{3,1},{4,6},{6,4},{5,7},{7,5},{8,10},{10,8},{9,1... | collective-permute-start | bytes 688136 | tf_op jit(solution)/shard_map/ppermute | solution.py:194
  31.1 2.6 %collective-permute-start.9 = (bf16[56,2048]{1,0:T(8,128)(2,1)S(1)}, bf16[56,2048]{1,0:T(8,128)(2,1)S(1)}, u32[]{:S(2)}, u32[]{:S(2)}) collective-permute-start(bf16[56,2048]{1,0:T(8,128)(2,1)S(1)} %collective-permute-done.5), channel_id=1, source_target_pairs={{0,1},{1,0},{2,3},{3,2},{4,5},{5,4},{6,7},{7,6},{8,9},{9,8},{10,11... | collective-permute-start | bytes 688136 | tf_op jit(solution)/shard_map/ppermute | solution.py:194
  31.1 9.0 %collective-permute-start.8 = (bf16[56,2048]{1,0:T(8,128)(2,1)S(1)}, bf16[56,2048]{1,0:T(8,128)(2,1)S(1)}, u32[]{:S(2)}, u32[]{:S(2)}) collective-permute-start(bf16[56,2048]{1,0:T(8,128)(2,1)S(1)} %collective-permute-done.5), channel_id=1, source_target_pairs={{0,4},{4,12},{12,8},{8,0},{1,5},{5,13},{13,9},{9,1},{2,6},{6,14},{... | collective-permute-start | bytes 688136 | tf_op jit(solution)/shard_map/ppermute | solution.py:249
  33.7 6.4 %collective-permute-start.10 = (bf16[56,1024]{1,0:T(8,128)(2,1)S(1)}, bf16[56,1024]{1,0:T(8,128)(2,1)S(1)}, u32[]{:S(2)}, u32[]{:S(2)}) collective-permute-start(bf16[56,1024]{1,0:T(8,128)(2,1)S(1)} %slice_select_fusion.3), channel_id=1, source_target_pairs={{0,2},{2,0},{1,3},{3,1},{4,6},{6,4},{5,7},{7,5},{8,10},{10,8},{9,1... | collective-permute-start | bytes 344072 | tf_op jit(solution)/shard_map/ppermute | solution.py:194
  35.3 7.1 %collective-permute-start.14 = (bf16[56,1024]{1,0:T(8,128)(2,1)S(1)}, bf16[56,1024]{1,0:T(8,128)(2,1)S(1)}, u32[]{:S(2)}, u32[]{:S(2)}) collective-permute-start(bf16[56,1024]{1,0:T(8,128)(2,1)S(1)} %get-tuple-element.41), channel_id=1, source_target_pairs={{4,0},{12,4},{8,12},{0,8},{5,1},{13,5},{9,13},{1,9},{6,2},{14,6},{... | collective-permute-start | bytes 344072 | tf_op jit(solution)/shard_map/ppermute | solution.py:253
  40.1 2.5 %collective-permute-start.12 = (bf16[56,2048]{1,0:T(8,128)(2,1)S(1)}, bf16[56,2048]{1,0:T(8,128)(2,1)S(1)}, u32[]{:S(2)}, u32[]{:S(2)}) collective-permute-start(bf16[56,2048]{1,0:T(8,128)(2,1)S(1)} %collective-permute-done.8), channel_id=1, source_target_pairs={{0,1},{1,0},{2,3},{3,2},{4,5},{5,4},{6,7},{7,6},{8,9},{9,8},{10,11... | collective-permute-start | bytes 688136 | tf_op jit(solution)/shard_map/ppermute | solution.py:194
  40.1 8.9 %collective-permute-start.11 = (bf16[56,2048]{1,0:T(8,128)(2,1)S(1)}, bf16[56,2048]{1,0:T(8,128)(2,1)S(1)}, u32[]{:S(2)}, u32[]{:S(2)}) collective-permute-start(bf16[56,2048]{1,0:T(8,128)(2,1)S(1)} %collective-permute-done.8), channel_id=1, source_target_pairs={{0,4},{4,12},{12,8},{8,0},{1,5},{5,13},{13,9},{9,1},{2,6},{6,14},{... | collective-permute-start | bytes 688136 | tf_op jit(solution)/shard_map/ppermute | solution.py:249
  42.5 6.5 %collective-permute-start.15 = (bf16[168,1024]{1,0:T(8,128)(2,1)S(1)}, bf16[168,1024]{1,0:T(8,128)(2,1)S(1)}, u32[]{:S(2)}, u32[]{:S(2)}) collective-permute-start(bf16[168,1024]{1,0:T(8,128)(2,1)S(1)} %pad_maximum_fusion.3), channel_id=1, source_target_pairs={{0,1},{1,0},{2,3},{3,2},{4,5},{5,4},{6,7},{7,6},{8,9},{9,8},{10,11... | collective-permute-start | bytes 1032200 | tf_op jit(solution)/shard_map/ppermute | solution.py:194
  42.6 6.4 %collective-permute-start.13 = (bf16[56,1024]{1,0:T(8,128)(2,1)S(1)}, bf16[56,1024]{1,0:T(8,128)(2,1)S(1)}, u32[]{:S(2)}, u32[]{:S(2)}) collective-permute-start(bf16[56,1024]{1,0:T(8,128)(2,1)S(1)} %slice_select_fusion.2), channel_id=1, source_target_pairs={{0,2},{2,0},{1,3},{3,1},{4,6},{6,4},{5,7},{7,5},{8,10},{10,8},{9,1... | collective-permute-start | bytes 344072 | tf_op jit(solution)/shard_map/ppermute | solution.py:194
  49.0 3.7 %collective-permute-start.20 = (bf16[56,2048]{1,0:T(8,128)(2,1)S(1)}, bf16[56,2048]{1,0:T(8,128)(2,1)S(1)}, u32[]{:S(2)}, u32[]{:S(2)}) collective-permute-start(bf16[56,2048]{1,0:T(8,128)(2,1)S(1)} %collective-permute-done.11), channel_id=1, source_target_pairs={{0,1},{1,0},{2,3},{3,2},{4,5},{5,4},{6,7},{7,6},{8,9},{9,8},{10,11... | collective-permute-start | bytes 688136 | tf_op jit(solution)/shard_map/ppermute | solution.py:194
  49.2 3.4 %collective-permute-start.19 = (bf16[56,1024]{1,0:T(8,128)(2,1)S(1)}, bf16[56,1024]{1,0:T(8,128)(2,1)S(1)}, u32[]{:S(2)}, u32[]{:S(2)}) collective-permute-start(bf16[56,1024]{1,0:T(8,128)(2,1)S(1)} %collective-permute-done.13), channel_id=1, source_target_pairs={{0,1},{1,0},{2,3},{3,2},{4,5},{5,4},{6,7},{7,6},{8,9},{9,8},{10,11... | collective-permute-start | bytes 344072 | tf_op jit(solution)/shard_map/ppermute | solution.py:194
  50.5 8.7 %collective-permute-start.16 = (f32[56,64]{1,0:T(8,128)S(1)}, f32[56,64]{1,0:T(8,128)S(1)}, u32[]{:S(2)}, u32[]{:S(2)}) collective-permute-start(f32[56,64]{1,0:T(8,128)S(1)} %get-tuple-element.44), channel_id=1, source_target_pairs={{0,1},{1,0},{2,3},{3,2},{4,5},{5,4},{6,7},{7,6},{8,9},{9,8},{10,11... | collective-permute-start | bytes 43016 | tf_op jit(solution)/shard_map/ppermute | solution.py:345
  50.6 8.6 %collective-permute-start.17 = (f32[56,64]{1,0:T(8,128)S(1)}, f32[56,64]{1,0:T(8,128)S(1)}, u32[]{:S(2)}, u32[]{:S(2)}) collective-permute-start(f32[56,64]{1,0:T(8,128)S(1)} %get-tuple-element.43), channel_id=1, source_target_pairs={{0,2},{1,3},{2,0},{3,1},{4,6},{5,7},{6,4},{7,5},{8,10},{9,11},{10,... | collective-permute-start | bytes 43016 | tf_op jit(solution)/shard_map/ppermute | solution.py:345
  52.2 7.1 %collective-permute-start.18 = (f32[56,64]{1,0:T(8,128)S(1)}, f32[56,64]{1,0:T(8,128)S(1)}, u32[]{:S(2)}, u32[]{:S(2)}) collective-permute-start(f32[56,64]{1,0:T(8,128)S(1)} %get-tuple-element.42), channel_id=1, source_target_pairs={{0,3},{1,2},{2,1},{3,0},{4,7},{5,6},{6,5},{7,4},{8,11},{9,10},{10,... | collective-permute-start | bytes 43016 | tf_op jit(solution)/shard_map/ppermute | solution.py:345
